TPU v7x, 32 devices: a whole 2x2x4 slice. The times are simulated.
32 devices in a mesh: blk: 8 (over y, x, core), uly: 4 (over z).
Axes of the slice: x: 2, y: 2, z: 4, core: 2. Of those that a mesh axis runs over, the one named last changes fastest.
Arguments:
- q_code: bfloat16 [16384, 6144], P(('blk', 'uly')), may hold values from -6 to 6
- k_code: bfloat16 [16384, 6144], P(('blk', 'uly')), may hold values from -4 to 4
- v_code: bfloat16 [16384, 6144], P(('blk', 'uly')), may hold values from -6 to 6
- block_exp: int32 [128, 3, 48], P(('blk', 'uly')), may hold values from -2 to 1
- window: int32 [128, 27], P('blk'), may hold values from 0 to 47, as said below
- window_count: int32 [128], P('blk'), may hold values from 9 to 27, as said below
Outputs:
- attn_out: bfloat16 [16384, 6144], P(('blk', 'uly'))
Inputs may be any that keep to these rules, and one draw needn't show every extreme that they name: `window`: for s < window_count[g] the slots name distinct tiles in groups of nine: each group a 3 x 3 block of the 4 x 4 tile grid of one frame; the first group lies in the query's own frame and holds the query's own tile, the others in the frame before or after; no group reaches before the first frame or after the last. Unused slots hold some tile of the own frame. `window_count`: A multiple of 9.
All inputs are finite; a program needn't handle non-finite values.
Results may differ from a plain program's by a relative error of at most 0.0027.
Values may be sent and summed in bfloat16 or wider, within the bound.
No kernel may reach another device: no remote copies, remote signals or barrier semaphores. Data moves between devices by JAX's collectives and lax.ppermute only.
A program may use at most 192 MiB of HBM per device.

v0:
```python
import math

import jax
import jax.numpy as jnp
from jax import lax
from jax.sharding import PartitionSpec as P


def from_behind(block, axis, distance):
    devices = range(lax.axis_size(axis))
    route = [(i - distance, i) for i in devices if i - distance in devices]
    return lax.ppermute(block, axis, route)


def hadamard(order):
    indices = jnp.arange(order, dtype=jnp.int32)
    common = indices[:, None] & indices[None, :]
    parity = jnp.zeros((order, order), jnp.int32)
    for bit_pos in range(max(1, order.bit_length())):
        parity = parity + (common >> bit_pos & 1)
    signs = jnp.where(parity % 2 == 0, 1.0, -1.0).astype(jnp.float32)
    return signs / math.sqrt(order)


def dequantize(code, exponent, tile_len, head_count):
    row_total, model_width = code.shape
    factor = jnp.exp2(exponent.astype(jnp.float32)).astype(jnp.bfloat16)
    blocks = code.reshape(row_total // tile_len, tile_len, head_count, model_width // head_count)
    return blocks * factor[:, None, :, None]


def attend(queries, before, current, later, window, window_count):
    key_all = jnp.concatenate([before[0], current[0], later[0]], axis=0)
    value_all = jnp.concatenate([before[1], current[1], later[1]], axis=0)
    frame_tiles, slot_total = window.shape
    slab_rows, head_count, head_width = queries.shape
    tile_len = slab_rows // frame_tiles
    valid_slot = jnp.arange(slot_total, dtype=jnp.int32)[None, :] < window_count[:, None]
    inv_root = 1.0 / math.sqrt(head_width)
    rotation = hadamard(head_width)
    group_size = min(frame_tiles, max(1, 512 // tile_len))
    while frame_tiles % group_size:
        group_size -= 1

    def one_head(head_idx):
        query_head = lax.dynamic_index_in_dim(queries, head_idx, 1, False).reshape(
            frame_tiles, tile_len, head_width
        )
        key_head = lax.dynamic_index_in_dim(key_all, head_idx, 1, False).reshape(
            3 * frame_tiles, tile_len, head_width
        )
        value_head = lax.dynamic_index_in_dim(value_all, head_idx, 1, False).reshape(
            3 * frame_tiles, tile_len, head_width
        )

        def one_group(group_idx):
            first_tile = group_idx * group_size
            query_group = lax.dynamic_slice_in_dim(query_head, first_tile, group_size, 0)
            index_group = lax.dynamic_slice_in_dim(window, first_tile, group_size, 0)
            slot_group = lax.dynamic_slice_in_dim(valid_slot, first_tile, group_size, 0)
            key_tiles = jnp.take(key_head, index_group, axis=0)
            value_tiles = jnp.take(value_head, index_group, axis=0)
            scores = (
                jnp.einsum(
                    "gqd,gnkd->gqnk", query_group, key_tiles, preferred_element_type=jnp.float32
                )
                * inv_root
            )
            scores = jnp.where(slot_group[:, None, :, None], scores, -jnp.inf)
            largest = jnp.max(scores, axis=(2, 3), keepdims=True)
            expsum = jnp.exp(scores - largest)
            totals = jnp.sum(expsum, axis=(2, 3))
            summed = jnp.einsum(
                "gqnk,gnkd->gqd",
                expsum.astype(jnp.bfloat16),
                value_tiles,
                preferred_element_type=jnp.float32,
            )
            rotated = summed / totals[:, :, None]
            result = jnp.einsum("gqd,de->gqe", rotated, rotation, precision=lax.Precision.HIGHEST)
            return result.astype(jnp.bfloat16)

        blocks = lax.map(one_group, jnp.arange(frame_tiles // group_size, dtype=jnp.int32))
        return blocks.reshape(slab_rows, head_width)

    per_head = lax.map(one_head, jnp.arange(head_count, dtype=jnp.int32))
    return jnp.transpose(per_head, (1, 0, 2))


def shards(q_code, k_code, v_code, block_exp, window, window_count):
    row_total, model_width = q_code.shape
    tile_total = block_exp.shape[0]
    tile_len = row_total // tile_total
    head_count = block_exp.shape[2]
    head_width = model_width // head_count
    ulysses = lax.axis_size("uly")
    local_heads = head_count // ulysses

    def prepared(code, column):
        scaled = dequantize(code, block_exp[:, column], tile_len, head_count)
        return scaled.reshape(row_total, ulysses, local_heads, head_width)

    query_rows = prepared(q_code, 0)
    key_rows = prepared(k_code, 1)
    value_rows = prepared(v_code, 2)
    stacked = jnp.stack([query_rows, key_rows, value_rows])
    arrived = lax.all_to_all(stacked, "uly", split_axis=2, concat_axis=1, tiled=True)
    current = arrived[1:3, :, 0]
    before = from_behind(current, "blk", 1)
    later = from_behind(current, "blk", -1)
    mixed = attend(arrived[0, :, 0], before, current, later, window, window_count)
    slab_rows = mixed.shape[0]
    returned = lax.all_to_all(
        mixed.reshape(slab_rows, 1, mixed.shape[1], head_width),
        "uly",
        split_axis=0,
        concat_axis=1,
        tiled=True,
    )
    return returned.reshape(row_total, model_width)


def solution(mesh):
    return jax.shard_map(
        shards,
        mesh=mesh,
        in_specs=(
            P(("blk", "uly"), None),
            P(("blk", "uly"), None),
            P(("blk", "uly"), None),
            P(("blk", "uly"), None, None),
            P("blk", None),
            P("blk"),
        ),
        out_specs=P(("blk", "uly"), None),
        check_vma=False,
    )
```

profile of v0, /device:TPU:11, one launch (start us, length us, event | category | flops | bytes accessed | tf_op | source)
XLA Modules:
  0.0 2249.2 jit_solution(4110483791857086199)
XLA Ops:
  1.3 8.7 copy.34
  9.9 8.6 copy.36
  18.8 8.6 copy.32
  41.0 410.4 %all_to_all.30 = bf16[3,512,4,12,128]{1,4,3,0,2:T(8,128)(2,1)} all-to-all(bf16[3,512,4,12,128]{1,4,3,0,2:T(8,128)(2,1)S(1)} %copy.38), channel_id=1, replica_groups=mesh['blk'=8,'uly'=4] {'uly'}, dimensions={2} | all-to-all | bytes 37748736 | tf_op jit(solution)/shard_map/all_to_all | solution.py:107
  451.4 24.7 %copy.39 = bf16[3,512,4,12,128]{4,1,2,3,0:T(8,128)(2,1)} copy(bf16[3,512,4,12,128]{1,4,3,0,2:T(8,128)(2,1)} %all_to_all.30) | data formatting | bytes 37748736 | tf_op jit(solution)/shard_map/all_to_all | solution.py:107
  476.1 10.6 slice.55
  493.2 10.3 fusion.45
  503.5 255.4 %collective-permute-done = bf16[2,2048,12,128]{3,1,2,0:T(8,128)(2,1)} collective-permute-done((bf16[2,2048,12,128]{3,1,2,0:T(8,128)(2,1)}, bf16[2,2048,12,128]{3,1,2,0:T(8,128)(2,1)}, u32[]{:S(2)}, u32[]{:S(2)}) %collective-permute-start) | collective-permute-done | bytes 12582944 | tf_op jit(solution)/shard_map/ppermute | solution.py:12
  764.2 8.2 slice_bitcast_fusion
  772.4 20.7 pad_maximum_fusion.2
  793.0 27.6 %pad_maximum_fusion.1 = bf16[6144,12,128]{2,0,1:T(8,128)(2,1)} fusion(bf16[2048,12,128]{2,0,1:T(8,128)(2,1)S(1)} %get-tuple-element.169, bf16[2048,12,128]{2,0,1:T(8,128)(2,1)S(1)} %bitcast.100, bf16[2048,12,128]{2,0,1:T(8,128)(2,1)S(1)} %get-tuple-element.167), kind=kLoop, calls=%fused_computation.50 | loop fusion | flops 56623104 | bytes 37748736 | tf_op jit(solution)/shard_map/concatenate | solution.py:33
  820.6 1214.7 %while.23 = (s32[]{:T(128)}, bf16[12,2048,128]{2,1,0:T(8,128)(2,1)}, s32[12]{0:T(128)S(1)}, bf16[2048,12,128]{2,0,1:T(8,128)(2,1)}, bf16[6144,12,128]{2,0,1:T(8,...) while((s32[]{:T(128)}, ...), condition=%wide.region_5.7_spmd.clone, body=%wide.region_0.6_spmd.clone.sunk | while | flops 1030390848 | bytes 80105280 | solution.py:86
  827.3 92.7 %while.24 = (s32[]{:T(128)}, bf16[4,4,128,128]{3,2,1,0:T(8,128)(2,1)}, s32[4]{0:T(128)S(1)}, pred[16,27]{1,0:T(8,128)(4,1)S(1)}, bf16[16,128,128]{2,1,0:T(8,128)...) while((s32[]{:T(128)}, ...), condition=%wide.region_4.5_spmd, body=%wide.region_1.4_spmd.sunk | while | flops 1029767808 | bytes 71649808 | solution.py:83
  843.1 6.3 fusion.61
  928.5 92.7 %while.24 = (s32[]{:T(128)}, bf16[4,4,128,128]{3,2,1,0:T(8,128)(2,1)}, s32[4]{0:T(128)S(1)}, pred[16,27]{1,0:T(8,128)(4,1)S(1)}, bf16[16,128,128]{2,1,0:T(8,128)...) while((s32[]{:T(128)}, ...), condition=%wide.region_4.5_spmd, body=%wide.region_1.4_spmd.sunk | while | flops 1029767808 | bytes 71649808 | solution.py:83
  967.5 6.3 fusion.61
  1013.8 6.3 fusion.61
  1029.7 92.7 %while.24 = (s32[]{:T(128)}, bf16[4,4,128,128]{3,2,1,0:T(8,128)(2,1)}, s32[4]{0:T(128)S(1)}, pred[16,27]{1,0:T(8,128)(4,1)S(1)}, bf16[16,128,128]{2,1,0:T(8,128)...) while((s32[]{:T(128)}, ...), condition=%wide.region_4.5_spmd, body=%wide.region_1.4_spmd.sunk | while | flops 1029767808 | bytes 71649808 | solution.py:83
  1045.5 6.3 fusion.61
  1130.9 92.7 %while.24 = (s32[]{:T(128)}, bf16[4,4,128,128]{3,2,1,0:T(8,128)(2,1)}, s32[4]{0:T(128)S(1)}, pred[16,27]{1,0:T(8,128)(4,1)S(1)}, bf16[16,128,128]{2,1,0:T(8,128)...) while((s32[]{:T(128)}, ...), condition=%wide.region_4.5_spmd, body=%wide.region_1.4_spmd.sunk | while | flops 1029767808 | bytes 71649808 | solution.py:83
  1232.2 92.7 %while.24 = (s32[]{:T(128)}, bf16[4,4,128,128]{3,2,1,0:T(8,128)(2,1)}, s32[4]{0:T(128)S(1)}, pred[16,27]{1,0:T(8,128)(4,1)S(1)}, bf16[16,128,128]{2,1,0:T(8,128)...) while((s32[]{:T(128)}, ...), condition=%wide.region_4.5_spmd, body=%wide.region_1.4_spmd.sunk | while | flops 1029767808 | bytes 71649808 | solution.py:83
  1333.4 92.7 %while.24 = (s32[]{:T(128)}, bf16[4,4,128,128]{3,2,1,0:T(8,128)(2,1)}, s32[4]{0:T(128)S(1)}, pred[16,27]{1,0:T(8,128)(4,1)S(1)}, bf16[16,128,128]{2,1,0:T(8,128)...) while((s32[]{:T(128)}, ...), condition=%wide.region_4.5_spmd, body=%wide.region_1.4_spmd.sunk | while | flops 1029767808 | bytes 71649808 | solution.py:83
  1434.6 92.7 %while.24 = (s32[]{:T(128)}, bf16[4,4,128,128]{3,2,1,0:T(8,128)(2,1)}, s32[4]{0:T(128)S(1)}, pred[16,27]{1,0:T(8,128)(4,1)S(1)}, bf16[16,128,128]{2,1,0:T(8,128)...) while((s32[]{:T(128)}, ...), condition=%wide.region_4.5_spmd, body=%wide.region_1.4_spmd.sunk | while | flops 1029767808 | bytes 71649808 | solution.py:83
  1535.8 92.7 %while.24 = (s32[]{:T(128)}, bf16[4,4,128,128]{3,2,1,0:T(8,128)(2,1)}, s32[4]{0:T(128)S(1)}, pred[16,27]{1,0:T(8,128)(4,1)S(1)}, bf16[16,128,128]{2,1,0:T(8,128)...) while((s32[]{:T(128)}, ...), condition=%wide.region_4.5_spmd, body=%wide.region_1.4_spmd.sunk | while | flops 1029767808 | bytes 71649808 | solution.py:83
  1637.0 92.7 %while.24 = (s32[]{:T(128)}, bf16[4,4,128,128]{3,2,1,0:T(8,128)(2,1)}, s32[4]{0:T(128)S(1)}, pred[16,27]{1,0:T(8,128)(4,1)S(1)}, bf16[16,128,128]{2,1,0:T(8,128)...) while((s32[]{:T(128)}, ...), condition=%wide.region_4.5_spmd, body=%wide.region_1.4_spmd.sunk | while | flops 1029767808 | bytes 71649808 | solution.py:83
  1738.3 92.7 %while.24 = (s32[]{:T(128)}, bf16[4,4,128,128]{3,2,1,0:T(8,128)(2,1)}, s32[4]{0:T(128)S(1)}, pred[16,27]{1,0:T(8,128)(4,1)S(1)}, bf16[16,128,128]{2,1,0:T(8,128)...) while((s32[]{:T(128)}, ...), condition=%wide.region_4.5_spmd, body=%wide.region_1.4_spmd.sunk | while | flops 1029767808 | bytes 71649808 | solution.py:83
  1839.5 92.7 %while.24 = (s32[]{:T(128)}, bf16[4,4,128,128]{3,2,1,0:T(8,128)(2,1)}, s32[4]{0:T(128)S(1)}, pred[16,27]{1,0:T(8,128)(4,1)S(1)}, bf16[16,128,128]{2,1,0:T(8,128)...) while((s32[]{:T(128)}, ...), condition=%wide.region_4.5_spmd, body=%wide.region_1.4_spmd.sunk | while | flops 1029767808 | bytes 71649808 | solution.py:83
  1940.7 92.7 %while.24 = (s32[]{:T(128)}, bf16[4,4,128,128]{3,2,1,0:T(8,128)(2,1)}, s32[4]{0:T(128)S(1)}, pred[16,27]{1,0:T(8,128)(4,1)S(1)}, bf16[16,128,128]{2,1,0:T(8,128)...) while((s32[]{:T(128)}, ...), condition=%wide.region_4.5_spmd, body=%wide.region_1.4_spmd.sunk | while | flops 1029767808 | bytes 71649808 | solution.py:83
  2035.2 6.9 copy.48
  2042.2 185.4 %all_to_all.31 = bf16[2048,1,12,128]{3,2,1,0:T(8,128)(2,1)S(1)} all-to-all(bf16[2048,1,12,128]{3,2,1,0:T(8,128)(2,1)S(1)} %bitcast.99), channel_id=1, replica_groups=mesh['blk'=8,'uly'=4] {'uly'}, dimensions={0} | all-to-all | bytes 12582912 | tf_op jit(solution)/shard_map/all_to_all | solution.py:113
  2231.9 8.7 copy.42
  2240.6 8.6 copy.43
  (691 shorter events, 1165.1 us)
Async XLA Ops:
  486.8 272.2 %collective-permute-start = (bf16[2,2048,12,128]{3,1,2,0:T(8,128)(2,1)}, bf16[2,2048,12,128]{3,1,2,0:T(8,128)(2,1)}, u32[]{:S(2)}, u32[]{:S(2)}) collective-permute-start(bf16[2,2048,12,128]{3,1,2,0:T(8,128)(2,1)} %bitcast.19), channel_id=1, source_target_pairs={{0,4},{4,8},{8,12},{12,16},{16,20},{20,24},{24,28},{1,5},{5,9},{9,... | collective-permute-start | bytes 37748744 | tf_op jit(solution)/shard_map/ppermute | solution.py:12
  491.3 272.9 %collective-permute-start.1 = (bf16[2,2048,12,128]{3,1,2,0:T(8,128)(2,1)}, bf16[2,2048,12,128]{3,1,2,0:T(8,128)(2,1)}, u32[]{:S(2)}, u32[]{:S(2)}) collective-permute-start(bf16[2,2048,12,128]{3,1,2,0:T(8,128)(2,1)} %bitcast.19), channel_id=1, source_target_pairs={{4,0},{8,4},{12,8},{16,12},{20,16},{24,20},{28,24},{5,1},{9,5},{13... | collective-permute-start | bytes 37748744 | tf_op jit(solution)/shard_map/ppermute | solution.py:12
  793.0 27.6 %copy-start.1 = (s32[16]{0:T(128)S(1)}, s32[16]{0:T(128)}, u32[]{:S(2)}) copy-start(s32[16]{0:T(128)} %param.17) | copy-start | bytes 196
  835.5 2.9 copy-start
  858.7 2.9 copy-start
  881.8 2.9 copy-start
  905.0 2.9 copy-start
  936.7 2.9 copy-start
  959.9 2.9 copy-start
  983.0 2.9 copy-start
  1006.2 2.9 copy-start
  1037.9 2.9 copy-start
  1061.1 2.9 copy-start
  1084.3 2.9 copy-start
  1107.4 2.9 copy-start
  1139.2 2.9 copy-start
  1162.3 2.9 copy-start
  1185.5 2.9 copy-start
  1208.6 2.9 copy-start
  1240.4 2.9 copy-start
  1263.5 2.9 copy-start
  1286.7 2.9 copy-start
  1309.9 2.9 copy-start
  1341.6 2.9 copy-start
  1364.8 2.9 copy-start
  1387.9 2.9 copy-start
  1466.0 2.9 copy-start
  1544.0 2.9 copy-start
  1714.7 2.9 copy-start
  1769.6 2.9 copy-start
  1792.8 2.9 copy-start
  2018.4 2.9 copy-start
  (19 other events, 54.6 us)
where the time goes:
time: 2260 us; the launch traced here: 2250 us
  local copies, waits for them, and re-layouts  642 us (28%)
  blocking collectives  596 us (26%)
  matrix products  514 us (23%)
  waiting for transfers between devices  255 us (11%)
  other arithmetic  180 us (8%)
  loops' own time  55.2 us (2%)
    all_to_all x1, blocking collectives, shards(): lax.all_to_all(stacked, 'uly', split_axis=2, concat_axis=1, tiled=True)  410 us
    dot_general x48, matrix products, one_group(): jnp.einsum('gqnk,gnkd->gqd', expsum.astype(jnp.bfloat16), value_tiles, pr...  304 us
    ppermute x2, waiting for transfers between devices, from_behind(): return lax.ppermute(block, axis, route)  255 us
    all_to_all x1, blocking collectives, shards(): lax.all_to_all(mixed.reshape(slab_rows, 1, mixed.shape[1], head_width), '...  185 us
    dot_general x48, matrix products, one_group(): jnp.einsum('gqd,gnkd->gqnk', query_group, key_tiles, preferred_element_ty...  161 us
    gather x48, local copies, waits for them, and re-layouts, one_group(): value_tiles = jnp.take(value_head, index_group, axis=0)  143 us
    while x96, local copies, waits for them, and re-layouts  137 us
    gather x48, local copies, waits for them, and re-layouts, one_group(): key_tiles = jnp.take(key_head, index_group, axis=0)  134 us
  transfers between devices with their start and end apart: 2, of which 1 were waited for; matrix products, arithmetic and copies ran while one was open for 1% of the time, Pallas kernels for 0%

commit v1 on v0

v1 whole, which is shorter than its diff:
```python
import math

import jax
import jax.numpy as jnp
from jax import lax
from jax.experimental import pallas as pl
from jax.experimental.pallas import tpu as pltpu
from jax.sharding import PartitionSpec as P

LOG2E = math.log2(math.e)
ANYWHERE = pl.BlockSpec(memory_space=pl.ANY)
GROUP = 9
VMEM = 60 << 20


def hadamard_signs(order):
    indices = jnp.arange(order, dtype=jnp.int32)
    common = indices[:, None] & indices[None, :]
    parity = jnp.zeros((order, order), jnp.int32)
    for bit_pos in range(max(1, order.bit_length())):
        parity = parity + (common >> bit_pos & 1)
    return jnp.where(parity % 2 == 0, 1.0, -1.0).astype(jnp.bfloat16)


def chunk_sizes(local_heads):
    if local_heads % 12 == 0:
        unit = local_heads // 12
        return [unit * size for size in (2, 2, 2, 2, 2, 1, 1)]
    return [1] * local_heads


def params():
    return pltpu.CompilerParams(vmem_limit_bytes=VMEM)


def light():
    return pl.CostEstimate(flops=0, bytes_accessed=1 << 20, transcendentals=0)


def pack(z, factor, q_code, k_code, v_code, first, heads, local_heads, width, ulysses, tile, after):
    rows = q_code.shape[0]

    def body(z_ref, factor_ref, *refs):
        codes = refs[: 3 * ulysses]
        outs = refs[-ulysses:]
        for k in range(ulysses):
            head = (z_ref[0] ^ k) * local_heads + first + pl.program_id(0)
            for part, column in enumerate((1, 2, 0)):
                for i in range(rows // tile):
                    span = slice(i * tile, (i + 1) * tile)
                    block = codes[3 * k + part][span, :].astype(jnp.float32) * factor_ref[i, column, head]
                    outs[k][part, span, :] = block.astype(jnp.bfloat16)

    in_specs = [pl.BlockSpec(memory_space=pltpu.SMEM)]
    operands = [factor]
    for k in range(ulysses):
        spec = pl.BlockSpec((rows, width), lambda h, z_ref, k=k: (0, (z_ref[0] ^ k) * local_heads + first + h))
        in_specs += [spec] * 3
        operands += [k_code, v_code, q_code]
    return pl.pallas_call(
        body,
        grid_spec=pltpu.PrefetchScalarGridSpec(
            num_scalar_prefetch=1,
            grid=(heads,),
            in_specs=in_specs + [ANYWHERE] * len(after),
            out_specs=[pl.BlockSpec((3, None, rows, width), lambda h, z_ref: (0, h, 0, 0))] * ulysses,
        ),
        out_shape=[jax.ShapeDtypeStruct((3, heads, rows, width), jnp.bfloat16)] * ulysses,
        compiler_params=params(),
        cost_estimate=light(),
        name="pack",
    )(z, *operands, *after)


def join(pieces, after):
    count = len(pieces)
    _, heads, rows, width = pieces[0].shape

    def body(*refs):
        out = refs[-1]
        for k in range(count):
            out[pl.ds(k * rows, rows), :] = refs[k][...]

    return pl.pallas_call(
        body,
        grid=(heads, 2),
        in_specs=[pl.BlockSpec((None, None, rows, width), lambda h, p: (p, h, 0, 0))] * count
        + [ANYWHERE] * len(after),
        out_specs=pl.BlockSpec((None, None, count * rows, width), lambda h, p: (h, p, 0, 0)),
        out_shape=jax.ShapeDtypeStruct((heads, 2, count * rows, width), jnp.bfloat16),
        compiler_params=params(),
        cost_estimate=light(),
        name="join",
    )(*pieces, *after)


def collect(z, returned, firsts, local_heads, tile):
    ulysses = len(returned[0])
    _, rows, width = returned[0][0].shape
    model_width = ulysses * local_heads * width
    pieces = [(c, k) for c in range(len(returned)) for k in range(ulysses)]

    def body(z_ref, *refs):
        out = refs[-1]
        for ref, (c, k) in zip(refs, pieces):
            for h in range(ref.shape[0]):
                column = ((z_ref[0] ^ k) * local_heads + firsts[c] + h) * width
                out[:, pl.ds(pl.multiple_of(column, width), width)] = ref[h]

    return pl.pallas_call(
        body,
        grid_spec=pltpu.PrefetchScalarGridSpec(
            num_scalar_prefetch=1,
            grid=(rows // tile,),
            in_specs=[
                pl.BlockSpec((returned[c][k].shape[0], tile, width), lambda i, z_ref: (0, i, 0))
                for c, k in pieces
            ],
            out_specs=pl.BlockSpec((tile, model_width), lambda i, z_ref: (i, 0)),
        ),
        out_shape=jax.ShapeDtypeStruct((rows, model_width), jnp.bfloat16),
        compiler_params=params(),
        cost_estimate=light(),
        name="collect",
    )(z, *[returned[c][k] for c, k in pieces])


def unit_table(window, window_count, z, per_piece, group):
    frame_tiles, slot_total = window.shape
    groups = window_count // group
    ends = jnp.cumsum(groups)
    unit = jnp.arange(frame_tiles * (slot_total // group) + 4, dtype=jnp.int32)
    owner = jnp.sum(unit[:, None] >= ends[None, :], axis=1).astype(jnp.int32)
    order = jnp.minimum(unit - (ends - groups)[jnp.minimum(owner, frame_tiles - 1)], slot_total // group - 1)

    def placed(tiles):
        frame, inside = tiles // frame_tiles, tiles % frame_tiles
        return frame * frame_tiles + ((inside // per_piece) ^ z) * per_piece + inside % per_piece

    members = placed(window).reshape(frame_tiles, slot_total // group, group)
    members = members[jnp.minimum(owner, frame_tiles - 1), order]
    spare = owner >= frame_tiles
    own = jnp.where(spare, frame_tiles, placed(jnp.minimum(owner, frame_tiles - 1)))
    first = (order == 0) | spare
    head = jnp.stack([own, first.astype(jnp.int32)], axis=1)
    return jnp.concatenate([head, members], axis=1).reshape(-1), ends[-1:]


def attend(z, units, unit_count, signs, queries, before, current, later, width, tile, group, after):
    ulysses = len(queries)
    heads, _, frame_rows, _ = current.shape
    rows = frame_rows // ulysses
    frame_tiles = frame_rows // tile
    span = group * tile
    stride = group + 2
    lag, ring = 3, 4
    to_log2 = LOG2E / math.sqrt(width)
    post = 1.0 / math.sqrt(width)

    def body(unit_ref, count_ref, signs_ref, *refs):
        query_refs = refs[:ulysses]
        frames = refs[ulysses : ulysses + 3]
        refs = refs[ulysses + 3 + len(after) :]
        outs = refs[:ulysses]
        keys, values, query_all, tops, total_all, sum_all = refs[ulysses : ulysses + 6]
        scores = refs[ulysses + 6 :]
        count = count_ref[0]
        for k in range(ulysses):
            query_all[pl.ds(k * rows, rows), :] = query_refs[k][...]
        for f in range(3):
            values[pl.ds(f * frame_rows, frame_rows), :] = frames[f][1]
            keys[pl.ds(f * frame_rows, frame_rows), :] = frames[f][0]
        total_all[...] = jnp.zeros_like(total_all)
        sum_all[...] = jnp.zeros_like(sum_all)

        def tiles_of(source, u):
            parts = []
            for s in range(group):
                start = pl.multiple_of(unit_ref[u * stride + 2 + s] * tile, tile)
                parts.append(source[pl.ds(start, tile), :])
            return jnp.concatenate(parts, axis=0)

        def score(u, slot):
            t = unit_ref[u * stride]
            query = query_all[pl.ds(pl.multiple_of(t * tile, tile), tile), :]
            block = lax.dot_general(
                query, tiles_of(keys, u), (((1,), (1,)), ((), ())), preferred_element_type=jnp.float32
            )
            scores[slot][...] = block
            top = block[:, :tile]
            for s in range(1, group):
                top = jnp.maximum(top, block[:, s * tile : (s + 1) * tile])
            known = tops[t]
            tops[t] = jnp.where(unit_ref[u * stride + 1] == 1, top, jnp.maximum(top, known))

        def weigh(u, slot, top):
            t = unit_ref[u * stride]
            expo = jnp.exp2(scores[slot][...] * to_log2 - top)
            total = expo[:, :tile]
            for s in range(1, group):
                total = total + expo[:, s * tile : (s + 1) * tile]
            total_all[t] += total
            sum_all[t] += lax.dot_general(
                expo.astype(jnp.bfloat16),
                tiles_of(values, u),
                (((1,), (0,)), ((), ())),
                preferred_element_type=jnp.float32,
            )

        for u in range(lag):
            score(u, u)

        def four_units(i, carry):
            for j in range(ring):
                u = i * ring + j
                top = jnp.max(tops[unit_ref[u * stride]], axis=1, keepdims=True) * to_log2
                score(u + lag, (j + lag) % ring)
                weigh(u, j, top)
            return carry

        lax.fori_loop(0, (count + ring - 1) // ring, four_units, 0)
        for k in range(ulysses):
            for i in range(rows // tile):
                t = k * (rows // tile) + i
                rotated = sum_all[t] * (post / jnp.sum(total_all[t], axis=1, keepdims=True))
                high = rotated.astype(jnp.bfloat16)
                rest = rotated - high.astype(jnp.float32)
                middle = rest.astype(jnp.bfloat16)
                low = (rest - middle.astype(jnp.float32)).astype(jnp.bfloat16)
                signs_val = signs_ref[...]
                result = jnp.dot(low, signs_val, preferred_element_type=jnp.float32)
                result += jnp.dot(middle, signs_val, preferred_element_type=jnp.float32)
                result += jnp.dot(high, signs_val, preferred_element_type=jnp.float32)
                outs[k][pl.ds(i * tile, tile), :] = result.astype(jnp.bfloat16)

    frame_spec = pl.BlockSpec((None, 2, frame_rows, width), lambda h, *_: (h, 0, 0, 0))
    return pl.pallas_call(
        body,
        grid_spec=pltpu.PrefetchScalarGridSpec(
            num_scalar_prefetch=2,
            grid=(heads,),
            in_specs=[pl.BlockSpec((width, width), lambda h, *_: (0, 0))]
            + [pl.BlockSpec((None, None, rows, width), lambda h, *_: (2, h, 0, 0))] * ulysses
            + [frame_spec] * 3
            + [ANYWHERE] * len(after),
            out_specs=[pl.BlockSpec((None, rows, width), lambda h, *_: (h, 0, 0))] * ulysses,
            scratch_shapes=[
                pltpu.VMEM((3 * frame_rows, width), jnp.bfloat16),
                pltpu.VMEM((3 * frame_rows, width), jnp.bfloat16),
                pltpu.VMEM((frame_rows + tile, width), jnp.bfloat16),
                pltpu.VMEM((frame_tiles + 1, tile, tile), jnp.float32),
                pltpu.VMEM((frame_tiles + 1, tile, tile), jnp.float32),
                pltpu.VMEM((frame_tiles + 1, tile, width), jnp.float32),
            ]
            + [pltpu.VMEM((tile, span), jnp.float32)] * ring,
        ),
        out_shape=[jax.ShapeDtypeStruct((heads, rows, width), jnp.bfloat16)] * ulysses,
        compiler_params=pltpu.CompilerParams(vmem_limit_bytes=60 << 20),
        cost_estimate=pl.CostEstimate(flops=0, bytes_accessed=1 << 20, transcendentals=0),
        name="attend",
    )(units, unit_count, signs, *queries, before, current, later, *after)


def across(block, step):
    size = lax.axis_size("uly")
    return lax.ppermute(block, "uly", [(i, i ^ step) for i in range(size)])


def from_behind(block, distance):
    devices = range(lax.axis_size("blk"))
    route = [(i - distance, i) for i in devices if i - distance in devices]
    return lax.ppermute(block, "blk", route)


def shards(q_code, k_code, v_code, block_exp, window, window_count):
    rows, model_width = q_code.shape
    tile = rows // block_exp.shape[0]
    head_count = block_exp.shape[2]
    width = model_width // head_count
    ulysses = lax.axis_size("uly")
    local_heads = head_count // ulysses
    place = lax.axis_index("uly").astype(jnp.int32)
    z = place.reshape(1)
    factor = jnp.exp2(block_exp.astype(jnp.float32))
    signs = hadamard_signs(width)
    sizes = chunk_sizes(local_heads)
    firsts = [sum(sizes[:c]) for c in range(len(sizes))]
    steps = len(sizes)
    ahead = 2
    units, unit_count = unit_table(window, window_count, place, rows // tile, GROUP)
    arrived, halos, returned = {}, {}, {}
    last = []

    def send(c):
        nonlocal last
        packed = pack(
            z, factor, q_code, k_code, v_code, firsts[c], sizes[c], local_heads, width, ulysses, tile, last
        )
        last = [packed[0]]
        arrived[c] = [packed[0]] + [across(packed[k], k) for k in range(1, ulysses)]

    def spread(c):
        nonlocal last
        current = join(arrived[c], last)
        last = [current]
        halos[c] = (from_behind(current, 1), current, from_behind(current, -1))

    def compute(c):
        nonlocal last
        mixed = attend(z, units, unit_count, signs, arrived[c], *halos[c], width, tile, GROUP, last)
        last = [mixed[0]]
        returned[c] = [mixed[0]] + [across(mixed[k], k) for k in range(1, ulysses)]

    for c in range(min(ahead, steps)):
        send(c)
    for c in range(steps):
        spread(c)
        if c + ahead < steps:
            send(c + ahead)
        if c >= 1:
            compute(c - 1)
    compute(steps - 1)
    return collect(z, [returned[c] for c in range(steps)], firsts, local_heads, tile)


def solution(mesh):
    return jax.shard_map(
        shards,
        mesh=mesh,
        in_specs=(
            P(("blk", "uly"), None),
            P(("blk", "uly"), None),
            P(("blk", "uly"), None),
            P(("blk", "uly"), None, None),
            P("blk", None),
            P("blk"),
        ),
        out_specs=P(("blk", "uly"), None),
        check_vma=False,
    )
```

time: 2260 us -> 658 us (0.29)
  local copies, waits for them, and re-layouts: 642 us -> 8.33 us
  blocking collectives: 596 us -> 0 us
  matrix products: 514 us -> 0 us
  Pallas kernels: 0 us -> 231 us
  other arithmetic: 180 us -> 2.68 us
  starting transfers between devices: 6.45 us -> 125 us
  loops' own time: 55.2 us -> 0 us
  waiting for transfers between devices: 255 us -> 279 us
    all_to_all x2 -> x0, blocking collectives: 596 us -> none  [the longest x1 410 us: shards(): lax.all_to_all(stacked, 'uly', split_axis=2, concat_axis=1, tiled=True)]
    dot_general x144 -> x0, matrix products: 514 us -> none  [the longest x48 304 us: one_group(): jnp.einsum('gqnk,gnkd->gqd', expsum.astype(jnp.bfloat16), value_tiles, pr...]
    gather x96 -> x3, local copies, waits for them, and re-layouts: 277 us -> 1.9 us  [the longest x1 1.01 us: unit_table(): members = members[jnp.minimum(owner, frame_tiles - 1), order]]
    pallas_call x0 -> x22, Pallas kernels: none -> 231 us  [the longest x7 177 us: attend(): pl.pallas_call(body, grid_spec=pltpu.PrefetchScalarGridSpec(num_scalar_pr...]
    while x97 -> x0, local copies, waits for them, and re-layouts: 144 us -> none
    ppermute x2 -> x56, starting transfers between devices: 6.45 us -> 125 us  [the longest x14 86.4 us: from_behind(): return lax.ppermute(block, 'blk', route)]
    reduce_sum x48 -> x1, other arithmetic: 84.4 us -> 0.09 us  [unit_table(): owner = jnp.sum(unit[:, None] >= ends[None, :], axis=1).astype(jnp.int32)]
    dynamic_slice x84 -> x0, local copies, waits for them, and re-layouts: 84.2 us -> none  [the longest x48 29.2 us: one_head(): lax.map(one_group, jnp.arange(frame_tiles // group_size, dtype=jnp.int32))]
  transfers between devices with their start and end apart: 2 -> 56, of which waited for: 1 -> 22; matrix products, arithmetic and copies ran while one was open for 1% -> 1% of each run, Pallas kernels for 0% -> 34%
where the time goes in v1:
time: 658 us; the launch traced here: 646 us
  waiting for transfers between devices  279 us (42%)
  Pallas kernels  231 us (35%)
  starting transfers between devices  125 us (19%)
  local copies, waits for them, and re-layouts  8.33 us (1%)
    ppermute x42, waiting for transfers between devices, across(): return lax.ppermute(block, 'uly', [(i, i ^ step) for i in range(size)])  279 us
    pallas_call x7, Pallas kernels, attend(): pl.pallas_call(body, grid_spec=pltpu.PrefetchScalarGridSpec(num_scalar_pr...  177 us
    ppermute x14, starting transfers between devices, from_behind(): return lax.ppermute(block, 'blk', route)  86.4 us
    ppermute x42, starting transfers between devices, across(): return lax.ppermute(block, 'uly', [(i, i ^ step) for i in range(size)])  38.3 us
    pallas_call x7, Pallas kernels, pack(): pl.pallas_call(body, grid_spec=pltpu.PrefetchScalarGridSpec(num_scalar_pr...  23.8 us
    pallas_call x7, Pallas kernels, join(): pl.pallas_call(body, grid=(heads, 2), in_specs=[pl.BlockSpec((None, None,...  23.6 us
  transfers between devices with their start and end apart: 56, of which 22 were waited for; matrix products, arithmetic and copies ran while one was open for 1% of the time, Pallas kernels for 34%

profile of v1, /device:TPU:11, one launch (start us, length us, event | category | flops | bytes accessed | tf_op | source)
XLA Modules:
  0.0 646.4 jit_solution(10776801197564642014)
XLA Ops:
  11.2 26.5 %collective-permute-done.refs_1_ = bf16[3,2,512,128]{3,2,1,0:T(8,128)(2,1)S(1)} collective-permute-done((bf16[3,2,512,128]{3,2,1,0:T(8,128)(2,1)}, bf16[3,2,512,128]{3,2,1,0:T(8,128)(2,1)S(1)}, u32[]{:S(2)}, u32[]{:S(2)}) %collective-permute-start) | collective-permute-done | bytes 786464 | tf_op jit(solution)/shard_map/ppermute | solution.py:266
  41.5 33.6 %collective-permute-done.2.refs_3_ = bf16[3,2,512,128]{3,2,1,0:T(8,128)(2,1)S(1)} collective-permute-done((bf16[3,2,512,128]{3,2,1,0:T(8,128)(2,1)}, bf16[3,2,512,128]{3,2,1,0:T(8,128)(2,1)S(1)}, u32[]{:S(2)}, u32[]{:S(2)}) %collective-permute-start.2) | collective-permute-done | bytes 786464 | tf_op jit(solution)/shard_map/ppermute | solution.py:266
  79.8 4.8 collective-permute-start.3
  93.2 26.4 %collective-permute-done.5.refs_1_ = bf16[3,2,512,128]{3,2,1,0:T(8,128)(2,1)S(1)} collective-permute-done((bf16[3,2,512,128]{3,2,1,0:T(8,128)(2,1)}, bf16[3,2,512,128]{3,2,1,0:T(8,128)(2,1)S(1)}, u32[]{:S(2)}, u32[]{:S(2)}) %collective-permute-start.5) | collective-permute-done | bytes 786464 | tf_op jit(solution)/shard_map/ppermute | solution.py:266
  124.2 32.7 %collective-permute-done.7.refs_3_ = bf16[3,2,512,128]{3,2,1,0:T(8,128)(2,1)} collective-permute-done((bf16[3,2,512,128]{3,2,1,0:T(8,128)(2,1)}, bf16[3,2,512,128]{3,2,1,0:T(8,128)(2,1)}, u32[]{:S(2)}, u32[]{:S(2)}) %collective-permute-start.7) | collective-permute-done | bytes 786464 | tf_op jit(solution)/shard_map/ppermute | solution.py:266
  160.8 23.9 %collective-permute-start.11 = (bf16[2,2,2048,128]{3,2,1,0:T(8,128)(2,1)}, bf16[2,2,2048,128]{3,2,1,0:T(8,128)(2,1)}, u32[]{:S(2)}, u32[]{:S(2)}) collective-permute-start(bf16[2,2,2048,128]{3,2,1,0:T(8,128)(2,1)} %join.8.refs_12_.refs_5_), channel_id=1, source_target_pairs={{0,4},{4,8},{8,12},{12,16},{16,20},{20,24},{24,28},{1,5},{5,9},{9,... | collective-permute-start | bytes 6291464 | tf_op jit(solution)/shard_map/ppermute | solution.py:272
  197.6 29.0 %attend.7 = (bf16[2,512,128]{2,1,0:T(8,128)(2,1)}, bf16[2,512,128]{2,1,0:T(8,128)(2,1)}, bf16[2,512,128]{2,1,0:T(8,128)(2,1)}, bf16[2,512,128]{2,1,0:T(8,128)(2,1)}) custom-call(s32[572]{0:T(1024)} %reshape.230.unit_ref, s32[1]{0:T(128)} %bitcast.5.count_ref, bf16[128,128]{1,0:T(8,128)(2,1)} %select_convert_fusion.signs_ref, ...), custom_call_target="tpu_custom_call" | custom-call | bytes 1048576 | tf_op jit(solution)/shard_map/attend/pallas_call | solution.py:237
  229.6 3.9 join.9.refs_12_.refs_5_
  233.5 6.1 collective-permute-start.19
  241.5 19.3 %collective-permute-done.22.refs_2_ = bf16[3,2,512,128]{3,2,1,0:T(8,128)(2,1)S(1)} collective-permute-done((bf16[3,2,512,128]{3,2,1,0:T(8,128)(2,1)}, bf16[3,2,512,128]{3,2,1,0:T(8,128)(2,1)S(1)}, u32[]{:S(2)}, u32[]{:S(2)}) %collective-permute-start.22) | collective-permute-done | bytes 786464 | tf_op jit(solution)/shard_map/ppermute | solution.py:266
  264.7 31.6 %collective-permute-done.23.refs_3_ = bf16[3,2,512,128]{3,2,1,0:T(8,128)(2,1)S(1)} collective-permute-done((bf16[3,2,512,128]{3,2,1,0:T(8,128)(2,1)S(1)}, bf16[3,2,512,128]{3,2,1,0:T(8,128)(2,1)S(1)}, u32[]{:S(2)}, u32[]{:S(2)}) %collective-permute-start.23) | collective-permute-done | bytes 786464 | tf_op jit(solution)/shard_map/ppermute | solution.py:266
  298.9 28.8 %attend.8 = (bf16[2,512,128]{2,1,0:T(8,128)(2,1)}, bf16[2,512,128]{2,1,0:T(8,128)(2,1)}, bf16[2,512,128]{2,1,0:T(8,128)(2,1)}, bf16[2,512,128]{2,1,0:T(8,128)(2,1)}) custom-call(s32[572]{0:T(1024)} %reshape.230.unit_ref, s32[1]{0:T(128)} %bitcast.5.count_ref, bf16[128,128]{1,0:T(8,128)(2,1)} %select_convert_fusion.signs_ref, ...), custom_call_target="tpu_custom_call" | custom-call | bytes 1048576 | tf_op jit(solution)/shard_map/attend/pallas_call | solution.py:237
  327.7 3.9 join.10.refs_12_.refs_5_
  335.1 18.4 %collective-permute-start.28 = (bf16[2,2,2048,128]{3,2,1,0:T(8,128)(2,1)}, bf16[2,2,2048,128]{3,2,1,0:T(8,128)(2,1)}, u32[]{:S(2)}, u32[]{:S(2)}) collective-permute-start(bf16[2,2,2048,128]{3,2,1,0:T(8,128)(2,1)} %join.10.refs_12_.refs_5_), channel_id=1, source_target_pairs={{4,0},{8,4},{12,8},{16,12},{20,16},{24,20},{28,24},{5,1},{9,5},{13... | collective-permute-start | bytes 6291464 | tf_op jit(solution)/shard_map/ppermute | solution.py:272
  353.5 12.1 %collective-permute-done.31.refs_3_ = bf16[3,2,512,128]{3,2,1,0:T(8,128)(2,1)S(1)} collective-permute-done((bf16[3,2,512,128]{3,2,1,0:T(8,128)(2,1)}, bf16[3,2,512,128]{3,2,1,0:T(8,128)(2,1)S(1)}, u32[]{:S(2)}, u32[]{:S(2)}) %collective-permute-start.31) | collective-permute-done | bytes 786464 | tf_op jit(solution)/shard_map/ppermute | solution.py:266
  371.1 28.9 %attend.9 = (bf16[2,512,128]{2,1,0:T(8,128)(2,1)}, bf16[2,512,128]{2,1,0:T(8,128)(2,1)}, bf16[2,512,128]{2,1,0:T(8,128)(2,1)}, bf16[2,512,128]{2,1,0:T(8,128)(2,1)}) custom-call(s32[572]{0:T(1024)} %reshape.230.unit_ref, s32[1]{0:T(128)} %bitcast.5.count_ref, bf16[128,128]{1,0:T(8,128)(2,1)} %select_convert_fusion.signs_ref, ...), custom_call_target="tpu_custom_call" | custom-call | bytes 1048576 | tf_op jit(solution)/shard_map/attend/pallas_call | solution.py:237
  407.1 4.0 collective-permute-start.36
  411.9 5.6 collective-permute-done.16.refs_5_
  418.2 7.3 %collective-permute-done.37.refs_1_ = bf16[3,1,512,128]{3,2,1,0:T(8,128)(2,1)S(1)} collective-permute-done((bf16[3,1,512,128]{3,2,1,0:T(8,128)(2,1)S(1)}, bf16[3,1,512,128]{3,2,1,0:T(8,128)(2,1)S(1)}, u32[]{:S(2)}, u32[]{:S(2)}) %collective-permute-start.37) | collective-permute-done | bytes 393248 | tf_op jit(solution)/shard_map/ppermute | solution.py:266
  426.2 16.8 %collective-permute-done.38.refs_2_ = bf16[3,1,512,128]{3,2,1,0:T(8,128)(2,1)S(1)} collective-permute-done((bf16[3,1,512,128]{3,2,1,0:T(8,128)(2,1)}, bf16[3,1,512,128]{3,2,1,0:T(8,128)(2,1)S(1)}, u32[]{:S(2)}, u32[]{:S(2)}) %collective-permute-start.38) | collective-permute-done | bytes 393248 | tf_op jit(solution)/shard_map/ppermute | solution.py:266
  447.2 13.7 %collective-permute-done.39.refs_3_ = bf16[3,1,512,128]{3,2,1,0:T(8,128)(2,1)S(1)} collective-permute-done((bf16[3,1,512,128]{3,2,1,0:T(8,128)(2,1)}, bf16[3,1,512,128]{3,2,1,0:T(8,128)(2,1)S(1)}, u32[]{:S(2)}, u32[]{:S(2)}) %collective-permute-start.39) | collective-permute-done | bytes 393248 | tf_op jit(solution)/shard_map/ppermute | solution.py:266
  464.5 28.8 %attend.10 = (bf16[2,512,128]{2,1,0:T(8,128)(2,1)}, bf16[2,512,128]{2,1,0:T(8,128)(2,1)}, bf16[2,512,128]{2,1,0:T(8,128)(2,1)}, bf16[2,512,128]{2,1,0:T(8,128)(2,1)}) custom-call(s32[572]{0:T(1024)} %reshape.230.unit_ref, s32[1]{0:T(128)} %bitcast.5.count_ref, bf16[128,128]{1,0:T(8,128)(2,1)} %select_convert_fusion.signs_ref, ...), custom_call_target="tpu_custom_call" | custom-call | bytes 1048576 | tf_op jit(solution)/shard_map/attend/pallas_call | solution.py:237
  495.5 6.9 %collective-permute-start.43 = (bf16[1,2,2048,128]{3,2,1,0:T(8,128)(2,1)}, bf16[1,2,2048,128]{3,2,1,0:T(8,128)(2,1)}, u32[]{:S(2)}, u32[]{:S(2)}) collective-permute-start(bf16[1,2,2048,128]{3,2,1,0:T(8,128)(2,1)} %join.12.refs_7_.refs_5_), channel_id=1, source_target_pairs={{0,4},{4,8},{8,12},{12,16},{16,20},{20,24},{24,28},{1,5},{5,9},{9,... | collective-permute-start | bytes 3145736 | tf_op jit(solution)/shard_map/ppermute | solution.py:272
  507.9 28.8 %attend.11 = (bf16[2,512,128]{2,1,0:T(8,128)(2,1)}, bf16[2,512,128]{2,1,0:T(8,128)(2,1)}, bf16[2,512,128]{2,1,0:T(8,128)(2,1)}, bf16[2,512,128]{2,1,0:T(8,128)(2,1)}) custom-call(s32[572]{0:T(1024)} %reshape.230.unit_ref, s32[1]{0:T(128)} %bitcast.5.count_ref, bf16[128,128]{1,0:T(8,128)(2,1)} %select_convert_fusion.signs_ref, ...), custom_call_target="tpu_custom_call" | custom-call | bytes 1048576 | tf_op jit(solution)/shard_map/attend/pallas_call | solution.py:237
  538.9 5.4 collective-permute-start.51
  547.8 10.7 %collective-permute-done.25.refs_10_ = bf16[2,512,128]{2,1,0:T(8,128)(2,1)S(1)} collective-permute-done((bf16[2,512,128]{2,1,0:T(8,128)(2,1)}, bf16[2,512,128]{2,1,0:T(8,128)(2,1)S(1)}, u32[]{:S(2)}, u32[]{:S(2)}) %collective-permute-start.25) | collective-permute-done | bytes 262176 | tf_op jit(solution)/shard_map/ppermute | solution.py:266
  558.8 11.4 %collective-permute-done.26.refs_11_ = bf16[2,512,128]{2,1,0:T(8,128)(2,1)S(1)} collective-permute-done((bf16[2,512,128]{2,1,0:T(8,128)(2,1)}, bf16[2,512,128]{2,1,0:T(8,128)(2,1)S(1)}, u32[]{:S(2)}, u32[]{:S(2)}) %collective-permute-start.26) | collective-permute-done | bytes 262176 | tf_op jit(solution)/shard_map/ppermute | solution.py:266
  573.0 16.5 %attend.12 = (bf16[1,512,128]{2,1,0:T(8,128)(2,1)}, bf16[1,512,128]{2,1,0:T(8,128)(2,1)}, bf16[1,512,128]{2,1,0:T(8,128)(2,1)}, bf16[1,512,128]{2,1,0:T(8,128)(2,1)}) custom-call(s32[572]{0:T(1024)} %reshape.230.unit_ref, s32[1]{0:T(128)} %bitcast.5.count_ref, bf16[128,128]{1,0:T(8,128)(2,1)} %select_convert_fusion.signs_ref, ...), custom_call_target="tpu_custom_call" | custom-call | bytes 1048576 | tf_op jit(solution)/shard_map/attend/pallas_call | solution.py:237
  598.7 16.3 %attend.13 = (bf16[1,512,128]{2,1,0:T(8,128)(2,1)}, bf16[1,512,128]{2,1,0:T(8,128)(2,1)}, bf16[1,512,128]{2,1,0:T(8,128)(2,1)}, bf16[1,512,128]{2,1,0:T(8,128)(2,1)}) custom-call(s32[572]{0:T(1024)} %reshape.230.unit_ref, s32[1]{0:T(128)} %bitcast.5.count_ref, bf16[128,128]{1,0:T(8,128)(2,1)} %select_convert_fusion.signs_ref, ...), custom_call_target="tpu_custom_call" | custom-call | bytes 1048576 | tf_op jit(solution)/shard_map/attend/pallas_call | solution.py:237
  623.4 7.8 %collective-permute-done.42.refs_19_ = bf16[2,512,128]{2,1,0:T(8,128)(2,1)S(1)} collective-permute-done((bf16[2,512,128]{2,1,0:T(8,128)(2,1)}, bf16[2,512,128]{2,1,0:T(8,128)(2,1)S(1)}, u32[]{:S(2)}, u32[]{:S(2)}) %collective-permute-start.42) | collective-permute-done | bytes 262176 | tf_op jit(solution)/shard_map/ppermute | solution.py:266
  632.7 6.6 %collective-permute-done.55.refs_27_ = bf16[1,512,128]{2,1,0:T(8,128)(2,1)S(1)} collective-permute-done((bf16[1,512,128]{2,1,0:T(8,128)(2,1)}, bf16[1,512,128]{2,1,0:T(8,128)(2,1)S(1)}, u32[]{:S(2)}, u32[]{:S(2)}) %collective-permute-start.55) | collective-permute-done | bytes 131104 | tf_op jit(solution)/shard_map/ppermute | solution.py:266
  640.0 6.3 collect.1
  (225 shorter events, 122.8 us)
Async XLA Ops:
  5.1 36.4 %collective-permute-start.1 = (bf16[3,2,512,128]{3,2,1,0:T(8,128)(2,1)}, bf16[3,2,512,128]{3,2,1,0:T(8,128)(2,1)S(1)}, u32[]{:S(2)}, u32[]{:S(2)}) collective-permute-start(bf16[3,2,512,128]{3,2,1,0:T(8,128)(2,1)} %get-tuple-element.63), channel_id=1, source_target_pairs={{0,2},{1,3},{2,0},{3,1},{4,6},{5,7},{6,4},{7,5},{8,10},{9,11},{10,... | collective-permute-start | bytes 2359304 | tf_op jit(solution)/shard_map/ppermute | solution.py:266
  7.4 67.7 %collective-permute-start.2 = (bf16[3,2,512,128]{3,2,1,0:T(8,128)(2,1)}, bf16[3,2,512,128]{3,2,1,0:T(8,128)(2,1)S(1)}, u32[]{:S(2)}, u32[]{:S(2)}) collective-permute-start(bf16[3,2,512,128]{3,2,1,0:T(8,128)(2,1)} %get-tuple-element.64), channel_id=1, source_target_pairs={{0,3},{1,2},{2,1},{3,0},{4,7},{5,6},{6,5},{7,4},{8,11},{9,10},{10,... | collective-permute-start | bytes 2359304 | tf_op jit(solution)/shard_map/ppermute | solution.py:266
  79.8 113.0 %collective-permute-start.3 = (bf16[2,2,2048,128]{3,2,1,0:T(8,128)(2,1)}, bf16[2,2,2048,128]{3,2,1,0:T(8,128)(2,1)}, u32[]{:S(2)}, u32[]{:S(2)}) collective-permute-start(bf16[2,2,2048,128]{3,2,1,0:T(8,128)(2,1)} %join.7.refs_12_.refs_5_), channel_id=1, source_target_pairs={{0,4},{4,8},{8,12},{12,16},{16,20},{20,24},{24,28},{1,5},{5,9},{9,... | collective-permute-start | bytes 6291464 | tf_op jit(solution)/shard_map/ppermute | solution.py:272
  84.6 109.5 %collective-permute-start.4 = (bf16[2,2,2048,128]{3,2,1,0:T(8,128)(2,1)}, bf16[2,2,2048,128]{3,2,1,0:T(8,128)(2,1)}, u32[]{:S(2)}, u32[]{:S(2)}) collective-permute-start(bf16[2,2,2048,128]{3,2,1,0:T(8,128)(2,1)} %join.7.refs_12_.refs_5_), channel_id=1, source_target_pairs={{4,0},{8,4},{12,8},{16,12},{20,16},{24,20},{28,24},{5,1},{9,5},{13... | collective-permute-start | bytes 6291464 | tf_op jit(solution)/shard_map/ppermute | solution.py:272
  86.6 36.6 %collective-permute-start.6 = (bf16[3,2,512,128]{3,2,1,0:T(8,128)(2,1)}, bf16[3,2,512,128]{3,2,1,0:T(8,128)(2,1)S(1)}, u32[]{:S(2)}, u32[]{:S(2)}) collective-permute-start(bf16[3,2,512,128]{3,2,1,0:T(8,128)(2,1)} %get-tuple-element.67), channel_id=1, source_target_pairs={{0,2},{1,3},{2,0},{3,1},{4,6},{5,7},{6,4},{7,5},{8,10},{9,11},{10,... | collective-permute-start | bytes 2359304 | tf_op jit(solution)/shard_map/ppermute | solution.py:266
  89.1 67.9 %collective-permute-start.7 = (bf16[3,2,512,128]{3,2,1,0:T(8,128)(2,1)}, bf16[3,2,512,128]{3,2,1,0:T(8,128)(2,1)}, u32[]{:S(2)}, u32[]{:S(2)}) collective-permute-start(bf16[3,2,512,128]{3,2,1,0:T(8,128)(2,1)} %get-tuple-element.68), channel_id=1, source_target_pairs={{0,3},{1,2},{2,1},{3,0},{4,7},{5,6},{6,5},{7,4},{8,11},{9,10},{10,... | collective-permute-start | bytes 2359304 | tf_op jit(solution)/shard_map/ppermute | solution.py:266
  119.6 65.2 %collective-permute-start.13 = (bf16[3,2,512,128]{3,2,1,0:T(8,128)(2,1)}, bf16[3,2,512,128]{3,2,1,0:T(8,128)(2,1)S(1)}, u32[]{:S(2)}, u32[]{:S(2)}) collective-permute-start(bf16[3,2,512,128]{3,2,1,0:T(8,128)(2,1)} %get-tuple-element.75), channel_id=1, source_target_pairs={{0,1},{1,0},{2,3},{3,2},{4,5},{5,4},{6,7},{7,6},{8,9},{9,8},{10,11... | collective-permute-start | bytes 2359304 | tf_op jit(solution)/shard_map/ppermute | solution.py:266
  124.1 67.3 %collective-permute-start.14 = (bf16[3,2,512,128]{3,2,1,0:T(8,128)(2,1)}, bf16[3,2,512,128]{3,2,1,0:T(8,128)(2,1)S(1)}, u32[]{:S(2)}, u32[]{:S(2)}) collective-permute-start(bf16[3,2,512,128]{3,2,1,0:T(8,128)(2,1)} %get-tuple-element.76), channel_id=1, source_target_pairs={{0,2},{1,3},{2,0},{3,1},{4,6},{5,7},{6,4},{7,5},{8,10},{9,11},{10,... | collective-permute-start | bytes 2359304 | tf_op jit(solution)/shard_map/ppermute | solution.py:266
  160.8 135.5 %collective-permute-start.11 = (bf16[2,2,2048,128]{3,2,1,0:T(8,128)(2,1)}, bf16[2,2,2048,128]{3,2,1,0:T(8,128)(2,1)}, u32[]{:S(2)}, u32[]{:S(2)}) collective-permute-start(bf16[2,2,2048,128]{3,2,1,0:T(8,128)(2,1)} %join.8.refs_12_.refs_5_), channel_id=1, source_target_pairs={{0,4},{4,8},{8,12},{12,16},{16,20},{20,24},{24,28},{1,5},{5,9},{9,... | collective-permute-start | bytes 6291464 | tf_op jit(solution)/shard_map/ppermute | solution.py:272
  184.8 112.4 %collective-permute-start.12 = (bf16[2,2,2048,128]{3,2,1,0:T(8,128)(2,1)}, bf16[2,2,2048,128]{3,2,1,0:T(8,128)(2,1)}, u32[]{:S(2)}, u32[]{:S(2)}) collective-permute-start(bf16[2,2,2048,128]{3,2,1,0:T(8,128)(2,1)} %join.8.refs_12_.refs_5_), channel_id=1, source_target_pairs={{4,0},{8,4},{12,8},{16,12},{20,16},{24,20},{28,24},{5,1},{9,5},{13... | collective-permute-start | bytes 6291464 | tf_op jit(solution)/shard_map/ppermute | solution.py:272
  191.4 37.2 %collective-permute-start.15 = (bf16[3,2,512,128]{3,2,1,0:T(8,128)(2,1)}, bf16[3,2,512,128]{3,2,1,0:T(8,128)(2,1)S(1)}, u32[]{:S(2)}, u32[]{:S(2)}) collective-permute-start(bf16[3,2,512,128]{3,2,1,0:T(8,128)(2,1)} %get-tuple-element.77), channel_id=1, source_target_pairs={{0,3},{1,2},{2,1},{3,0},{4,7},{5,6},{6,5},{7,4},{8,11},{9,10},{10,... | collective-permute-start | bytes 2359304 | tf_op jit(solution)/shard_map/ppermute | solution.py:266
  192.8 46.8 %collective-permute-start.21 = (bf16[3,2,512,128]{3,2,1,0:T(8,128)(2,1)}, bf16[3,2,512,128]{3,2,1,0:T(8,128)(2,1)S(1)}, u32[]{:S(2)}, u32[]{:S(2)}) collective-permute-start(bf16[3,2,512,128]{3,2,1,0:T(8,128)(2,1)} %get-tuple-element.83), channel_id=1, source_target_pairs={{0,1},{1,0},{2,3},{3,2},{4,5},{5,4},{6,7},{7,6},{8,9},{9,8},{10,11... | collective-permute-start | bytes 2359304 | tf_op jit(solution)/shard_map/ppermute | solution.py:266
  194.1 66.7 %collective-permute-start.22 = (bf16[3,2,512,128]{3,2,1,0:T(8,128)(2,1)}, bf16[3,2,512,128]{3,2,1,0:T(8,128)(2,1)S(1)}, u32[]{:S(2)}, u32[]{:S(2)}) collective-permute-start(bf16[3,2,512,128]{3,2,1,0:T(8,128)(2,1)} %get-tuple-element.84), channel_id=1, source_target_pairs={{0,2},{1,3},{2,0},{3,1},{4,6},{5,7},{6,4},{7,5},{8,10},{9,11},{10,... | collective-permute-start | bytes 2359304 | tf_op jit(solution)/shard_map/ppermute | solution.py:266
  233.5 132.1 %collective-permute-start.19 = (bf16[2,2,2048,128]{3,2,1,0:T(8,128)(2,1)}, bf16[2,2,2048,128]{3,2,1,0:T(8,128)(2,1)}, u32[]{:S(2)}, u32[]{:S(2)}) collective-permute-start(bf16[2,2,2048,128]{3,2,1,0:T(8,128)(2,1)} %join.9.refs_12_.refs_5_), channel_id=1, source_target_pairs={{0,4},{4,8},{8,12},{12,16},{16,20},{20,24},{24,28},{1,5},{5,9},{9,... | collective-permute-start | bytes 6291464 | tf_op jit(solution)/shard_map/ppermute | solution.py:272
  239.6 126.8 %collective-permute-start.20 = (bf16[2,2,2048,128]{3,2,1,0:T(8,128)(2,1)}, bf16[2,2,2048,128]{3,2,1,0:T(8,128)(2,1)}, u32[]{:S(2)}, u32[]{:S(2)}) collective-permute-start(bf16[2,2,2048,128]{3,2,1,0:T(8,128)(2,1)} %join.9.refs_12_.refs_5_), channel_id=1, source_target_pairs={{4,0},{8,4},{12,8},{16,12},{20,16},{24,20},{28,24},{5,1},{9,5},{13... | collective-permute-start | bytes 6291464 | tf_op jit(solution)/shard_map/ppermute | solution.py:272
  296.2 38.8 %collective-permute-start.30 = (bf16[3,2,512,128]{3,2,1,0:T(8,128)(2,1)}, bf16[3,2,512,128]{3,2,1,0:T(8,128)(2,1)S(1)}, u32[]{:S(2)}, u32[]{:S(2)}) collective-permute-start(bf16[3,2,512,128]{3,2,1,0:T(8,128)(2,1)} %get-tuple-element.92), channel_id=1, source_target_pairs={{0,2},{1,3},{2,0},{3,1},{4,6},{5,7},{6,4},{7,5},{8,10},{9,11},{10,... | collective-permute-start | bytes 2359304 | tf_op jit(solution)/shard_map/ppermute | solution.py:266
  297.2 68.4 %collective-permute-start.31 = (bf16[3,2,512,128]{3,2,1,0:T(8,128)(2,1)}, bf16[3,2,512,128]{3,2,1,0:T(8,128)(2,1)S(1)}, u32[]{:S(2)}, u32[]{:S(2)}) collective-permute-start(bf16[3,2,512,128]{3,2,1,0:T(8,128)(2,1)} %get-tuple-element.93), channel_id=1, source_target_pairs={{0,3},{1,2},{2,1},{3,0},{4,7},{5,6},{6,5},{7,4},{8,11},{9,10},{10,... | collective-permute-start | bytes 2359304 | tf_op jit(solution)/shard_map/ppermute | solution.py:266
  331.6 130.0 %collective-permute-start.27 = (bf16[2,2,2048,128]{3,2,1,0:T(8,128)(2,1)}, bf16[2,2,2048,128]{3,2,1,0:T(8,128)(2,1)}, u32[]{:S(2)}, u32[]{:S(2)}) collective-permute-start(bf16[2,2,2048,128]{3,2,1,0:T(8,128)(2,1)} %join.10.refs_12_.refs_5_), channel_id=1, source_target_pairs={{0,4},{4,8},{8,12},{12,16},{16,20},{20,24},{24,28},{1,5},{5,9},{9,... | collective-permute-start | bytes 6291464 | tf_op jit(solution)/shard_map/ppermute | solution.py:272
  335.1 129.4 %collective-permute-start.28 = (bf16[2,2,2048,128]{3,2,1,0:T(8,128)(2,1)}, bf16[2,2,2048,128]{3,2,1,0:T(8,128)(2,1)}, u32[]{:S(2)}, u32[]{:S(2)}) collective-permute-start(bf16[2,2,2048,128]{3,2,1,0:T(8,128)(2,1)} %join.10.refs_12_.refs_5_), channel_id=1, source_target_pairs={{4,0},{8,4},{12,8},{16,12},{20,16},{24,20},{28,24},{5,1},{9,5},{13... | collective-permute-start | bytes 6291464 | tf_op jit(solution)/shard_map/ppermute | solution.py:272
  365.6 38.2 %collective-permute-start.8 = (bf16[2,512,128]{2,1,0:T(8,128)(2,1)}, bf16[2,512,128]{2,1,0:T(8,128)(2,1)S(1)}, u32[]{:S(2)}, u32[]{:S(2)}) collective-permute-start(bf16[2,512,128]{2,1,0:T(8,128)(2,1)} %get-tuple-element.72), channel_id=1, source_target_pairs={{0,1},{1,0},{2,3},{3,2},{4,5},{5,4},{6,7},{7,6},{8,9},{9,8},{10,11... | collective-permute-start | bytes 786440 | tf_op jit(solution)/shard_map/ppermute | solution.py:266
  365.6 41.5 %collective-permute-start.9 = (bf16[2,512,128]{2,1,0:T(8,128)(2,1)S(1)}, bf16[2,512,128]{2,1,0:T(8,128)(2,1)S(1)}, u32[]{:S(2)}, u32[]{:S(2)}) collective-permute-start(bf16[2,512,128]{2,1,0:T(8,128)(2,1)S(1)} %copy-done.47), channel_id=1, source_target_pairs={{0,2},{1,3},{2,0},{3,1},{4,6},{5,7},{6,4},{7,5},{8,10},{9,11},{10,... | collective-permute-start | bytes 786440 | tf_op jit(solution)/shard_map/ppermute | solution.py:266
  366.4 44.7 %collective-permute-start.10 = (bf16[2,512,128]{2,1,0:T(8,128)(2,1)S(1)}, bf16[2,512,128]{2,1,0:T(8,128)(2,1)S(1)}, u32[]{:S(2)}, u32[]{:S(2)}) collective-permute-start(bf16[2,512,128]{2,1,0:T(8,128)(2,1)S(1)} %copy-done.46), channel_id=1, source_target_pairs={{0,3},{1,2},{2,1},{3,0},{4,7},{5,6},{6,5},{7,4},{8,11},{9,10},{10,... | collective-permute-start | bytes 786440 | tf_op jit(solution)/shard_map/ppermute | solution.py:266
  403.8 102.3 %collective-permute-start.35 = (bf16[2,2,2048,128]{3,2,1,0:T(8,128)(2,1)}, bf16[2,2,2048,128]{3,2,1,0:T(8,128)(2,1)S(1)}, u32[]{:S(2)}, u32[]{:S(2)}) collective-permute-start(bf16[2,2,2048,128]{3,2,1,0:T(8,128)(2,1)} %join.11.refs_12_.refs_5_), channel_id=1, source_target_pairs={{0,4},{4,8},{8,12},{12,16},{16,20},{20,24},{24,28},{1,5},{5,9},{9,... | collective-permute-start | bytes 6291464 | tf_op jit(solution)/shard_map/ppermute | solution.py:272
  407.1 99.4 %collective-permute-start.36 = (bf16[2,2,2048,128]{3,2,1,0:T(8,128)(2,1)}, bf16[2,2,2048,128]{3,2,1,0:T(8,128)(2,1)}, u32[]{:S(2)}, u32[]{:S(2)}) collective-permute-start(bf16[2,2,2048,128]{3,2,1,0:T(8,128)(2,1)} %join.11.refs_12_.refs_5_), channel_id=1, source_target_pairs={{4,0},{8,4},{12,8},{16,12},{20,16},{24,20},{28,24},{5,1},{9,5},{13... | collective-permute-start | bytes 6291464 | tf_op jit(solution)/shard_map/ppermute | solution.py:272
  461.6 40.7 %collective-permute-start.46 = (bf16[3,1,512,128]{3,2,1,0:T(8,128)(2,1)}, bf16[3,1,512,128]{3,2,1,0:T(8,128)(2,1)S(1)}, u32[]{:S(2)}, u32[]{:S(2)}) collective-permute-start(bf16[3,1,512,128]{3,2,1,0:T(8,128)(2,1)} %get-tuple-element.107), channel_id=1, source_target_pairs={{0,2},{1,3},{2,0},{3,1},{4,6},{5,7},{6,4},{7,5},{8,10},{9,11},{10,... | collective-permute-start | bytes 1179656 | tf_op jit(solution)/shard_map/ppermute | solution.py:266
  464.5 39.8 %collective-permute-start.47 = (bf16[3,1,512,128]{3,2,1,0:T(8,128)(2,1)}, bf16[3,1,512,128]{3,2,1,0:T(8,128)(2,1)S(1)}, u32[]{:S(2)}, u32[]{:S(2)}) collective-permute-start(bf16[3,1,512,128]{3,2,1,0:T(8,128)(2,1)} %get-tuple-element.108), channel_id=1, source_target_pairs={{0,3},{1,2},{2,1},{3,0},{4,7},{5,6},{6,5},{7,4},{8,11},{9,10},{10,... | collective-permute-start | bytes 1179656 | tf_op jit(solution)/shard_map/ppermute | solution.py:266
  495.5 74.8 %collective-permute-start.43 = (bf16[1,2,2048,128]{3,2,1,0:T(8,128)(2,1)}, bf16[1,2,2048,128]{3,2,1,0:T(8,128)(2,1)}, u32[]{:S(2)}, u32[]{:S(2)}) collective-permute-start(bf16[1,2,2048,128]{3,2,1,0:T(8,128)(2,1)} %join.12.refs_7_.refs_5_), channel_id=1, source_target_pairs={{0,4},{4,8},{8,12},{12,16},{16,20},{20,24},{24,28},{1,5},{5,9},{9,... | collective-permute-start | bytes 3145736 | tf_op jit(solution)/shard_map/ppermute | solution.py:272
  502.4 69.9 %collective-permute-start.44 = (bf16[1,2,2048,128]{3,2,1,0:T(8,128)(2,1)}, bf16[1,2,2048,128]{3,2,1,0:T(8,128)(2,1)}, u32[]{:S(2)}, u32[]{:S(2)}) collective-permute-start(bf16[1,2,2048,128]{3,2,1,0:T(8,128)(2,1)} %join.12.refs_7_.refs_5_), channel_id=1, source_target_pairs={{4,0},{8,4},{12,8},{16,12},{20,16},{24,20},{28,24},{5,1},{9,5},{13... | collective-permute-start | bytes 3145736 | tf_op jit(solution)/shard_map/ppermute | solution.py:272
  506.2 38.2 %collective-permute-start.18 = (bf16[2,512,128]{2,1,0:T(8,128)(2,1)}, bf16[2,512,128]{2,1,0:T(8,128)(2,1)S(1)}, u32[]{:S(2)}, u32[]{:S(2)}) collective-permute-start(bf16[2,512,128]{2,1,0:T(8,128)(2,1)} %get-tuple-element.82), channel_id=1, source_target_pairs={{0,3},{1,2},{2,1},{3,0},{4,7},{5,6},{6,5},{7,4},{8,11},{9,10},{10,... | collective-permute-start | bytes 786440 | tf_op jit(solution)/shard_map/ppermute | solution.py:266
  506.5 40.3 %collective-permute-start.24 = (bf16[2,512,128]{2,1,0:T(8,128)(2,1)}, bf16[2,512,128]{2,1,0:T(8,128)(2,1)S(1)}, u32[]{:S(2)}, u32[]{:S(2)}) collective-permute-start(bf16[2,512,128]{2,1,0:T(8,128)(2,1)} %get-tuple-element.88), channel_id=1, source_target_pairs={{0,1},{1,0},{2,3},{3,2},{4,5},{5,4},{6,7},{7,6},{8,9},{9,8},{10,11... | collective-permute-start | bytes 786440 | tf_op jit(solution)/shard_map/ppermute | solution.py:266
  538.9 57.8 %collective-permute-start.51 = (bf16[1,2,2048,128]{3,2,1,0:T(8,128)(2,1)}, bf16[1,2,2048,128]{3,2,1,0:T(8,128)(2,1)S(1)}, u32[]{:S(2)}, u32[]{:S(2)}) collective-permute-start(bf16[1,2,2048,128]{3,2,1,0:T(8,128)(2,1)} %join.13.refs_7_.refs_5_), channel_id=1, source_target_pairs={{0,4},{4,8},{8,12},{12,16},{16,20},{20,24},{24,28},{1,5},{5,9},{9,... | collective-permute-start | bytes 3145736 | tf_op jit(solution)/shard_map/ppermute | solution.py:272
  544.4 53.3 %collective-permute-start.52 = (bf16[1,2,2048,128]{3,2,1,0:T(8,128)(2,1)}, bf16[1,2,2048,128]{3,2,1,0:T(8,128)(2,1)S(1)}, u32[]{:S(2)}, u32[]{:S(2)}) collective-permute-start(bf16[1,2,2048,128]{3,2,1,0:T(8,128)(2,1)} %join.13.refs_7_.refs_5_), channel_id=1, source_target_pairs={{4,0},{8,4},{12,8},{16,12},{20,16},{24,20},{28,24},{5,1},{9,5},{13... | collective-permute-start | bytes 3145736 | tf_op jit(solution)/shard_map/ppermute | solution.py:272
  (73 other events, 1674.1 us)

commit v2 on v1

--- a/solution.py
+++ b/solution.py
@@ -11,6 +11,9 @@
 ANYWHERE = pl.BlockSpec(memory_space=pl.ANY)
 GROUP = 9
 VMEM = 60 << 20
+SIZES = (2, 2, 2, 2, 2, 2)
+BACK = (4, 2)
+AHEAD = 2
 
 
 def hadamard_signs(order):
@@ -22,11 +25,11 @@
     return jnp.where(parity % 2 == 0, 1.0, -1.0).astype(jnp.bfloat16)
 
 
-def chunk_sizes(local_heads):
+def cut(local_heads):
     if local_heads % 12 == 0:
         unit = local_heads // 12
-        return [unit * size for size in (2, 2, 2, 2, 2, 1, 1)]
-    return [1] * local_heads
+        return [unit * size for size in SIZES], BACK
+    return [1] * local_heads, [local_heads - 2, 2] if local_heads > 2 else [local_heads]
 
 
 def params():
@@ -94,7 +97,7 @@
     )(*pieces, *after)
 
 
-def collect(z, returned, firsts, local_heads, tile):
+def collect(z, returned, heads_before, local_heads, tile):
     ulysses = len(returned[0])
     _, rows, width = returned[0][0].shape
     model_width = ulysses * local_heads * width
@@ -104,7 +107,7 @@
         out = refs[-1]
         for ref, (c, k) in zip(refs, pieces):
             for h in range(ref.shape[0]):
-                column = ((z_ref[0] ^ k) * local_heads + firsts[c] + h) * width
+                column = ((z_ref[0] ^ k) * local_heads + heads_before[c] + h) * width
                 out[:, pl.ds(pl.multiple_of(column, width), width)] = ref[h]
 
     return pl.pallas_call(
@@ -125,7 +128,7 @@
     )(z, *[returned[c][k] for c, k in pieces])
 
 
-def unit_table(window, window_count, z, per_piece, group):
+def unit_table(window, window_count, z, odd, per_piece, group):
     frame_tiles, slot_total = window.shape
     groups = window_count // group
     ends = jnp.cumsum(groups)
@@ -135,18 +138,20 @@
 
     def placed(tiles):
         frame, inside = tiles // frame_tiles, tiles % frame_tiles
-        return frame * frame_tiles + ((inside // per_piece) ^ z) * per_piece + inside % per_piece
+        slot = jnp.where(frame == 1, 1, jnp.where(odd == 1, frame, 2 - frame))
+        return slot * frame_tiles + ((inside // per_piece) ^ z) * per_piece + inside % per_piece
 
     members = placed(window).reshape(frame_tiles, slot_total // group, group)
     members = members[jnp.minimum(owner, frame_tiles - 1), order]
     spare = owner >= frame_tiles
-    own = jnp.where(spare, frame_tiles, placed(jnp.minimum(owner, frame_tiles - 1)))
+    inside = jnp.minimum(owner, frame_tiles - 1)
+    own = jnp.where(spare, frame_tiles, ((inside // per_piece) ^ z) * per_piece + inside % per_piece)
     first = (order == 0) | spare
     head = jnp.stack([own, first.astype(jnp.int32)], axis=1)
     return jnp.concatenate([head, members], axis=1).reshape(-1), ends[-1:]
 
 
-def attend(z, units, unit_count, signs, queries, before, current, later, width, tile, group, after):
+def attend(units, unit_count, signs, queries, near, current, far, filled, place, total_heads, width, tile, group, after):
     ulysses = len(queries)
     heads, _, frame_rows, _ = current.shape
     rows = frame_rows // ulysses
@@ -160,7 +165,7 @@
     def body(unit_ref, count_ref, signs_ref, *refs):
         query_refs = refs[:ulysses]
         frames = refs[ulysses : ulysses + 3]
-        refs = refs[ulysses + 3 + len(after) :]
+        refs = refs[ulysses + 3 + len(filled) + len(after) :]
         outs = refs[:ulysses]
         keys, values, query_all, tops, total_all, sum_all = refs[ulysses : ulysses + 6]
         scores = refs[ulysses + 6 :]
@@ -242,8 +247,8 @@
             in_specs=[pl.BlockSpec((width, width), lambda h, *_: (0, 0))]
             + [pl.BlockSpec((None, None, rows, width), lambda h, *_: (2, h, 0, 0))] * ulysses
             + [frame_spec] * 3
-            + [ANYWHERE] * len(after),
-            out_specs=[pl.BlockSpec((None, rows, width), lambda h, *_: (h, 0, 0))] * ulysses,
+            + [ANYWHERE] * (len(filled) + len(after)),
+            out_specs=[pl.BlockSpec((None, rows, width), lambda h, *_: (place + h, 0, 0))] * ulysses,
             scratch_shapes=[
                 pltpu.VMEM((3 * frame_rows, width), jnp.bfloat16),
                 pltpu.VMEM((3 * frame_rows, width), jnp.bfloat16),
@@ -254,11 +259,12 @@
             ]
             + [pltpu.VMEM((tile, span), jnp.float32)] * ring,
         ),
-        out_shape=[jax.ShapeDtypeStruct((heads, rows, width), jnp.bfloat16)] * ulysses,
+        out_shape=[jax.ShapeDtypeStruct((total_heads, rows, width), jnp.bfloat16)] * ulysses,
+        input_output_aliases={6 + ulysses + k: k for k in range(len(filled))},
         compiler_params=pltpu.CompilerParams(vmem_limit_bytes=60 << 20),
         cost_estimate=pl.CostEstimate(flops=0, bytes_accessed=1 << 20, transcendentals=0),
         name="attend",
-    )(units, unit_count, signs, *queries, before, current, later, *after)
+    )(units, unit_count, signs, *queries, near, current, far, *filled, *after)
 
 
 def across(block, step):
@@ -266,10 +272,10 @@
     return lax.ppermute(block, "uly", [(i, i ^ step) for i in range(size)])
 
 
-def from_behind(block, distance):
-    devices = range(lax.axis_size("blk"))
-    route = [(i - distance, i) for i in devices if i - distance in devices]
-    return lax.ppermute(block, "blk", route)
+def swapped(block, odd):
+    size = lax.axis_size("blk")
+    pairs = [(i, i + 1) for i in range(odd, size - 1, 2)]
+    return lax.ppermute(block, "blk", pairs + [(b, a) for a, b in pairs])
 
 
 def shards(q_code, k_code, v_code, block_exp, window, window_count):
@@ -283,13 +289,15 @@
     z = place.reshape(1)
     factor = jnp.exp2(block_exp.astype(jnp.float32))
     signs = hadamard_signs(width)
-    sizes = chunk_sizes(local_heads)
+    sizes, shared = cut(local_heads)
     firsts = [sum(sizes[:c]) for c in range(len(sizes))]
     steps = len(sizes)
-    ahead = 2
-    units, unit_count = unit_table(window, window_count, place, rows // tile, GROUP)
-    arrived, halos, returned = {}, {}, {}
+    odd = lax.axis_index("blk").astype(jnp.int32) % 2
+    units, unit_count = unit_table(window, window_count, place, odd, rows // tile, GROUP)
+    arrived, halos, returned = {}, {}, []
     last = []
+    ends = [sum(shared[: g + 1]) for g in range(len(shared))]
+    filled, group_first, heads_before = [], 0, []
 
     def send(c):
         nonlocal last
@@ -303,24 +311,32 @@
         nonlocal last
         current = join(arrived[c], last)
         last = [current]
-        halos[c] = (from_behind(current, 1), current, from_behind(current, -1))
+        halos[c] = (swapped(current, 0), current, swapped(current, 1))
 
     def compute(c):
-        nonlocal last
-        mixed = attend(z, units, unit_count, signs, arrived[c], *halos[c], width, tile, GROUP, last)
-        last = [mixed[0]]
-        returned[c] = [mixed[0]] + [across(mixed[k], k) for k in range(1, ulysses)]
-
-    for c in range(min(ahead, steps)):
+        nonlocal last, filled, group_first
+        group_end = min(end for end in ends if end > c)
+        total_heads = sum(sizes[group_first:group_end])
+        filled = attend(
+            units, unit_count, signs, arrived[c], *halos[c], filled,
+            firsts[c] - firsts[group_first], total_heads, width, tile, GROUP, last,
+        )
+        last = [filled[0]]
+        if c + 1 == group_end:
+            returned.append([filled[0]] + [across(filled[k], k) for k in range(1, ulysses)])
+            heads_before.append(firsts[group_first])
+            filled, group_first = [], group_end
+
+    for c in range(min(AHEAD, steps)):
         send(c)
     for c in range(steps):
         spread(c)
-        if c + ahead < steps:
-            send(c + ahead)
+        if c + AHEAD < steps:
+            send(c + AHEAD)
         if c >= 1:
             compute(c - 1)
     compute(steps - 1)
-    return collect(z, [returned[c] for c in range(steps)], firsts, local_heads, tile)
+    return collect(z, returned, heads_before, local_heads, tile)
 
 
 def solution(mesh):

time: 658 us -> 597 us (0.907); the launches traced: 646 us -> 597 us
  waiting for transfers between devices: 279 us -> 253 us
  starting transfers between devices: 125 us -> 107 us
  Pallas kernels: 231 us -> 224 us
    ppermute x42 -> x24, waiting for transfers between devices: 279 us -> 234 us  [across(): return lax.ppermute(block, 'uly', [(i, i ^ step) for i in range(size)])]
    ppermute x14 -> x12, waiting for transfers between devices: 0.04 us -> 19.1 us  [swapped(): return lax.ppermute(block, 'blk', pairs + [(b, a) for a, b in pairs])]
    ppermute x42 -> x24, starting transfers between devices: 38.3 us -> 25.7 us  [across(): return lax.ppermute(block, 'uly', [(i, i ^ step) for i in range(size)])]
    ppermute x14 -> x12, starting transfers between devices: 86.4 us -> 80.8 us  [swapped(): return lax.ppermute(block, 'blk', pairs + [(b, a) for a, b in pairs])]
    pallas_call x7 -> x6, Pallas kernels: 177 us -> 173 us  [attend(): pl.pallas_call(body, grid_spec=pltpu.PrefetchScalarGridSpec(num_scalar_pr...]
    pallas_call x7 -> x6, Pallas kernels: 23.8 us -> 21.9 us  [pack(): pl.pallas_call(body, grid_spec=pltpu.PrefetchScalarGridSpec(num_scalar_pr...]
    pallas_call x7 -> x6, Pallas kernels: 23.6 us -> 23.2 us  [join(): pl.pallas_call(body, grid=(heads, 2), in_specs=[pl.BlockSpec((None, None,...]
  transfers between devices with their start and end apart: 56 -> 36, of which waited for: 22 -> 15; matrix products, arithmetic and copies ran while one was open for 1% -> 1% of each run, Pallas kernels for 34% -> 36%
where the time goes in v2:
time: 597 us
  waiting for transfers between devices  253 us (42%)
  Pallas kernels  224 us (38%)
  starting transfers between devices  107 us (18%)
  local copies, waits for them, and re-layouts  9.89 us (2%)
    ppermute x24, waiting for transfers between devices, across(): return lax.ppermute(block, 'uly', [(i, i ^ step) for i in range(size)])  234 us
    pallas_call x6, Pallas kernels, attend(): pl.pallas_call(body, grid_spec=pltpu.PrefetchScalarGridSpec(num_scalar_pr...  173 us
    ppermute x12, starting transfers between devices, swapped(): return lax.ppermute(block, 'blk', pairs + [(b, a) for a, b in pairs])  80.8 us
    ppermute x24, starting transfers between devices, across(): return lax.ppermute(block, 'uly', [(i, i ^ step) for i in range(size)])  25.7 us
    pallas_call x6, Pallas kernels, join(): pl.pallas_call(body, grid=(heads, 2), in_specs=[pl.BlockSpec((None, None,...  23.2 us
    pallas_call x6, Pallas kernels, pack(): pl.pallas_call(body, grid_spec=pltpu.PrefetchScalarGridSpec(num_scalar_pr...  21.9 us
    ppermute x12, waiting for transfers between devices, swapped(): return lax.ppermute(block, 'blk', pairs + [(b, a) for a, b in pairs])  19.1 us
  transfers between devices with their start and end apart: 36, of which 15 were waited for; matrix products, arithmetic and copies ran while one was open for 1% of the time, Pallas kernels for 36%

profile of v2, /device:TPU:11, one launch (start us, length us, event | category | flops | bytes accessed | tf_op | source)
XLA Modules:
  0.0 596.6 jit_solution(17626059363896865394)
XLA Ops:
  14.6 23.2 %collective-permute-done.3.refs_1_ = bf16[3,2,512,128]{3,2,1,0:T(8,128)(2,1)S(1)} collective-permute-done((bf16[3,2,512,128]{3,2,1,0:T(8,128)(2,1)}, bf16[3,2,512,128]{3,2,1,0:T(8,128)(2,1)S(1)}, u32[]{:S(2)}, u32[]{:S(2)}) %collective-permute-start.3) | collective-permute-done | bytes 786464 | tf_op jit(solution)/shard_map/ppermute | solution.py:272
  41.5 33.7 %collective-permute-done.5.refs_3_ = bf16[3,2,512,128]{3,2,1,0:T(8,128)(2,1)S(1)} collective-permute-done((bf16[3,2,512,128]{3,2,1,0:T(8,128)(2,1)}, bf16[3,2,512,128]{3,2,1,0:T(8,128)(2,1)S(1)}, u32[]{:S(2)}, u32[]{:S(2)}) %collective-permute-start.5) | collective-permute-done | bytes 786464 | tf_op jit(solution)/shard_map/ppermute | solution.py:272
  76.1 3.8 join.6.refs_12_.refs_5_
  87.2 36.4 %collective-permute-start.11 = (bf16[2,2,2048,128]{3,2,1,0:T(8,128)(2,1)S(1)}, bf16[2,2,2048,128]{3,2,1,0:T(8,128)(2,1)}, u32[]{:S(2)}, u32[]{:S(2)}) collective-permute-start(bf16[2,2,2048,128]{3,2,1,0:T(8,128)(2,1)S(1)} %copy-done), channel_id=1, source_target_pairs={{0,4},{8,12},{16,20},{24,28},{4,0},{12,8},{20,16},{28,24},{1,5},{9... | collective-permute-start | bytes 6291464 | tf_op jit(solution)/shard_map/ppermute | solution.py:278
  123.6 9.8 %collective-permute-done.1.refs_2_ = bf16[3,2,512,128]{3,2,1,0:T(8,128)(2,1)} collective-permute-done((bf16[3,2,512,128]{3,2,1,0:T(8,128)(2,1)}, bf16[3,2,512,128]{3,2,1,0:T(8,128)(2,1)}, u32[]{:S(2)}, u32[]{:S(2)}) %collective-permute-start.1) | collective-permute-done | bytes 786464 | tf_op jit(solution)/shard_map/ppermute | solution.py:272
  133.4 14.7 %collective-permute-start.12 = (bf16[2,2,2048,128]{3,2,1,0:T(8,128)(2,1)S(1)}, bf16[2,2,2048,128]{3,2,1,0:T(8,128)(2,1)}, u32[]{:S(2)}, u32[]{:S(2)}) collective-permute-start(bf16[2,2,2048,128]{3,2,1,0:T(8,128)(2,1)S(1)} %copy-done), channel_id=1, source_target_pairs={{4,8},{12,16},{20,24},{8,4},{16,12},{24,20},{5,9},{13,17},{21,25},... | collective-permute-start | bytes 6291464 | tf_op jit(solution)/shard_map/ppermute | solution.py:278
  148.3 11.2 %collective-permute-done.2.refs_3_ = bf16[3,2,512,128]{3,2,1,0:T(8,128)(2,1)} collective-permute-done((bf16[3,2,512,128]{3,2,1,0:T(8,128)(2,1)}, bf16[3,2,512,128]{3,2,1,0:T(8,128)(2,1)}, u32[]{:S(2)}, u32[]{:S(2)}) %collective-permute-start.2) | collective-permute-done | bytes 786464 | tf_op jit(solution)/shard_map/ppermute | solution.py:272
  159.6 3.8 join.7.refs_12_.refs_5_
  163.4 6.2 %collective-permute-start.10 = (bf16[2,2,2048,128]{3,2,1,0:T(8,128)(2,1)}, bf16[2,2,2048,128]{3,2,1,0:T(8,128)(2,1)}, u32[]{:S(2)}, u32[]{:S(2)}) collective-permute-start(bf16[2,2,2048,128]{3,2,1,0:T(8,128)(2,1)} %join.7.refs_12_.refs_5_), channel_id=1, source_target_pairs={{4,8},{12,16},{20,24},{8,4},{16,12},{24,20},{5,9},{13,17},{21,25},... | collective-permute-start | bytes 6291464 | tf_op jit(solution)/shard_map/ppermute | solution.py:278
  169.8 5.7 collective-permute-done.14.refs_2_
  180.6 28.9 %collective-permute-done.15.refs_3_ = bf16[3,2,512,128]{3,2,1,0:T(8,128)(2,1)} collective-permute-done((bf16[3,2,512,128]{3,2,1,0:T(8,128)(2,1)}, bf16[3,2,512,128]{3,2,1,0:T(8,128)(2,1)}, u32[]{:S(2)}, u32[]{:S(2)}) %collective-permute-start.15) | collective-permute-done | bytes 786464 | tf_op jit(solution)/shard_map/ppermute | solution.py:272
  215.6 28.8 %attend.6 = (bf16[8,512,128]{2,1,0:T(8,128)(2,1)}, bf16[8,512,128]{2,1,0:T(8,128)(2,1)}, bf16[8,512,128]{2,1,0:T(8,128)(2,1)}, bf16[8,512,128]{2,1,0:T(8,128)(2,1)}) custom-call(s32[572]{0:T(1024)} %reshape.160.unit_ref, s32[1]{0:T(128)} %bitcast.5.count_ref, bf16[128,128]{1,0:T(8,128)(2,1)} %select_convert_fusion.signs_ref, ...), custom_call_target="tpu_custom_call" | custom-call | bytes 1048576 | tf_op jit(solution)/shard_map/attend/pallas_call | solution.py:242
  244.4 3.8 join.8.refs_12_.refs_5_
  248.2 3.7 pack.10
  253.3 5.8 collective-permute-start.18
  261.0 28.8 %attend.7 = (bf16[8,512,128]{2,1,0:T(8,128)(2,1)}, bf16[8,512,128]{2,1,0:T(8,128)(2,1)}, bf16[8,512,128]{2,1,0:T(8,128)(2,1)}, bf16[8,512,128]{2,1,0:T(8,128)(2,1)}) custom-call(s32[572]{0:T(1024)} %reshape.160.unit_ref, s32[1]{0:T(128)} %bitcast.5.count_ref, ...), custom_call_target="tpu_custom_call", output_to_operand_aliasing={{0}: (10, {}), {1}: (11, {}), {2}: (12, {}), {3}: (13, {})} | custom-call | bytes 1048576 | tf_op jit(solution)/shard_map/attend/pallas_call | solution.py:242
  289.9 3.9 join.9.refs_12_.refs_5_
  299.8 34.2 %collective-permute-done.21.refs_2_ = bf16[3,2,512,128]{3,2,1,0:T(8,128)(2,1)} collective-permute-done((bf16[3,2,512,128]{3,2,1,0:T(8,128)(2,1)S(1)}, bf16[3,2,512,128]{3,2,1,0:T(8,128)(2,1)}, u32[]{:S(2)}, u32[]{:S(2)}) %collective-permute-start.21) | collective-permute-done | bytes 786464 | tf_op jit(solution)/shard_map/ppermute | solution.py:272
  338.5 31.1 %collective-permute-done.22.refs_3_ = bf16[3,2,512,128]{3,2,1,0:T(8,128)(2,1)S(1)} collective-permute-done((bf16[3,2,512,128]{3,2,1,0:T(8,128)(2,1)S(1)}, bf16[3,2,512,128]{3,2,1,0:T(8,128)(2,1)S(1)}, u32[]{:S(2)}, u32[]{:S(2)}) %collective-permute-start.22) | collective-permute-done | bytes 786464 | tf_op jit(solution)/shard_map/ppermute | solution.py:272
  372.2 28.8 %attend.8 = (bf16[8,512,128]{2,1,0:T(8,128)(2,1)}, bf16[8,512,128]{2,1,0:T(8,128)(2,1)}, bf16[8,512,128]{2,1,0:T(8,128)(2,1)}, bf16[8,512,128]{2,1,0:T(8,128)(2,1)}) custom-call(s32[572]{0:T(1024)} %reshape.160.unit_ref, s32[1]{0:T(128)} %bitcast.5.count_ref, ...), custom_call_target="tpu_custom_call", output_to_operand_aliasing={{0}: (10, {}), {1}: (11, {}), {2}: (12, {}), {3}: (13, {})} | custom-call | bytes 1048576 | tf_op jit(solution)/shard_map/attend/pallas_call | solution.py:242
  401.0 3.8 join.10.refs_11_.refs_5_
  404.8 4.2 collective-permute-start.31
  411.0 28.9 %attend.9 = (bf16[8,512,128]{2,1,0:T(8,128)(2,1)}, bf16[8,512,128]{2,1,0:T(8,128)(2,1)}, bf16[8,512,128]{2,1,0:T(8,128)(2,1)}, bf16[8,512,128]{2,1,0:T(8,128)(2,1)}) custom-call(s32[572]{0:T(1024)} %reshape.160.unit_ref, s32[1]{0:T(128)} %bitcast.5.count_ref, ...), custom_call_target="tpu_custom_call", output_to_operand_aliasing={{0}: (10, {}), {1}: (11, {}), {2}: (12, {}), {3}: (13, {})} | custom-call | bytes 1048576 | tf_op jit(solution)/shard_map/attend/pallas_call | solution.py:242
  441.7 4.0 join.11.refs_7_.refs_5_
  452.8 7.4 %collective-permute-done.32.refs_6_ = bf16[2,2,2048,128]{3,2,1,0:T(8,128)(2,1)} collective-permute-done((bf16[2,2,2048,128]{3,2,1,0:T(8,128)(2,1)}, bf16[2,2,2048,128]{3,2,1,0:T(8,128)(2,1)}, u32[]{:S(2)}, u32[]{:S(2)}) %collective-permute-start.32) | collective-permute-done | bytes 2097184 | tf_op jit(solution)/shard_map/ppermute | solution.py:278
  461.0 28.8 %attend.10 = (bf16[4,512,128]{2,1,0:T(8,128)(2,1)}, bf16[4,512,128]{2,1,0:T(8,128)(2,1)}, bf16[4,512,128]{2,1,0:T(8,128)(2,1)}, bf16[4,512,128]{2,1,0:T(8,128)(2,1)}) custom-call(s32[572]{0:T(1024)} %reshape.160.unit_ref, s32[1]{0:T(128)} %bitcast.5.count_ref, bf16[128,128]{1,0:T(8,128)(2,1)} %select_convert_fusion.signs_ref, ...), custom_call_target="tpu_custom_call" | custom-call | bytes 1048576 | tf_op jit(solution)/shard_map/attend/pallas_call | solution.py:242
  491.7 11.7 %collective-permute-done.30.refs_6_ = bf16[2,2,2048,128]{3,2,1,0:T(8,128)(2,1)} collective-permute-done((bf16[2,2,2048,128]{3,2,1,0:T(8,128)(2,1)}, bf16[2,2,2048,128]{3,2,1,0:T(8,128)(2,1)}, u32[]{:S(2)}, u32[]{:S(2)}) %collective-permute-start.30) | collective-permute-done | bytes 2097184 | tf_op jit(solution)/shard_map/ppermute | solution.py:278
  503.4 28.8 %attend.11 = (bf16[4,512,128]{2,1,0:T(8,128)(2,1)}, bf16[4,512,128]{2,1,0:T(8,128)(2,1)}, bf16[4,512,128]{2,1,0:T(8,128)(2,1)}, bf16[4,512,128]{2,1,0:T(8,128)(2,1)}) custom-call(s32[572]{0:T(1024)} %reshape.160.unit_ref, s32[1]{0:T(128)} %bitcast.5.count_ref, ...), custom_call_target="tpu_custom_call", output_to_operand_aliasing={{0}: (10, {}), {1}: (11, {}), {2}: (12, {}), {3}: (13, {})} | custom-call | bytes 1048576 | tf_op jit(solution)/shard_map/attend/pallas_call | solution.py:242
  535.3 9.2 %collective-permute-done.25.refs_3_ = bf16[8,512,128]{2,1,0:T(8,128)(2,1)} collective-permute-done((bf16[8,512,128]{2,1,0:T(8,128)(2,1)S(1)}, bf16[8,512,128]{2,1,0:T(8,128)(2,1)}, u32[]{:S(2)}, u32[]{:S(2)}) %collective-permute-start.25) | collective-permute-done | bytes 1048608 | tf_op jit(solution)/shard_map/ppermute | solution.py:272
  547.8 29.2 %collective-permute-done.34.refs_6_ = bf16[4,512,128]{2,1,0:T(8,128)(2,1)} collective-permute-done((bf16[4,512,128]{2,1,0:T(8,128)(2,1)}, bf16[4,512,128]{2,1,0:T(8,128)(2,1)}, u32[]{:S(2)}, u32[]{:S(2)}) %collective-permute-start.34) | collective-permute-done | bytes 524320 | tf_op jit(solution)/shard_map/ppermute | solution.py:272
  576.9 12.5 %collective-permute-done.35.refs_7_ = bf16[4,512,128]{2,1,0:T(8,128)(2,1)S(1)} collective-permute-done((bf16[4,512,128]{2,1,0:T(8,128)(2,1)}, bf16[4,512,128]{2,1,0:T(8,128)(2,1)S(1)}, u32[]{:S(2)}, u32[]{:S(2)}) %collective-permute-start.35) | collective-permute-done | bytes 524320 | tf_op jit(solution)/shard_map/ppermute | solution.py:272
  590.2 6.3 %collect.1 = bf16[512,6144]{1,0:T(8,128)(2,1)} custom-call(s32[1]{0:T(128)} %bitcast.z_ref, bf16[8,512,128]{2,1,0:T(8,128)(2,1)} %get-tuple-element.86.refs_4_.refs_0_, bf16[8,512,128]{2,1,0:T(8,128)(2,1)} %collective-permute-done.23.refs_1_, bf16[8,512,128]{2,1,0:T(8,128)(2,1)} %collective-permute-done.24.refs_2_, ...), custom_call_target="tpu_custom_call" | custom-call | bytes 1048576 | tf_op jit(solution)/shard_map/collect/pallas_call | solution.py:113
  (125 shorter events, 75.0 us)
Async XLA Ops:
  5.1 36.4 %collective-permute-start.4 = (bf16[3,2,512,128]{3,2,1,0:T(8,128)(2,1)}, bf16[3,2,512,128]{3,2,1,0:T(8,128)(2,1)S(1)}, u32[]{:S(2)}, u32[]{:S(2)}) collective-permute-start(bf16[3,2,512,128]{3,2,1,0:T(8,128)(2,1)} %get-tuple-element.59), channel_id=1, source_target_pairs={{0,2},{1,3},{2,0},{3,1},{4,6},{5,7},{6,4},{7,5},{8,10},{9,11},{10,... | collective-permute-start | bytes 2359304 | tf_op jit(solution)/shard_map/ppermute | solution.py:272
  7.4 67.8 %collective-permute-start.5 = (bf16[3,2,512,128]{3,2,1,0:T(8,128)(2,1)}, bf16[3,2,512,128]{3,2,1,0:T(8,128)(2,1)S(1)}, u32[]{:S(2)}, u32[]{:S(2)}) collective-permute-start(bf16[3,2,512,128]{3,2,1,0:T(8,128)(2,1)} %get-tuple-element.60), channel_id=1, source_target_pairs={{0,3},{1,2},{2,1},{3,0},{4,7},{5,6},{6,5},{7,4},{8,11},{9,10},{10,... | collective-permute-start | bytes 2359304 | tf_op jit(solution)/shard_map/ppermute | solution.py:272
  11.2 76.0 %collective-permute-start = (bf16[3,2,512,128]{3,2,1,0:T(8,128)(2,1)}, bf16[3,2,512,128]{3,2,1,0:T(8,128)(2,1)}, u32[]{:S(2)}, u32[]{:S(2)}) collective-permute-start(bf16[3,2,512,128]{3,2,1,0:T(8,128)(2,1)} %get-tuple-element.55), channel_id=1, source_target_pairs={{0,1},{1,0},{2,3},{3,2},{4,5},{5,4},{6,7},{7,6},{8,9},{9,8},{10,11... | collective-permute-start | bytes 2359304 | tf_op jit(solution)/shard_map/ppermute | solution.py:272
  12.4 121.0 %collective-permute-start.1 = (bf16[3,2,512,128]{3,2,1,0:T(8,128)(2,1)}, bf16[3,2,512,128]{3,2,1,0:T(8,128)(2,1)}, u32[]{:S(2)}, u32[]{:S(2)}) collective-permute-start(bf16[3,2,512,128]{3,2,1,0:T(8,128)(2,1)} %get-tuple-element.56), channel_id=1, source_target_pairs={{0,2},{1,3},{2,0},{3,1},{4,6},{5,7},{6,4},{7,5},{8,10},{9,11},{10,... | collective-permute-start | bytes 2359304 | tf_op jit(solution)/shard_map/ppermute | solution.py:272
  37.7 121.8 %collective-permute-start.2 = (bf16[3,2,512,128]{3,2,1,0:T(8,128)(2,1)}, bf16[3,2,512,128]{3,2,1,0:T(8,128)(2,1)}, u32[]{:S(2)}, u32[]{:S(2)}) collective-permute-start(bf16[3,2,512,128]{3,2,1,0:T(8,128)(2,1)} %get-tuple-element.57), channel_id=1, source_target_pairs={{0,3},{1,2},{2,1},{3,0},{4,7},{5,6},{6,5},{7,4},{8,11},{9,10},{10,... | collective-permute-start | bytes 2359304 | tf_op jit(solution)/shard_map/ppermute | solution.py:272
  83.6 86.0 %collective-permute-start.13 = (bf16[3,2,512,128]{3,2,1,0:T(8,128)(2,1)}, bf16[3,2,512,128]{3,2,1,0:T(8,128)(2,1)S(1)}, u32[]{:S(2)}, u32[]{:S(2)}) collective-permute-start(bf16[3,2,512,128]{3,2,1,0:T(8,128)(2,1)} %get-tuple-element.70), channel_id=1, source_target_pairs={{0,1},{1,0},{2,3},{3,2},{4,5},{5,4},{6,7},{7,6},{8,9},{9,8},{10,11... | collective-permute-start | bytes 2359304 | tf_op jit(solution)/shard_map/ppermute | solution.py:272
  83.7 91.8 %collective-permute-start.14 = (bf16[3,2,512,128]{3,2,1,0:T(8,128)(2,1)}, bf16[3,2,512,128]{3,2,1,0:T(8,128)(2,1)}, u32[]{:S(2)}, u32[]{:S(2)}) collective-permute-start(bf16[3,2,512,128]{3,2,1,0:T(8,128)(2,1)} %get-tuple-element.71), channel_id=1, source_target_pairs={{0,2},{1,3},{2,0},{3,1},{4,6},{5,7},{6,4},{7,5},{8,10},{9,11},{10,... | collective-permute-start | bytes 2359304 | tf_op jit(solution)/shard_map/ppermute | solution.py:272
  87.2 122.5 %collective-permute-start.11 = (bf16[2,2,2048,128]{3,2,1,0:T(8,128)(2,1)S(1)}, bf16[2,2,2048,128]{3,2,1,0:T(8,128)(2,1)}, u32[]{:S(2)}, u32[]{:S(2)}) collective-permute-start(bf16[2,2,2048,128]{3,2,1,0:T(8,128)(2,1)S(1)} %copy-done), channel_id=1, source_target_pairs={{0,4},{8,12},{16,20},{24,28},{4,0},{12,8},{20,16},{28,24},{1,5},{9... | collective-permute-start | bytes 6291464 | tf_op jit(solution)/shard_map/ppermute | solution.py:278
  133.4 79.0 %collective-permute-start.12 = (bf16[2,2,2048,128]{3,2,1,0:T(8,128)(2,1)S(1)}, bf16[2,2,2048,128]{3,2,1,0:T(8,128)(2,1)}, u32[]{:S(2)}, u32[]{:S(2)}) collective-permute-start(bf16[2,2,2048,128]{3,2,1,0:T(8,128)(2,1)S(1)} %copy-done), channel_id=1, source_target_pairs={{4,8},{12,16},{20,24},{8,4},{16,12},{24,20},{5,9},{13,17},{21,25},... | collective-permute-start | bytes 6291464 | tf_op jit(solution)/shard_map/ppermute | solution.py:278
  163.4 89.9 %collective-permute-start.10 = (bf16[2,2,2048,128]{3,2,1,0:T(8,128)(2,1)}, bf16[2,2,2048,128]{3,2,1,0:T(8,128)(2,1)}, u32[]{:S(2)}, u32[]{:S(2)}) collective-permute-start(bf16[2,2,2048,128]{3,2,1,0:T(8,128)(2,1)} %join.7.refs_12_.refs_5_), channel_id=1, source_target_pairs={{4,8},{12,16},{20,24},{8,4},{16,12},{24,20},{5,9},{13,17},{21,25},... | collective-permute-start | bytes 6291464 | tf_op jit(solution)/shard_map/ppermute | solution.py:278
  169.7 89.4 %collective-permute-start.9 = (bf16[2,2,2048,128]{3,2,1,0:T(8,128)(2,1)}, bf16[2,2,2048,128]{3,2,1,0:T(8,128)(2,1)}, u32[]{:S(2)}, u32[]{:S(2)}) collective-permute-start(bf16[2,2,2048,128]{3,2,1,0:T(8,128)(2,1)} %join.7.refs_12_.refs_5_), channel_id=1, source_target_pairs={{0,4},{8,12},{16,20},{24,28},{4,0},{12,8},{20,16},{28,24},{1,5},{9... | collective-permute-start | bytes 6291464 | tf_op jit(solution)/shard_map/ppermute | solution.py:278
  209.6 42.4 %collective-permute-start.6 = (bf16[3,2,512,128]{3,2,1,0:T(8,128)(2,1)}, bf16[3,2,512,128]{3,2,1,0:T(8,128)(2,1)S(1)}, u32[]{:S(2)}, u32[]{:S(2)}) collective-permute-start(bf16[3,2,512,128]{3,2,1,0:T(8,128)(2,1)} %get-tuple-element.63), channel_id=1, source_target_pairs={{0,1},{1,0},{2,3},{3,2},{4,5},{5,4},{6,7},{7,6},{8,9},{9,8},{10,11... | collective-permute-start | bytes 2359304 | tf_op jit(solution)/shard_map/ppermute | solution.py:272
  209.7 80.1 %collective-permute-start.7 = (bf16[3,2,512,128]{3,2,1,0:T(8,128)(2,1)}, bf16[3,2,512,128]{3,2,1,0:T(8,128)(2,1)}, u32[]{:S(2)}, u32[]{:S(2)}) collective-permute-start(bf16[3,2,512,128]{3,2,1,0:T(8,128)(2,1)} %get-tuple-element.64), channel_id=1, source_target_pairs={{0,2},{1,3},{2,0},{3,1},{4,6},{5,7},{6,4},{7,5},{8,10},{9,11},{10,... | collective-permute-start | bytes 2359304 | tf_op jit(solution)/shard_map/ppermute | solution.py:272
  212.4 77.4 %collective-permute-start.8 = (bf16[3,2,512,128]{3,2,1,0:T(8,128)(2,1)}, bf16[3,2,512,128]{3,2,1,0:T(8,128)(2,1)}, u32[]{:S(2)}, u32[]{:S(2)}) collective-permute-start(bf16[3,2,512,128]{3,2,1,0:T(8,128)(2,1)} %get-tuple-element.65), channel_id=1, source_target_pairs={{0,3},{1,2},{2,1},{3,0},{4,7},{5,6},{6,5},{7,4},{8,11},{9,10},{10,... | collective-permute-start | bytes 2359304 | tf_op jit(solution)/shard_map/ppermute | solution.py:272
  252.0 46.5 %collective-permute-start.20 = (bf16[3,2,512,128]{3,2,1,0:T(8,128)(2,1)}, bf16[3,2,512,128]{3,2,1,0:T(8,128)(2,1)}, u32[]{:S(2)}, u32[]{:S(2)}) collective-permute-start(bf16[3,2,512,128]{3,2,1,0:T(8,128)(2,1)} %get-tuple-element.83), channel_id=1, source_target_pairs={{0,1},{1,0},{2,3},{3,2},{4,5},{5,4},{6,7},{7,6},{8,9},{9,8},{10,11... | collective-permute-start | bytes 2359304 | tf_op jit(solution)/shard_map/ppermute | solution.py:272
  253.3 116.3 %collective-permute-start.18 = (bf16[2,2,2048,128]{3,2,1,0:T(8,128)(2,1)S(1)}, bf16[2,2,2048,128]{3,2,1,0:T(8,128)(2,1)}, u32[]{:S(2)}, u32[]{:S(2)}) collective-permute-start(bf16[2,2,2048,128]{3,2,1,0:T(8,128)(2,1)S(1)} %copy-done.1), channel_id=1, source_target_pairs={{0,4},{8,12},{16,20},{24,28},{4,0},{12,8},{20,16},{28,24},{1,5},{9... | collective-permute-start | bytes 6291464 | tf_op jit(solution)/shard_map/ppermute | solution.py:278
  259.1 112.5 %collective-permute-start.19 = (bf16[2,2,2048,128]{3,2,1,0:T(8,128)(2,1)S(1)}, bf16[2,2,2048,128]{3,2,1,0:T(8,128)(2,1)}, u32[]{:S(2)}, u32[]{:S(2)}) collective-permute-start(bf16[2,2,2048,128]{3,2,1,0:T(8,128)(2,1)S(1)} %copy-done.1), channel_id=1, source_target_pairs={{4,8},{12,16},{20,24},{8,4},{16,12},{24,20},{5,9},{13,17},{21,25},... | collective-permute-start | bytes 6291464 | tf_op jit(solution)/shard_map/ppermute | solution.py:278
  293.8 111.0 %collective-permute-start.16 = (bf16[2,2,2048,128]{3,2,1,0:T(8,128)(2,1)}, bf16[2,2,2048,128]{3,2,1,0:T(8,128)(2,1)}, u32[]{:S(2)}, u32[]{:S(2)}) collective-permute-start(bf16[2,2,2048,128]{3,2,1,0:T(8,128)(2,1)} %join.9.refs_12_.refs_5_), channel_id=1, source_target_pairs={{0,4},{8,12},{16,20},{24,28},{4,0},{12,8},{20,16},{28,24},{1,5},{9... | collective-permute-start | bytes 6291464 | tf_op jit(solution)/shard_map/ppermute | solution.py:278
  296.0 113.1 %collective-permute-start.17 = (bf16[2,2,2048,128]{3,2,1,0:T(8,128)(2,1)}, bf16[2,2,2048,128]{3,2,1,0:T(8,128)(2,1)}, u32[]{:S(2)}, u32[]{:S(2)}) collective-permute-start(bf16[2,2,2048,128]{3,2,1,0:T(8,128)(2,1)} %join.9.refs_12_.refs_5_), channel_id=1, source_target_pairs={{4,8},{12,16},{20,24},{8,4},{16,12},{24,20},{5,9},{13,17},{21,25},... | collective-permute-start | bytes 6291464 | tf_op jit(solution)/shard_map/ppermute | solution.py:278
  334.0 35.5 %collective-permute-start.22 = (bf16[3,2,512,128]{3,2,1,0:T(8,128)(2,1)S(1)}, bf16[3,2,512,128]{3,2,1,0:T(8,128)(2,1)S(1)}, u32[]{:S(2)}, u32[]{:S(2)}) collective-permute-start(bf16[3,2,512,128]{3,2,1,0:T(8,128)(2,1)S(1)} %copy-done.17), channel_id=1, source_target_pairs={{0,3},{1,2},{2,1},{3,0},{4,7},{5,6},{6,5},{7,4},{8,11},{9,10},{10,... | collective-permute-start | bytes 2359304 | tf_op jit(solution)/shard_map/ppermute | solution.py:272
  369.5 70.3 %collective-permute-start.26 = (bf16[3,2,512,128]{3,2,1,0:T(8,128)(2,1)}, bf16[3,2,512,128]{3,2,1,0:T(8,128)(2,1)S(1)}, u32[]{:S(2)}, u32[]{:S(2)}) collective-permute-start(bf16[3,2,512,128]{3,2,1,0:T(8,128)(2,1)} %get-tuple-element.90), channel_id=1, source_target_pairs={{0,1},{1,0},{2,3},{3,2},{4,5},{5,4},{6,7},{7,6},{8,9},{9,8},{10,11... | collective-permute-start | bytes 2359304 | tf_op jit(solution)/shard_map/ppermute | solution.py:272
  370.4 69.4 %collective-permute-start.27 = (bf16[3,2,512,128]{3,2,1,0:T(8,128)(2,1)}, bf16[3,2,512,128]{3,2,1,0:T(8,128)(2,1)S(1)}, u32[]{:S(2)}, u32[]{:S(2)}) collective-permute-start(bf16[3,2,512,128]{3,2,1,0:T(8,128)(2,1)} %get-tuple-element.91), channel_id=1, source_target_pairs={{0,2},{1,3},{2,0},{3,1},{4,6},{5,7},{6,4},{7,5},{8,10},{9,11},{10,... | collective-permute-start | bytes 2359304 | tf_op jit(solution)/shard_map/ppermute | solution.py:272
  371.6 68.3 %collective-permute-start.28 = (bf16[3,2,512,128]{3,2,1,0:T(8,128)(2,1)}, bf16[3,2,512,128]{3,2,1,0:T(8,128)(2,1)S(1)}, u32[]{:S(2)}, u32[]{:S(2)}) collective-permute-start(bf16[3,2,512,128]{3,2,1,0:T(8,128)(2,1)} %get-tuple-element.92), channel_id=1, source_target_pairs={{0,3},{1,2},{2,1},{3,0},{4,7},{5,6},{6,5},{7,4},{8,11},{9,10},{10,... | collective-permute-start | bytes 2359304 | tf_op jit(solution)/shard_map/ppermute | solution.py:272
  404.8 47.3 %collective-permute-start.31 = (bf16[2,2,2048,128]{3,2,1,0:T(8,128)(2,1)}, bf16[2,2,2048,128]{3,2,1,0:T(8,128)(2,1)}, u32[]{:S(2)}, u32[]{:S(2)}) collective-permute-start(bf16[2,2,2048,128]{3,2,1,0:T(8,128)(2,1)} %join.10.refs_11_.refs_5_), channel_id=1, source_target_pairs={{0,4},{8,12},{16,20},{24,28},{4,0},{12,8},{20,16},{28,24},{1,5},{9... | collective-permute-start | bytes 6291464 | tf_op jit(solution)/shard_map/ppermute | solution.py:278
  409.1 51.1 %collective-permute-start.32 = (bf16[2,2,2048,128]{3,2,1,0:T(8,128)(2,1)}, bf16[2,2,2048,128]{3,2,1,0:T(8,128)(2,1)}, u32[]{:S(2)}, u32[]{:S(2)}) collective-permute-start(bf16[2,2,2048,128]{3,2,1,0:T(8,128)(2,1)} %join.10.refs_11_.refs_5_), channel_id=1, source_target_pairs={{4,8},{12,16},{20,24},{8,4},{16,12},{24,20},{5,9},{13,17},{21,25},... | collective-permute-start | bytes 6291464 | tf_op jit(solution)/shard_map/ppermute | solution.py:278
  445.7 46.0 %collective-permute-start.29 = (bf16[2,2,2048,128]{3,2,1,0:T(8,128)(2,1)}, bf16[2,2,2048,128]{3,2,1,0:T(8,128)(2,1)}, u32[]{:S(2)}, u32[]{:S(2)}) collective-permute-start(bf16[2,2,2048,128]{3,2,1,0:T(8,128)(2,1)} %join.11.refs_7_.refs_5_), channel_id=1, source_target_pairs={{0,4},{8,12},{16,20},{24,28},{4,0},{12,8},{20,16},{28,24},{1,5},{9... | collective-permute-start | bytes 6291464 | tf_op jit(solution)/shard_map/ppermute | solution.py:278
  447.9 55.5 %collective-permute-start.30 = (bf16[2,2,2048,128]{3,2,1,0:T(8,128)(2,1)}, bf16[2,2,2048,128]{3,2,1,0:T(8,128)(2,1)}, u32[]{:S(2)}, u32[]{:S(2)}) collective-permute-start(bf16[2,2,2048,128]{3,2,1,0:T(8,128)(2,1)} %join.11.refs_7_.refs_5_), channel_id=1, source_target_pairs={{4,8},{12,16},{20,24},{8,4},{16,12},{24,20},{5,9},{13,17},{21,25},... | collective-permute-start | bytes 6291464 | tf_op jit(solution)/shard_map/ppermute | solution.py:278
  450.5 84.2 %collective-permute-start.23 = (bf16[8,512,128]{2,1,0:T(8,128)(2,1)S(1)}, bf16[8,512,128]{2,1,0:T(8,128)(2,1)}, u32[]{:S(2)}, u32[]{:S(2)}) collective-permute-start(bf16[8,512,128]{2,1,0:T(8,128)(2,1)S(1)} %copy-done.2), channel_id=1, source_target_pairs={{0,1},{1,0},{2,3},{3,2},{4,5},{5,4},{6,7},{7,6},{8,9},{9,8},{10,11... | collective-permute-start | bytes 3145736 | tf_op jit(solution)/shard_map/ppermute | solution.py:272
  452.1 83.2 %collective-permute-start.24 = (bf16[8,512,128]{2,1,0:T(8,128)(2,1)S(1)}, bf16[8,512,128]{2,1,0:T(8,128)(2,1)}, u32[]{:S(2)}, u32[]{:S(2)}) collective-permute-start(bf16[8,512,128]{2,1,0:T(8,128)(2,1)S(1)} %copy-done.3), channel_id=1, source_target_pairs={{0,2},{1,3},{2,0},{3,1},{4,6},{5,7},{6,4},{7,5},{8,10},{9,11},{10,... | collective-permute-start | bytes 3145736 | tf_op jit(solution)/shard_map/ppermute | solution.py:272
  460.2 84.4 %collective-permute-start.25 = (bf16[8,512,128]{2,1,0:T(8,128)(2,1)S(1)}, bf16[8,512,128]{2,1,0:T(8,128)(2,1)}, u32[]{:S(2)}, u32[]{:S(2)}) collective-permute-start(bf16[8,512,128]{2,1,0:T(8,128)(2,1)S(1)} %copy-done.4), channel_id=1, source_target_pairs={{0,3},{1,2},{2,1},{3,0},{4,7},{5,6},{6,5},{7,4},{8,11},{9,10},{10,... | collective-permute-start | bytes 3145736 | tf_op jit(solution)/shard_map/ppermute | solution.py:272
  534.1 42.9 %collective-permute-start.34 = (bf16[4,512,128]{2,1,0:T(8,128)(2,1)}, bf16[4,512,128]{2,1,0:T(8,128)(2,1)}, u32[]{:S(2)}, u32[]{:S(2)}) collective-permute-start(bf16[4,512,128]{2,1,0:T(8,128)(2,1)} %get-tuple-element.99), channel_id=1, source_target_pairs={{0,2},{1,3},{2,0},{3,1},{4,6},{5,7},{6,4},{7,5},{8,10},{9,11},{10,... | collective-permute-start | bytes 1572872 | tf_op jit(solution)/shard_map/ppermute | solution.py:272
  534.7 54.7 %collective-permute-start.35 = (bf16[4,512,128]{2,1,0:T(8,128)(2,1)}, bf16[4,512,128]{2,1,0:T(8,128)(2,1)S(1)}, u32[]{:S(2)}, u32[]{:S(2)}) collective-permute-start(bf16[4,512,128]{2,1,0:T(8,128)(2,1)} %get-tuple-element.100), channel_id=1, source_target_pairs={{0,3},{1,2},{2,1},{3,0},{4,7},{5,6},{6,5},{7,4},{8,11},{9,10},{10,... | collective-permute-start | bytes 1572872 | tf_op jit(solution)/shard_map/ppermute | solution.py:272
  (24 other events, 492.3 us)

commit v3 on v2

--- a/solution.py
+++ b/solution.py
@@ -11,8 +11,8 @@
 ANYWHERE = pl.BlockSpec(memory_space=pl.ANY)
 GROUP = 9
 VMEM = 60 << 20
-SIZES = (2, 2, 2, 2, 2, 2)
-BACK = (4, 2)
+STEPS = 6
+BACK = (2, 3, 1)
 AHEAD = 2
 
 
@@ -26,10 +26,9 @@
 
 
 def cut(local_heads):
-    if local_heads % 12 == 0:
-        unit = local_heads // 12
-        return [unit * size for size in SIZES], BACK
-    return [1] * local_heads, [local_heads - 2, 2] if local_heads > 2 else [local_heads]
+    if local_heads % STEPS == 0:
+        return [local_heads // STEPS] * STEPS, BACK
+    return [1] * local_heads, [1] * local_heads
 
 
 def params():
@@ -132,7 +131,7 @@
     frame_tiles, slot_total = window.shape
     groups = window_count // group
     ends = jnp.cumsum(groups)
-    unit = jnp.arange(frame_tiles * (slot_total // group) + 4, dtype=jnp.int32)
+    unit = jnp.arange(frame_tiles * (slot_total // group) + 16, dtype=jnp.int32)
     owner = jnp.sum(unit[:, None] >= ends[None, :], axis=1).astype(jnp.int32)
     order = jnp.minimum(unit - (ends - groups)[jnp.minimum(owner, frame_tiles - 1)], slot_total // group - 1)
 
@@ -158,7 +157,7 @@
     frame_tiles = frame_rows // tile
     span = group * tile
     stride = group + 2
-    lag, ring = 3, 4
+    lag, ring, batch = 6, 8, 4
     to_log2 = LOG2E / math.sqrt(width)
     post = 1.0 / math.sqrt(width)
 
@@ -204,8 +203,9 @@
             total = expo[:, :tile]
             for s in range(1, group):
                 total = total + expo[:, s * tile : (s + 1) * tile]
-            total_all[t] += total
-            sum_all[t] += lax.dot_general(
+            place = pl.ds(pl.multiple_of(t * tile, tile), tile)
+            total_all[place, :] += total
+            sum_all[place, :] += lax.dot_general(
                 expo.astype(jnp.bfloat16),
                 tiles_of(values, u),
                 (((1,), (0,)), ((), ())),
@@ -215,28 +215,36 @@
         for u in range(lag):
             score(u, u)
 
-        def four_units(i, carry):
-            for j in range(ring):
-                u = i * ring + j
-                top = jnp.max(tops[unit_ref[u * stride]], axis=1, keepdims=True) * to_log2
-                score(u + lag, (j + lag) % ring)
-                weigh(u, j, top)
+        def one_batch(u, slot):
+            most = [
+                jnp.max(tops[unit_ref[(u + j) * stride]], axis=1, keepdims=True) * to_log2 for j in range(batch)
+            ]
+            for j in range(batch):
+                score(u + j + lag, (slot + j + lag) % ring)
+                weigh(u + j, slot + j, most[j])
+
+        def two_batches(i, carry):
+            one_batch(i * ring, 0)
+
+            @pl.when(i * ring + batch < count)
+            def _():
+                one_batch(i * ring + batch, batch)
+
             return carry
 
-        lax.fori_loop(0, (count + ring - 1) // ring, four_units, 0)
+        lax.fori_loop(0, (count + ring - 1) // ring, two_batches, 0)
         for k in range(ulysses):
-            for i in range(rows // tile):
-                t = k * (rows // tile) + i
-                rotated = sum_all[t] * (post / jnp.sum(total_all[t], axis=1, keepdims=True))
-                high = rotated.astype(jnp.bfloat16)
-                rest = rotated - high.astype(jnp.float32)
-                middle = rest.astype(jnp.bfloat16)
-                low = (rest - middle.astype(jnp.float32)).astype(jnp.bfloat16)
-                signs_val = signs_ref[...]
-                result = jnp.dot(low, signs_val, preferred_element_type=jnp.float32)
-                result += jnp.dot(middle, signs_val, preferred_element_type=jnp.float32)
-                result += jnp.dot(high, signs_val, preferred_element_type=jnp.float32)
-                outs[k][pl.ds(i * tile, tile), :] = result.astype(jnp.bfloat16)
+            part = pl.ds(k * rows, rows)
+            rotated = sum_all[part, :] * (post / jnp.sum(total_all[part, :], axis=1, keepdims=True))
+            high = rotated.astype(jnp.bfloat16)
+            rest = rotated - high.astype(jnp.float32)
+            middle = rest.astype(jnp.bfloat16)
+            low = (rest - middle.astype(jnp.float32)).astype(jnp.bfloat16)
+            signs_val = signs_ref[...]
+            result = jnp.dot(low, signs_val, preferred_element_type=jnp.float32)
+            result += jnp.dot(middle, signs_val, preferred_element_type=jnp.float32)
+            result += jnp.dot(high, signs_val, preferred_element_type=jnp.float32)
+            outs[k][...] = result.astype(jnp.bfloat16)
 
     frame_spec = pl.BlockSpec((None, 2, frame_rows, width), lambda h, *_: (h, 0, 0, 0))
     return pl.pallas_call(
@@ -254,8 +262,8 @@
                 pltpu.VMEM((3 * frame_rows, width), jnp.bfloat16),
                 pltpu.VMEM((frame_rows + tile, width), jnp.bfloat16),
                 pltpu.VMEM((frame_tiles + 1, tile, tile), jnp.float32),
-                pltpu.VMEM((frame_tiles + 1, tile, tile), jnp.float32),
-                pltpu.VMEM((frame_tiles + 1, tile, width), jnp.float32),
+                pltpu.VMEM((frame_rows + tile, tile), jnp.float32),
+                pltpu.VMEM((frame_rows + tile, width), jnp.float32),
             ]
             + [pltpu.VMEM((tile, span), jnp.float32)] * ring,
         ),

time: 597 us -> 575 us (0.963)
  waiting for transfers between devices: 253 us -> 229 us
    ppermute x24 -> x27, waiting for transfers between devices: 234 us -> 212 us  [across(): return lax.ppermute(block, 'uly', [(i, i ^ step) for i in range(size)])]
    ppermute x24 -> x27, starting transfers between devices: 25.7 us -> 30.3 us  [across(): return lax.ppermute(block, 'uly', [(i, i ^ step) for i in range(size)])]
  transfers between devices with their start and end apart: 36 -> 39, of which waited for: 15 -> 13; matrix products, arithmetic and copies ran while one was open for 1% -> 1% of each run, Pallas kernels for 36% -> 37%
where the time goes in v3:
time: 575 us; the launch traced here: 573 us
  waiting for transfers between devices  229 us (40%)
  Pallas kernels  221 us (38%)
  starting transfers between devices  112 us (19%)
  local copies, waits for them, and re-layouts  7.61 us (1%)
    ppermute x27, waiting for transfers between devices, across(): return lax.ppermute(block, 'uly', [(i, i ^ step) for i in range(size)])  212 us
    pallas_call x6, Pallas kernels, attend(): pl.pallas_call(body, grid_spec=pltpu.PrefetchScalarGridSpec(num_scalar_pr...  170 us
    ppermute x12, starting transfers between devices, swapped(): return lax.ppermute(block, 'blk', pairs + [(b, a) for a, b in pairs])  82 us
    ppermute x27, starting transfers between devices, across(): return lax.ppermute(block, 'uly', [(i, i ^ step) for i in range(size)])  30.3 us
    pallas_call x6, Pallas kernels, join(): pl.pallas_call(body, grid=(heads, 2), in_specs=[pl.BlockSpec((None, None,...  23 us
    pallas_call x6, Pallas kernels, pack(): pl.pallas_call(body, grid_spec=pltpu.PrefetchScalarGridSpec(num_scalar_pr...  21.8 us
    ppermute x12, waiting for transfers between devices, swapped(): return lax.ppermute(block, 'blk', pairs + [(b, a) for a, b in pairs])  17.2 us
  transfers between devices with their start and end apart: 39, of which 13 were waited for; matrix products, arithmetic and copies ran while one was open for 1% of the time, Pallas kernels for 37%

profile of v3, /device:TPU:11, one launch (start us, length us, event | category | flops | bytes accessed | tf_op | source)
XLA Modules:
  0.0 573.4 jit_solution(2861766552159240064)
XLA Ops:
  7.6 3.7 pack.7
  14.6 23.1 %collective-permute-done.3.refs_1_ = bf16[3,2,512,128]{3,2,1,0:T(8,128)(2,1)S(1)} collective-permute-done((bf16[3,2,512,128]{3,2,1,0:T(8,128)(2,1)}, bf16[3,2,512,128]{3,2,1,0:T(8,128)(2,1)S(1)}, u32[]{:S(2)}, u32[]{:S(2)}) %collective-permute-start.3) | collective-permute-done | bytes 786464 | tf_op jit(solution)/shard_map/ppermute | solution.py:280
  37.7 3.8 collective-permute-done.4.refs_2_
  41.5 33.7 %collective-permute-done.5.refs_3_ = bf16[3,2,512,128]{3,2,1,0:T(8,128)(2,1)S(1)} collective-permute-done((bf16[3,2,512,128]{3,2,1,0:T(8,128)(2,1)}, bf16[3,2,512,128]{3,2,1,0:T(8,128)(2,1)S(1)}, u32[]{:S(2)}, u32[]{:S(2)}) %collective-permute-start.5) | collective-permute-done | bytes 786464 | tf_op jit(solution)/shard_map/ppermute | solution.py:280
  76.1 3.8 join.6.refs_12_.refs_5_
  79.9 36.8 %collective-permute-start.8 = (bf16[2,2,2048,128]{3,2,1,0:T(8,128)(2,1)}, bf16[2,2,2048,128]{3,2,1,0:T(8,128)(2,1)}, u32[]{:S(2)}, u32[]{:S(2)}) collective-permute-start(bf16[2,2,2048,128]{3,2,1,0:T(8,128)(2,1)} %join.6.refs_12_.refs_5_), channel_id=1, source_target_pairs={{0,4},{8,12},{16,20},{24,28},{4,0},{12,8},{20,16},{28,24},{1,5},{9... | collective-permute-start | bytes 6291464 | tf_op jit(solution)/shard_map/ppermute | solution.py:286
  128.0 48.4 %collective-permute-done.2.refs_3_ = bf16[3,2,512,128]{3,2,1,0:T(8,128)(2,1)} collective-permute-done((bf16[3,2,512,128]{3,2,1,0:T(8,128)(2,1)}, bf16[3,2,512,128]{3,2,1,0:T(8,128)(2,1)}, u32[]{:S(2)}, u32[]{:S(2)}) %collective-permute-start.2) | collective-permute-done | bytes 786464 | tf_op jit(solution)/shard_map/ppermute | solution.py:280
  176.4 3.8 join.7.refs_12_.refs_5_
  185.3 7.0 %collective-permute-done.11.refs_2_ = bf16[3,2,512,128]{3,2,1,0:T(8,128)(2,1)} collective-permute-done((bf16[3,2,512,128]{3,2,1,0:T(8,128)(2,1)}, bf16[3,2,512,128]{3,2,1,0:T(8,128)(2,1)}, u32[]{:S(2)}, u32[]{:S(2)}) %collective-permute-start.11) | collective-permute-done | bytes 786464 | tf_op jit(solution)/shard_map/ppermute | solution.py:280
  192.3 6.2 %collective-permute-start.7 = (bf16[2,2,2048,128]{3,2,1,0:T(8,128)(2,1)}, bf16[2,2,2048,128]{3,2,1,0:T(8,128)(2,1)}, u32[]{:S(2)}, u32[]{:S(2)}) collective-permute-start(bf16[2,2,2048,128]{3,2,1,0:T(8,128)(2,1)} %join.7.refs_12_.refs_5_), channel_id=1, source_target_pairs={{4,8},{12,16},{20,24},{8,4},{16,12},{24,20},{5,9},{13,17},{21,25},... | collective-permute-start | bytes 6291464 | tf_op jit(solution)/shard_map/ppermute | solution.py:286
  203.4 6.7 %collective-permute-done.12.refs_3_ = bf16[3,2,512,128]{3,2,1,0:T(8,128)(2,1)} collective-permute-done((bf16[3,2,512,128]{3,2,1,0:T(8,128)(2,1)}, bf16[3,2,512,128]{3,2,1,0:T(8,128)(2,1)}, u32[]{:S(2)}, u32[]{:S(2)}) %collective-permute-start.12) | collective-permute-done | bytes 786464 | tf_op jit(solution)/shard_map/ppermute | solution.py:280
  216.1 28.4 %attend.6 = (bf16[4,512,128]{2,1,0:T(8,128)(2,1)}, bf16[4,512,128]{2,1,0:T(8,128)(2,1)}, bf16[4,512,128]{2,1,0:T(8,128)(2,1)}, bf16[4,512,128]{2,1,0:T(8,128)(2,1)}) custom-call(s32[704]{0:T(1024)} %reshape.160.unit_ref, s32[1]{0:T(128)} %bitcast.5.count_ref, bf16[128,128]{1,0:T(8,128)(2,1)} %select_convert_fusion.signs_ref, ...), custom_call_target="tpu_custom_call" | custom-call | bytes 1048576 | tf_op jit(solution)/shard_map/attend/pallas_call | solution.py:250
  244.5 3.8 join.8.refs_12_.refs_5_
  248.3 3.7 pack.10
  253.1 13.9 %collective-permute-start.19 = (bf16[2,2,2048,128]{3,2,1,0:T(8,128)(2,1)S(1)}, bf16[2,2,2048,128]{3,2,1,0:T(8,128)(2,1)}, u32[]{:S(2)}, u32[]{:S(2)}) collective-permute-start(bf16[2,2,2048,128]{3,2,1,0:T(8,128)(2,1)S(1)} %copy-done.1), channel_id=1, source_target_pairs={{0,4},{8,12},{16,20},{24,28},{4,0},{12,8},{20,16},{28,24},{1,5},{9... | collective-permute-start | bytes 6291464 | tf_op jit(solution)/shard_map/ppermute | solution.py:286
  273.4 28.4 %attend.7 = (bf16[4,512,128]{2,1,0:T(8,128)(2,1)}, bf16[4,512,128]{2,1,0:T(8,128)(2,1)}, bf16[4,512,128]{2,1,0:T(8,128)(2,1)}, bf16[4,512,128]{2,1,0:T(8,128)(2,1)}) custom-call(s32[704]{0:T(1024)} %reshape.160.unit_ref, s32[1]{0:T(128)} %bitcast.5.count_ref, ...), custom_call_target="tpu_custom_call", output_to_operand_aliasing={{0}: (10, {}), {1}: (11, {}), {2}: (12, {}), {3}: (13, {})} | custom-call | bytes 1048576 | tf_op jit(solution)/shard_map/attend/pallas_call | solution.py:250
  301.8 3.9 join.9.refs_12_.refs_5_
  305.7 3.7 collective-permute-start.27
  315.9 31.1 %collective-permute-done.18.refs_3_ = bf16[3,2,512,128]{3,2,1,0:T(8,128)(2,1)S(1)} collective-permute-done((bf16[3,2,512,128]{3,2,1,0:T(8,128)(2,1)S(1)}, bf16[3,2,512,128]{3,2,1,0:T(8,128)(2,1)S(1)}, u32[]{:S(2)}, u32[]{:S(2)}) %collective-permute-start.18) | collective-permute-done | bytes 786464 | tf_op jit(solution)/shard_map/ppermute | solution.py:280
  349.6 28.4 %attend.8 = (bf16[6,512,128]{2,1,0:T(8,128)(2,1)}, bf16[6,512,128]{2,1,0:T(8,128)(2,1)}, bf16[6,512,128]{2,1,0:T(8,128)(2,1)}, bf16[6,512,128]{2,1,0:T(8,128)(2,1)}) custom-call(s32[704]{0:T(1024)} %reshape.160.unit_ref, s32[1]{0:T(128)} %bitcast.5.count_ref, bf16[128,128]{1,0:T(8,128)(2,1)} %select_convert_fusion.signs_ref, ...), custom_call_target="tpu_custom_call" | custom-call | bytes 1048576 | tf_op jit(solution)/shard_map/attend/pallas_call | solution.py:250
  377.9 3.8 join.10.refs_11_.refs_5_
  381.8 6.7 %collective-permute-start.25 = (bf16[2,2,2048,128]{3,2,1,0:T(8,128)(2,1)}, bf16[2,2,2048,128]{3,2,1,0:T(8,128)(2,1)}, u32[]{:S(2)}, u32[]{:S(2)}) collective-permute-start(bf16[2,2,2048,128]{3,2,1,0:T(8,128)(2,1)} %join.10.refs_11_.refs_5_), channel_id=1, source_target_pairs={{4,8},{12,16},{20,24},{8,4},{16,12},{24,20},{5,9},{13,17},{21,25},... | collective-permute-start | bytes 6291464 | tf_op jit(solution)/shard_map/ppermute | solution.py:286
  388.5 28.4 %attend.9 = (bf16[6,512,128]{2,1,0:T(8,128)(2,1)}, bf16[6,512,128]{2,1,0:T(8,128)(2,1)}, bf16[6,512,128]{2,1,0:T(8,128)(2,1)}, bf16[6,512,128]{2,1,0:T(8,128)(2,1)}) custom-call(s32[704]{0:T(1024)} %reshape.160.unit_ref, s32[1]{0:T(128)} %bitcast.5.count_ref, ...), custom_call_target="tpu_custom_call", output_to_operand_aliasing={{0}: (10, {}), {1}: (11, {}), {2}: (12, {}), {3}: (13, {})} | custom-call | bytes 1048576 | tf_op jit(solution)/shard_map/attend/pallas_call | solution.py:250
  418.1 3.8 join.11.refs_11_.refs_5_
  429.3 4.5 collective-permute-done.25.refs_6_
  435.1 28.4 %attend.10 = (bf16[6,512,128]{2,1,0:T(8,128)(2,1)}, bf16[6,512,128]{2,1,0:T(8,128)(2,1)}, bf16[6,512,128]{2,1,0:T(8,128)(2,1)}, bf16[6,512,128]{2,1,0:T(8,128)(2,1)}) custom-call(s32[704]{0:T(1024)} %reshape.160.unit_ref, s32[1]{0:T(128)} %bitcast.5.count_ref, ...), custom_call_target="tpu_custom_call", output_to_operand_aliasing={{0}: (10, {}), {1}: (11, {}), {2}: (12, {}), {3}: (13, {})} | custom-call | bytes 1048576 | tf_op jit(solution)/shard_map/attend/pallas_call | solution.py:250
  466.3 12.6 %collective-permute-done.35.refs_6_ = bf16[2,2,2048,128]{3,2,1,0:T(8,128)(2,1)} collective-permute-done((bf16[2,2,2048,128]{3,2,1,0:T(8,128)(2,1)}, bf16[2,2,2048,128]{3,2,1,0:T(8,128)(2,1)}, u32[]{:S(2)}, u32[]{:S(2)}) %collective-permute-start.35) | collective-permute-done | bytes 2097184 | tf_op jit(solution)/shard_map/ppermute | solution.py:286
  480.3 28.4 %attend.11 = (bf16[2,512,128]{2,1,0:T(8,128)(2,1)}, bf16[2,512,128]{2,1,0:T(8,128)(2,1)}, bf16[2,512,128]{2,1,0:T(8,128)(2,1)}, bf16[2,512,128]{2,1,0:T(8,128)(2,1)}) custom-call(s32[704]{0:T(1024)} %reshape.160.unit_ref, s32[1]{0:T(128)} %bitcast.5.count_ref, bf16[128,128]{1,0:T(8,128)(2,1)} %select_convert_fusion.signs_ref, ...), custom_call_target="tpu_custom_call" | custom-call | bytes 1048576 | tf_op jit(solution)/shard_map/attend/pallas_call | solution.py:250
  510.4 15.1 %collective-permute-done.36.refs_9_ = bf16[2,512,128]{2,1,0:T(8,128)(2,1)S(1)} collective-permute-done((bf16[2,512,128]{2,1,0:T(8,128)(2,1)}, bf16[2,512,128]{2,1,0:T(8,128)(2,1)S(1)}, u32[]{:S(2)}, u32[]{:S(2)}) %collective-permute-start.36) | collective-permute-done | bytes 262176 | tf_op jit(solution)/shard_map/ppermute | solution.py:280
  525.5 33.8 %collective-permute-done.37.refs_10_ = bf16[2,512,128]{2,1,0:T(8,128)(2,1)S(1)} collective-permute-done((bf16[2,512,128]{2,1,0:T(8,128)(2,1)}, bf16[2,512,128]{2,1,0:T(8,128)(2,1)S(1)}, u32[]{:S(2)}, u32[]{:S(2)}) %collective-permute-start.37) | collective-permute-done | bytes 262176 | tf_op jit(solution)/shard_map/ppermute | solution.py:280
  559.3 6.5 %collective-permute-done.38.refs_11_ = bf16[2,512,128]{2,1,0:T(8,128)(2,1)S(1)} collective-permute-done((bf16[2,512,128]{2,1,0:T(8,128)(2,1)}, bf16[2,512,128]{2,1,0:T(8,128)(2,1)S(1)}, u32[]{:S(2)}, u32[]{:S(2)}) %collective-permute-start.38) | collective-permute-done | bytes 262176 | tf_op jit(solution)/shard_map/ppermute | solution.py:280
  567.0 6.4 %collect.1 = bf16[512,6144]{1,0:T(8,128)(2,1)} custom-call(s32[1]{0:T(128)} %bitcast.z_ref, bf16[4,512,128]{2,1,0:T(8,128)(2,1)} %get-tuple-element.71.refs_4_.refs_0_, bf16[4,512,128]{2,1,0:T(8,128)(2,1)} %copy-done.13, bf16[4,512,128]{2,1,0:T(8,128)(2,1)} %collective-permute-done.14.refs_2_, bf16[4,512,128]{2,1,0:T(8,128)(2,1)} %collective-permute-done.15.refs_3_, ...), custom_call_target="tpu_custom_call" | custom-call | bytes 1048576 | tf_op jit(solution)/shard_map/collect/pallas_call | solution.py:112
  (130 shorter events, 72.3 us)
Async XLA Ops:
  7.4 67.8 %collective-permute-start.5 = (bf16[3,2,512,128]{3,2,1,0:T(8,128)(2,1)}, bf16[3,2,512,128]{3,2,1,0:T(8,128)(2,1)S(1)}, u32[]{:S(2)}, u32[]{:S(2)}) collective-permute-start(bf16[3,2,512,128]{3,2,1,0:T(8,128)(2,1)} %get-tuple-element.60), channel_id=1, source_target_pairs={{0,3},{1,2},{2,1},{3,0},{4,7},{5,6},{6,5},{7,4},{8,11},{9,10},{10,... | collective-permute-start | bytes 2359304 | tf_op jit(solution)/shard_map/ppermute | solution.py:280
  11.3 110.5 %collective-permute-start = (bf16[3,2,512,128]{3,2,1,0:T(8,128)(2,1)}, bf16[3,2,512,128]{3,2,1,0:T(8,128)(2,1)}, u32[]{:S(2)}, u32[]{:S(2)}) collective-permute-start(bf16[3,2,512,128]{3,2,1,0:T(8,128)(2,1)} %get-tuple-element.55), channel_id=1, source_target_pairs={{0,1},{1,0},{2,3},{3,2},{4,5},{5,4},{6,7},{7,6},{8,9},{9,8},{10,11... | collective-permute-start | bytes 2359304 | tf_op jit(solution)/shard_map/ppermute | solution.py:280
  12.5 112.6 %collective-permute-start.1 = (bf16[3,2,512,128]{3,2,1,0:T(8,128)(2,1)}, bf16[3,2,512,128]{3,2,1,0:T(8,128)(2,1)}, u32[]{:S(2)}, u32[]{:S(2)}) collective-permute-start(bf16[3,2,512,128]{3,2,1,0:T(8,128)(2,1)} %get-tuple-element.56), channel_id=1, source_target_pairs={{0,2},{1,3},{2,0},{3,1},{4,6},{5,7},{6,4},{7,5},{8,10},{9,11},{10,... | collective-permute-start | bytes 2359304 | tf_op jit(solution)/shard_map/ppermute | solution.py:280
  79.9 130.2 %collective-permute-start.8 = (bf16[2,2,2048,128]{3,2,1,0:T(8,128)(2,1)}, bf16[2,2,2048,128]{3,2,1,0:T(8,128)(2,1)}, u32[]{:S(2)}, u32[]{:S(2)}) collective-permute-start(bf16[2,2,2048,128]{3,2,1,0:T(8,128)(2,1)} %join.6.refs_12_.refs_5_), channel_id=1, source_target_pairs={{0,4},{8,12},{16,20},{24,28},{4,0},{12,8},{20,16},{28,24},{1,5},{9... | collective-permute-start | bytes 6291464 | tf_op jit(solution)/shard_map/ppermute | solution.py:286
  116.8 59.6 %collective-permute-start.2 = (bf16[3,2,512,128]{3,2,1,0:T(8,128)(2,1)}, bf16[3,2,512,128]{3,2,1,0:T(8,128)(2,1)}, u32[]{:S(2)}, u32[]{:S(2)}) collective-permute-start(bf16[3,2,512,128]{3,2,1,0:T(8,128)(2,1)} %get-tuple-element.57), channel_id=1, source_target_pairs={{0,3},{1,2},{2,1},{3,0},{4,7},{5,6},{6,5},{7,4},{8,11},{9,10},{10,... | collective-permute-start | bytes 2359304 | tf_op jit(solution)/shard_map/ppermute | solution.py:280
  121.6 62.2 %collective-permute-start.10 = (bf16[3,2,512,128]{3,2,1,0:T(8,128)(2,1)}, bf16[3,2,512,128]{3,2,1,0:T(8,128)(2,1)S(1)}, u32[]{:S(2)}, u32[]{:S(2)}) collective-permute-start(bf16[3,2,512,128]{3,2,1,0:T(8,128)(2,1)} %get-tuple-element.67), channel_id=1, source_target_pairs={{0,1},{1,0},{2,3},{3,2},{4,5},{5,4},{6,7},{7,6},{8,9},{9,8},{10,11... | collective-permute-start | bytes 2359304 | tf_op jit(solution)/shard_map/ppermute | solution.py:280
  121.7 91.0 %collective-permute-start.9 = (bf16[2,2,2048,128]{3,2,1,0:T(8,128)(2,1)S(1)}, bf16[2,2,2048,128]{3,2,1,0:T(8,128)(2,1)}, u32[]{:S(2)}, u32[]{:S(2)}) collective-permute-start(bf16[2,2,2048,128]{3,2,1,0:T(8,128)(2,1)S(1)} %copy-done), channel_id=1, source_target_pairs={{4,8},{12,16},{20,24},{8,4},{16,12},{24,20},{5,9},{13,17},{21,25},... | collective-permute-start | bytes 6291464 | tf_op jit(solution)/shard_map/ppermute | solution.py:286
  125.1 67.2 %collective-permute-start.11 = (bf16[3,2,512,128]{3,2,1,0:T(8,128)(2,1)}, bf16[3,2,512,128]{3,2,1,0:T(8,128)(2,1)}, u32[]{:S(2)}, u32[]{:S(2)}) collective-permute-start(bf16[3,2,512,128]{3,2,1,0:T(8,128)(2,1)} %get-tuple-element.68), channel_id=1, source_target_pairs={{0,2},{1,3},{2,0},{3,1},{4,6},{5,7},{6,4},{7,5},{8,10},{9,11},{10,... | collective-permute-start | bytes 2359304 | tf_op jit(solution)/shard_map/ppermute | solution.py:280
  180.2 86.8 %collective-permute-start.6 = (bf16[2,2,2048,128]{3,2,1,0:T(8,128)(2,1)}, bf16[2,2,2048,128]{3,2,1,0:T(8,128)(2,1)}, u32[]{:S(2)}, u32[]{:S(2)}) collective-permute-start(bf16[2,2,2048,128]{3,2,1,0:T(8,128)(2,1)} %join.7.refs_12_.refs_5_), channel_id=1, source_target_pairs={{0,4},{8,12},{16,20},{24,28},{4,0},{12,8},{20,16},{28,24},{1,5},{9... | collective-permute-start | bytes 6291464 | tf_op jit(solution)/shard_map/ppermute | solution.py:286
  192.3 77.9 %collective-permute-start.7 = (bf16[2,2,2048,128]{3,2,1,0:T(8,128)(2,1)}, bf16[2,2,2048,128]{3,2,1,0:T(8,128)(2,1)}, u32[]{:S(2)}, u32[]{:S(2)}) collective-permute-start(bf16[2,2,2048,128]{3,2,1,0:T(8,128)(2,1)} %join.7.refs_12_.refs_5_), channel_id=1, source_target_pairs={{4,8},{12,16},{20,24},{8,4},{16,12},{24,20},{5,9},{13,17},{21,25},... | collective-permute-start | bytes 6291464 | tf_op jit(solution)/shard_map/ppermute | solution.py:286
  210.1 41.9 %collective-permute-start.21 = (bf16[3,2,512,128]{3,2,1,0:T(8,128)(2,1)}, bf16[3,2,512,128]{3,2,1,0:T(8,128)(2,1)S(1)}, u32[]{:S(2)}, u32[]{:S(2)}) collective-permute-start(bf16[3,2,512,128]{3,2,1,0:T(8,128)(2,1)} %get-tuple-element.78), channel_id=1, source_target_pairs={{0,1},{1,0},{2,3},{3,2},{4,5},{5,4},{6,7},{7,6},{8,9},{9,8},{10,11... | collective-permute-start | bytes 2359304 | tf_op jit(solution)/shard_map/ppermute | solution.py:280
  210.1 43.0 %collective-permute-start.22 = (bf16[3,2,512,128]{3,2,1,0:T(8,128)(2,1)}, bf16[3,2,512,128]{3,2,1,0:T(8,128)(2,1)}, u32[]{:S(2)}, u32[]{:S(2)}) collective-permute-start(bf16[3,2,512,128]{3,2,1,0:T(8,128)(2,1)} %get-tuple-element.79), channel_id=1, source_target_pairs={{0,2},{1,3},{2,0},{3,1},{4,6},{5,7},{6,4},{7,5},{8,10},{9,11},{10,... | collective-permute-start | bytes 2359304 | tf_op jit(solution)/shard_map/ppermute | solution.py:280
  212.8 89.0 %collective-permute-start.23 = (bf16[3,2,512,128]{3,2,1,0:T(8,128)(2,1)}, bf16[3,2,512,128]{3,2,1,0:T(8,128)(2,1)}, u32[]{:S(2)}, u32[]{:S(2)}) collective-permute-start(bf16[3,2,512,128]{3,2,1,0:T(8,128)(2,1)} %get-tuple-element.80), channel_id=1, source_target_pairs={{0,3},{1,2},{2,1},{3,0},{4,7},{5,6},{6,5},{7,4},{8,11},{9,10},{10,... | collective-permute-start | bytes 2359304 | tf_op jit(solution)/shard_map/ppermute | solution.py:280
  252.0 53.7 %collective-permute-start.16 = (bf16[3,2,512,128]{3,2,1,0:T(8,128)(2,1)}, bf16[3,2,512,128]{3,2,1,0:T(8,128)(2,1)}, u32[]{:S(2)}, u32[]{:S(2)}) collective-permute-start(bf16[3,2,512,128]{3,2,1,0:T(8,128)(2,1)} %get-tuple-element.75), channel_id=1, source_target_pairs={{0,1},{1,0},{2,3},{3,2},{4,5},{5,4},{6,7},{7,6},{8,9},{9,8},{10,11... | collective-permute-start | bytes 2359304 | tf_op jit(solution)/shard_map/ppermute | solution.py:280
  253.1 93.8 %collective-permute-start.19 = (bf16[2,2,2048,128]{3,2,1,0:T(8,128)(2,1)S(1)}, bf16[2,2,2048,128]{3,2,1,0:T(8,128)(2,1)}, u32[]{:S(2)}, u32[]{:S(2)}) collective-permute-start(bf16[2,2,2048,128]{3,2,1,0:T(8,128)(2,1)S(1)} %copy-done.1), channel_id=1, source_target_pairs={{0,4},{8,12},{16,20},{24,28},{4,0},{12,8},{20,16},{28,24},{1,5},{9... | collective-permute-start | bytes 6291464 | tf_op jit(solution)/shard_map/ppermute | solution.py:286
  267.0 82.4 %collective-permute-start.20 = (bf16[2,2,2048,128]{3,2,1,0:T(8,128)(2,1)S(1)}, bf16[2,2,2048,128]{3,2,1,0:T(8,128)(2,1)}, u32[]{:S(2)}, u32[]{:S(2)}) collective-permute-start(bf16[2,2,2048,128]{3,2,1,0:T(8,128)(2,1)S(1)} %copy-done.1), channel_id=1, source_target_pairs={{4,8},{12,16},{20,24},{8,4},{16,12},{24,20},{5,9},{13,17},{21,25},... | collective-permute-start | bytes 6291464 | tf_op jit(solution)/shard_map/ppermute | solution.py:286
  270.2 41.8 %collective-permute-start.17 = (bf16[3,2,512,128]{3,2,1,0:T(8,128)(2,1)}, bf16[3,2,512,128]{3,2,1,0:T(8,128)(2,1)}, u32[]{:S(2)}, u32[]{:S(2)}) collective-permute-start(bf16[3,2,512,128]{3,2,1,0:T(8,128)(2,1)} %get-tuple-element.76), channel_id=1, source_target_pairs={{0,2},{1,3},{2,0},{3,1},{4,6},{5,7},{6,4},{7,5},{8,10},{9,11},{10,... | collective-permute-start | bytes 2359304 | tf_op jit(solution)/shard_map/ppermute | solution.py:280
  305.7 76.0 %collective-permute-start.26 = (bf16[2,2,2048,128]{3,2,1,0:T(8,128)(2,1)}, bf16[2,2,2048,128]{3,2,1,0:T(8,128)(2,1)}, u32[]{:S(2)}, u32[]{:S(2)}) collective-permute-start(bf16[2,2,2048,128]{3,2,1,0:T(8,128)(2,1)} %join.9.refs_12_.refs_5_), channel_id=1, source_target_pairs={{0,4},{8,12},{16,20},{24,28},{4,0},{12,8},{20,16},{28,24},{1,5},{9... | collective-permute-start | bytes 6291464 | tf_op jit(solution)/shard_map/ppermute | solution.py:286
  305.7 76.0 %collective-permute-start.27 = (bf16[2,2,2048,128]{3,2,1,0:T(8,128)(2,1)}, bf16[2,2,2048,128]{3,2,1,0:T(8,128)(2,1)}, u32[]{:S(2)}, u32[]{:S(2)}) collective-permute-start(bf16[2,2,2048,128]{3,2,1,0:T(8,128)(2,1)} %join.9.refs_12_.refs_5_), channel_id=1, source_target_pairs={{4,8},{12,16},{20,24},{8,4},{16,12},{24,20},{5,9},{13,17},{21,25},... | collective-permute-start | bytes 6291464 | tf_op jit(solution)/shard_map/ppermute | solution.py:286
  346.9 69.9 %collective-permute-start.28 = (bf16[3,2,512,128]{3,2,1,0:T(8,128)(2,1)}, bf16[3,2,512,128]{3,2,1,0:T(8,128)(2,1)S(1)}, u32[]{:S(2)}, u32[]{:S(2)}) collective-permute-start(bf16[3,2,512,128]{3,2,1,0:T(8,128)(2,1)} %get-tuple-element.90), channel_id=1, source_target_pairs={{0,1},{1,0},{2,3},{3,2},{4,5},{5,4},{6,7},{7,6},{8,9},{9,8},{10,11... | collective-permute-start | bytes 2359304 | tf_op jit(solution)/shard_map/ppermute | solution.py:280
  346.9 69.9 %collective-permute-start.29 = (bf16[3,2,512,128]{3,2,1,0:T(8,128)(2,1)}, bf16[3,2,512,128]{3,2,1,0:T(8,128)(2,1)}, u32[]{:S(2)}, u32[]{:S(2)}) collective-permute-start(bf16[3,2,512,128]{3,2,1,0:T(8,128)(2,1)} %get-tuple-element.91), channel_id=1, source_target_pairs={{0,2},{1,3},{2,0},{3,1},{4,6},{5,7},{6,4},{7,5},{8,10},{9,11},{10,... | collective-permute-start | bytes 2359304 | tf_op jit(solution)/shard_map/ppermute | solution.py:280
  349.4 67.5 %collective-permute-start.30 = (bf16[3,2,512,128]{3,2,1,0:T(8,128)(2,1)}, bf16[3,2,512,128]{3,2,1,0:T(8,128)(2,1)S(1)}, u32[]{:S(2)}, u32[]{:S(2)}) collective-permute-start(bf16[3,2,512,128]{3,2,1,0:T(8,128)(2,1)} %get-tuple-element.92), channel_id=1, source_target_pairs={{0,3},{1,2},{2,1},{3,0},{4,7},{5,6},{6,5},{7,4},{8,11},{9,10},{10,... | collective-permute-start | bytes 2359304 | tf_op jit(solution)/shard_map/ppermute | solution.py:280
  381.8 45.1 %collective-permute-start.24 = (bf16[2,2,2048,128]{3,2,1,0:T(8,128)(2,1)}, bf16[2,2,2048,128]{3,2,1,0:T(8,128)(2,1)}, u32[]{:S(2)}, u32[]{:S(2)}) collective-permute-start(bf16[2,2,2048,128]{3,2,1,0:T(8,128)(2,1)} %join.10.refs_11_.refs_5_), channel_id=1, source_target_pairs={{0,4},{8,12},{16,20},{24,28},{4,0},{12,8},{20,16},{28,24},{1,5},{9... | collective-permute-start | bytes 6291464 | tf_op jit(solution)/shard_map/ppermute | solution.py:286
  381.8 52.1 %collective-permute-start.25 = (bf16[2,2,2048,128]{3,2,1,0:T(8,128)(2,1)}, bf16[2,2,2048,128]{3,2,1,0:T(8,128)(2,1)}, u32[]{:S(2)}, u32[]{:S(2)}) collective-permute-start(bf16[2,2,2048,128]{3,2,1,0:T(8,128)(2,1)} %join.10.refs_11_.refs_5_), channel_id=1, source_target_pairs={{4,8},{12,16},{20,24},{8,4},{16,12},{24,20},{5,9},{13,17},{21,25},... | collective-permute-start | bytes 6291464 | tf_op jit(solution)/shard_map/ppermute | solution.py:286
  421.9 44.3 %collective-permute-start.34 = (bf16[2,2,2048,128]{3,2,1,0:T(8,128)(2,1)}, bf16[2,2,2048,128]{3,2,1,0:T(8,128)(2,1)S(1)}, u32[]{:S(2)}, u32[]{:S(2)}) collective-permute-start(bf16[2,2,2048,128]{3,2,1,0:T(8,128)(2,1)} %join.11.refs_11_.refs_5_), channel_id=1, source_target_pairs={{0,4},{8,12},{16,20},{24,28},{4,0},{12,8},{20,16},{28,24},{1,5},{9... | collective-permute-start | bytes 6291464 | tf_op jit(solution)/shard_map/ppermute | solution.py:286
  423.6 55.3 %collective-permute-start.35 = (bf16[2,2,2048,128]{3,2,1,0:T(8,128)(2,1)}, bf16[2,2,2048,128]{3,2,1,0:T(8,128)(2,1)}, u32[]{:S(2)}, u32[]{:S(2)}) collective-permute-start(bf16[2,2,2048,128]{3,2,1,0:T(8,128)(2,1)} %join.11.refs_11_.refs_5_), channel_id=1, source_target_pairs={{4,8},{12,16},{20,24},{8,4},{16,12},{24,20},{5,9},{13,17},{21,25},... | collective-permute-start | bytes 6291464 | tf_op jit(solution)/shard_map/ppermute | solution.py:286
  426.8 81.8 %collective-permute-start.14 = (bf16[4,512,128]{2,1,0:T(8,128)(2,1)}, bf16[4,512,128]{2,1,0:T(8,128)(2,1)}, u32[]{:S(2)}, u32[]{:S(2)}) collective-permute-start(bf16[4,512,128]{2,1,0:T(8,128)(2,1)} %get-tuple-element.73), channel_id=1, source_target_pairs={{0,2},{1,3},{2,0},{3,1},{4,6},{5,7},{6,4},{7,5},{8,10},{9,11},{10,... | collective-permute-start | bytes 1572872 | tf_op jit(solution)/shard_map/ppermute | solution.py:280
  433.8 76.5 %collective-permute-start.15 = (bf16[4,512,128]{2,1,0:T(8,128)(2,1)}, bf16[4,512,128]{2,1,0:T(8,128)(2,1)}, u32[]{:S(2)}, u32[]{:S(2)}) collective-permute-start(bf16[4,512,128]{2,1,0:T(8,128)(2,1)} %get-tuple-element.74), channel_id=1, source_target_pairs={{0,3},{1,2},{2,1},{3,0},{4,7},{5,6},{6,5},{7,4},{8,11},{9,10},{10,... | collective-permute-start | bytes 1572872 | tf_op jit(solution)/shard_map/ppermute | solution.py:280
  464.4 101.4 %collective-permute-start.31 = (bf16[6,512,128]{2,1,0:T(8,128)(2,1)}, bf16[6,512,128]{2,1,0:T(8,128)(2,1)S(1)}, u32[]{:S(2)}, u32[]{:S(2)}) collective-permute-start(bf16[6,512,128]{2,1,0:T(8,128)(2,1)} %get-tuple-element.94), channel_id=1, source_target_pairs={{0,1},{1,0},{2,3},{3,2},{4,5},{5,4},{6,7},{7,6},{8,9},{9,8},{10,11... | collective-permute-start | bytes 2359304 | tf_op jit(solution)/shard_map/ppermute | solution.py:280
  466.2 99.5 %collective-permute-start.32 = (bf16[6,512,128]{2,1,0:T(8,128)(2,1)}, bf16[6,512,128]{2,1,0:T(8,128)(2,1)S(1)}, u32[]{:S(2)}, u32[]{:S(2)}) collective-permute-start(bf16[6,512,128]{2,1,0:T(8,128)(2,1)} %get-tuple-element.95), channel_id=1, source_target_pairs={{0,2},{1,3},{2,0},{3,1},{4,6},{5,7},{6,4},{7,5},{8,10},{9,11},{10,... | collective-permute-start | bytes 2359304 | tf_op jit(solution)/shard_map/ppermute | solution.py:280
  479.0 86.8 %collective-permute-start.33 = (bf16[6,512,128]{2,1,0:T(8,128)(2,1)}, bf16[6,512,128]{2,1,0:T(8,128)(2,1)}, u32[]{:S(2)}, u32[]{:S(2)}) collective-permute-start(bf16[6,512,128]{2,1,0:T(8,128)(2,1)} %get-tuple-element.96), channel_id=1, source_target_pairs={{0,3},{1,2},{2,1},{3,0},{4,7},{5,6},{6,5},{7,4},{8,11},{9,10},{10,... | collective-permute-start | bytes 2359304 | tf_op jit(solution)/shard_map/ppermute | solution.py:280
  510.3 49.0 %collective-permute-start.37 = (bf16[2,512,128]{2,1,0:T(8,128)(2,1)}, bf16[2,512,128]{2,1,0:T(8,128)(2,1)S(1)}, u32[]{:S(2)}, u32[]{:S(2)}) collective-permute-start(bf16[2,512,128]{2,1,0:T(8,128)(2,1)} %get-tuple-element.99), channel_id=1, source_target_pairs={{0,2},{1,3},{2,0},{3,1},{4,6},{5,7},{6,4},{7,5},{8,10},{9,11},{10,... | collective-permute-start | bytes 786440 | tf_op jit(solution)/shard_map/ppermute | solution.py:280
  (27 other events, 499.2 us)

commit v4 on v3

--- a/solution.py
+++ b/solution.py
@@ -344,7 +344,7 @@
         if c >= 1:
             compute(c - 1)
     compute(steps - 1)
-    return collect(z, returned, heads_before, local_heads, tile)
+    return collect(z, returned, heads_before, local_heads, min(rows, 2 * tile))
 
 
 def solution(mesh):

time: 575 us -> 574 us (level)
  Pallas kernels: 221 us -> 209 us
  starting transfers between devices: 112 us -> 119 us
    pallas_call x6, Pallas kernels: 170 us -> 159 us  [attend(): pl.pallas_call(body, grid_spec=pltpu.PrefetchScalarGridSpec(num_scalar_pr...]
  transfers between devices with their start and end apart: 39 -> 39, of which waited for: 13 -> 14; matrix products, arithmetic and copies ran while one was open for 1% -> 1% of each run, Pallas kernels for 37% -> 35%
where the time goes in v4:
time: 574 us; the launch traced here: 573 us
  waiting for transfers between devices  234 us (41%)
  Pallas kernels  209 us (36%)
  starting transfers between devices  119 us (21%)
  local copies, waits for them, and re-layouts  7.36 us (1%)
    ppermute x27, waiting for transfers between devices, across(): return lax.ppermute(block, 'uly', [(i, i ^ step) for i in range(size)])  215 us
    pallas_call x6, Pallas kernels, attend(): pl.pallas_call(body, grid_spec=pltpu.PrefetchScalarGridSpec(num_scalar_pr...  159 us
    ppermute x12, starting transfers between devices, swapped(): return lax.ppermute(block, 'blk', pairs + [(b, a) for a, b in pairs])  87.7 us
    ppermute x27, starting transfers between devices, across(): return lax.ppermute(block, 'uly', [(i, i ^ step) for i in range(size)])  31.8 us
    pallas_call x6, Pallas kernels, join(): pl.pallas_call(body, grid=(heads, 2), in_specs=[pl.BlockSpec((None, None,...  23 us
    pallas_call x6, Pallas kernels, pack(): pl.pallas_call(body, grid_spec=pltpu.PrefetchScalarGridSpec(num_scalar_pr...  21.8 us
    ppermute x12, waiting for transfers between devices, swapped(): return lax.ppermute(block, 'blk', pairs + [(b, a) for a, b in pairs])  18.6 us
  transfers between devices with their start and end apart: 39, of which 14 were waited for; matrix products, arithmetic and copies ran while one was open for 1% of the time, Pallas kernels for 35%

profile of v4, /device:TPU:11, one launch (start us, length us, event | category | flops | bytes accessed | tf_op | source)
XLA Modules:
  0.0 572.6 jit_solution(1032569041549669029)
XLA Ops:
  7.6 3.7 pack.7
  14.6 23.1 %collective-permute-done.3.refs_1_ = bf16[3,2,512,128]{3,2,1,0:T(8,128)(2,1)S(1)} collective-permute-done((bf16[3,2,512,128]{3,2,1,0:T(8,128)(2,1)}, bf16[3,2,512,128]{3,2,1,0:T(8,128)(2,1)S(1)}, u32[]{:S(2)}, u32[]{:S(2)}) %collective-permute-start.3) | collective-permute-done | bytes 786464 | tf_op jit(solution)/shard_map/ppermute | solution.py:280
  37.7 3.8 collective-permute-done.4.refs_2_
  41.5 33.7 %collective-permute-done.5.refs_3_ = bf16[3,2,512,128]{3,2,1,0:T(8,128)(2,1)S(1)} collective-permute-done((bf16[3,2,512,128]{3,2,1,0:T(8,128)(2,1)}, bf16[3,2,512,128]{3,2,1,0:T(8,128)(2,1)S(1)}, u32[]{:S(2)}, u32[]{:S(2)}) %collective-permute-start.5) | collective-permute-done | bytes 786464 | tf_op jit(solution)/shard_map/ppermute | solution.py:280
  76.1 3.8 join.6.refs_12_.refs_5_
  79.9 36.8 %collective-permute-start.8 = (bf16[2,2,2048,128]{3,2,1,0:T(8,128)(2,1)}, bf16[2,2,2048,128]{3,2,1,0:T(8,128)(2,1)}, u32[]{:S(2)}, u32[]{:S(2)}) collective-permute-start(bf16[2,2,2048,128]{3,2,1,0:T(8,128)(2,1)} %join.6.refs_12_.refs_5_), channel_id=1, source_target_pairs={{0,4},{8,12},{16,20},{24,28},{4,0},{12,8},{20,16},{28,24},{1,5},{9... | collective-permute-start | bytes 6291464 | tf_op jit(solution)/shard_map/ppermute | solution.py:286
  128.0 48.4 %collective-permute-done.2.refs_3_ = bf16[3,2,512,128]{3,2,1,0:T(8,128)(2,1)} collective-permute-done((bf16[3,2,512,128]{3,2,1,0:T(8,128)(2,1)}, bf16[3,2,512,128]{3,2,1,0:T(8,128)(2,1)}, u32[]{:S(2)}, u32[]{:S(2)}) %collective-permute-start.2) | collective-permute-done | bytes 786464 | tf_op jit(solution)/shard_map/ppermute | solution.py:280
  176.4 3.8 join.7.refs_12_.refs_5_
  185.3 7.0 %collective-permute-done.11.refs_2_ = bf16[3,2,512,128]{3,2,1,0:T(8,128)(2,1)} collective-permute-done((bf16[3,2,512,128]{3,2,1,0:T(8,128)(2,1)}, bf16[3,2,512,128]{3,2,1,0:T(8,128)(2,1)}, u32[]{:S(2)}, u32[]{:S(2)}) %collective-permute-start.11) | collective-permute-done | bytes 786464 | tf_op jit(solution)/shard_map/ppermute | solution.py:280
  192.3 6.2 %collective-permute-start.7 = (bf16[2,2,2048,128]{3,2,1,0:T(8,128)(2,1)}, bf16[2,2,2048,128]{3,2,1,0:T(8,128)(2,1)}, u32[]{:S(2)}, u32[]{:S(2)}) collective-permute-start(bf16[2,2,2048,128]{3,2,1,0:T(8,128)(2,1)} %join.7.refs_12_.refs_5_), channel_id=1, source_target_pairs={{4,8},{12,16},{20,24},{8,4},{16,12},{24,20},{5,9},{13,17},{21,25},... | collective-permute-start | bytes 6291464 | tf_op jit(solution)/shard_map/ppermute | solution.py:286
  203.4 6.7 %collective-permute-done.12.refs_3_ = bf16[3,2,512,128]{3,2,1,0:T(8,128)(2,1)} collective-permute-done((bf16[3,2,512,128]{3,2,1,0:T(8,128)(2,1)}, bf16[3,2,512,128]{3,2,1,0:T(8,128)(2,1)}, u32[]{:S(2)}, u32[]{:S(2)}) %collective-permute-start.12) | collective-permute-done | bytes 786464 | tf_op jit(solution)/shard_map/ppermute | solution.py:280
  216.1 26.5 %attend.6 = (bf16[4,512,128]{2,1,0:T(8,128)(2,1)}, bf16[4,512,128]{2,1,0:T(8,128)(2,1)}, bf16[4,512,128]{2,1,0:T(8,128)(2,1)}, bf16[4,512,128]{2,1,0:T(8,128)(2,1)}) custom-call(s32[704]{0:T(1024)} %reshape.160.unit_ref, s32[1]{0:T(128)} %bitcast.5.count_ref, bf16[128,128]{1,0:T(8,128)(2,1)} %select_convert_fusion.signs_ref, ...), custom_call_target="tpu_custom_call" | custom-call | bytes 1048576 | tf_op jit(solution)/shard_map/attend/pallas_call | solution.py:250
  242.6 3.8 join.8.refs_12_.refs_5_
  246.4 3.7 pack.10
  251.2 15.8 %collective-permute-start.19 = (bf16[2,2,2048,128]{3,2,1,0:T(8,128)(2,1)S(1)}, bf16[2,2,2048,128]{3,2,1,0:T(8,128)(2,1)}, u32[]{:S(2)}, u32[]{:S(2)}) collective-permute-start(bf16[2,2,2048,128]{3,2,1,0:T(8,128)(2,1)S(1)} %copy-done.1), channel_id=1, source_target_pairs={{0,4},{8,12},{16,20},{24,28},{4,0},{12,8},{20,16},{28,24},{1,5},{9... | collective-permute-start | bytes 6291464 | tf_op jit(solution)/shard_map/ppermute | solution.py:286
  273.4 26.5 %attend.7 = (bf16[4,512,128]{2,1,0:T(8,128)(2,1)}, bf16[4,512,128]{2,1,0:T(8,128)(2,1)}, bf16[4,512,128]{2,1,0:T(8,128)(2,1)}, bf16[4,512,128]{2,1,0:T(8,128)(2,1)}) custom-call(s32[704]{0:T(1024)} %reshape.160.unit_ref, s32[1]{0:T(128)} %bitcast.5.count_ref, ...), custom_call_target="tpu_custom_call", output_to_operand_aliasing={{0}: (10, {}), {1}: (11, {}), {2}: (12, {}), {3}: (13, {})} | custom-call | bytes 1048576 | tf_op jit(solution)/shard_map/attend/pallas_call | solution.py:250
  299.9 3.9 join.9.refs_12_.refs_5_
  315.9 31.1 %collective-permute-done.18.refs_3_ = bf16[3,2,512,128]{3,2,1,0:T(8,128)(2,1)S(1)} collective-permute-done((bf16[3,2,512,128]{3,2,1,0:T(8,128)(2,1)S(1)}, bf16[3,2,512,128]{3,2,1,0:T(8,128)(2,1)S(1)}, u32[]{:S(2)}, u32[]{:S(2)}) %collective-permute-start.18) | collective-permute-done | bytes 786464 | tf_op jit(solution)/shard_map/ppermute | solution.py:280
  349.6 26.5 %attend.8 = (bf16[6,512,128]{2,1,0:T(8,128)(2,1)}, bf16[6,512,128]{2,1,0:T(8,128)(2,1)}, bf16[6,512,128]{2,1,0:T(8,128)(2,1)}, bf16[6,512,128]{2,1,0:T(8,128)(2,1)}) custom-call(s32[704]{0:T(1024)} %reshape.160.unit_ref, s32[1]{0:T(128)} %bitcast.5.count_ref, bf16[128,128]{1,0:T(8,128)(2,1)} %select_convert_fusion.signs_ref, ...), custom_call_target="tpu_custom_call" | custom-call | bytes 1048576 | tf_op jit(solution)/shard_map/attend/pallas_call | solution.py:250
  376.1 3.8 join.10.refs_11_.refs_5_
  379.9 5.3 collective-permute-start.24
  387.1 26.5 %attend.9 = (bf16[6,512,128]{2,1,0:T(8,128)(2,1)}, bf16[6,512,128]{2,1,0:T(8,128)(2,1)}, bf16[6,512,128]{2,1,0:T(8,128)(2,1)}, bf16[6,512,128]{2,1,0:T(8,128)(2,1)}) custom-call(s32[704]{0:T(1024)} %reshape.160.unit_ref, s32[1]{0:T(128)} %bitcast.5.count_ref, ...), custom_call_target="tpu_custom_call", output_to_operand_aliasing={{0}: (10, {}), {1}: (11, {}), {2}: (12, {}), {3}: (13, {})} | custom-call | bytes 1048576 | tf_op jit(solution)/shard_map/attend/pallas_call | solution.py:250
  416.1 3.8 join.11.refs_11_.refs_5_
  419.9 3.8 collective-permute-start.34
  429.5 6.8 %collective-permute-done.25.refs_6_ = bf16[2,2,2048,128]{3,2,1,0:T(8,128)(2,1)} collective-permute-done((bf16[2,2,2048,128]{3,2,1,0:T(8,128)(2,1)}, bf16[2,2,2048,128]{3,2,1,0:T(8,128)(2,1)}, u32[]{:S(2)}, u32[]{:S(2)}) %collective-permute-start.25) | collective-permute-done | bytes 2097184 | tf_op jit(solution)/shard_map/ppermute | solution.py:286
  437.6 26.5 %attend.10 = (bf16[6,512,128]{2,1,0:T(8,128)(2,1)}, bf16[6,512,128]{2,1,0:T(8,128)(2,1)}, bf16[6,512,128]{2,1,0:T(8,128)(2,1)}, bf16[6,512,128]{2,1,0:T(8,128)(2,1)}) custom-call(s32[704]{0:T(1024)} %reshape.160.unit_ref, s32[1]{0:T(128)} %bitcast.5.count_ref, ...), custom_call_target="tpu_custom_call", output_to_operand_aliasing={{0}: (10, {}), {1}: (11, {}), {2}: (12, {}), {3}: (13, {})} | custom-call | bytes 1048576 | tf_op jit(solution)/shard_map/attend/pallas_call | solution.py:250
  466.9 11.8 %collective-permute-done.35.refs_6_ = bf16[2,2,2048,128]{3,2,1,0:T(8,128)(2,1)} collective-permute-done((bf16[2,2,2048,128]{3,2,1,0:T(8,128)(2,1)}, bf16[2,2,2048,128]{3,2,1,0:T(8,128)(2,1)}, u32[]{:S(2)}, u32[]{:S(2)}) %collective-permute-start.35) | collective-permute-done | bytes 2097184 | tf_op jit(solution)/shard_map/ppermute | solution.py:286
  480.0 26.5 %attend.11 = (bf16[2,512,128]{2,1,0:T(8,128)(2,1)}, bf16[2,512,128]{2,1,0:T(8,128)(2,1)}, bf16[2,512,128]{2,1,0:T(8,128)(2,1)}, bf16[2,512,128]{2,1,0:T(8,128)(2,1)}) custom-call(s32[704]{0:T(1024)} %reshape.160.unit_ref, s32[1]{0:T(128)} %bitcast.5.count_ref, bf16[128,128]{1,0:T(8,128)(2,1)} %select_convert_fusion.signs_ref, ...), custom_call_target="tpu_custom_call" | custom-call | bytes 1048576 | tf_op jit(solution)/shard_map/attend/pallas_call | solution.py:250
  508.5 20.0 %collective-permute-done.36.refs_9_ = bf16[2,512,128]{2,1,0:T(8,128)(2,1)S(1)} collective-permute-done((bf16[2,512,128]{2,1,0:T(8,128)(2,1)}, bf16[2,512,128]{2,1,0:T(8,128)(2,1)S(1)}, u32[]{:S(2)}, u32[]{:S(2)}) %collective-permute-start.36) | collective-permute-done | bytes 262176 | tf_op jit(solution)/shard_map/ppermute | solution.py:280
  529.8 29.7 %collective-permute-done.37.refs_10_ = bf16[2,512,128]{2,1,0:T(8,128)(2,1)S(1)} collective-permute-done((bf16[2,512,128]{2,1,0:T(8,128)(2,1)}, bf16[2,512,128]{2,1,0:T(8,128)(2,1)S(1)}, u32[]{:S(2)}, u32[]{:S(2)}) %collective-permute-start.37) | collective-permute-done | bytes 262176 | tf_op jit(solution)/shard_map/ppermute | solution.py:280
  559.5 6.4 %collective-permute-done.38.refs_11_ = bf16[2,512,128]{2,1,0:T(8,128)(2,1)S(1)} collective-permute-done((bf16[2,512,128]{2,1,0:T(8,128)(2,1)}, bf16[2,512,128]{2,1,0:T(8,128)(2,1)S(1)}, u32[]{:S(2)}, u32[]{:S(2)}) %collective-permute-start.38) | collective-permute-done | bytes 262176 | tf_op jit(solution)/shard_map/ppermute | solution.py:280
  567.2 5.5 collect.1
  (130 shorter events, 80.9 us)
Async XLA Ops:
  7.4 67.8 %collective-permute-start.5 = (bf16[3,2,512,128]{3,2,1,0:T(8,128)(2,1)}, bf16[3,2,512,128]{3,2,1,0:T(8,128)(2,1)S(1)}, u32[]{:S(2)}, u32[]{:S(2)}) collective-permute-start(bf16[3,2,512,128]{3,2,1,0:T(8,128)(2,1)} %get-tuple-element.60), channel_id=1, source_target_pairs={{0,3},{1,2},{2,1},{3,0},{4,7},{5,6},{6,5},{7,4},{8,11},{9,10},{10,... | collective-permute-start | bytes 2359304 | tf_op jit(solution)/shard_map/ppermute | solution.py:280
  11.3 110.5 %collective-permute-start = (bf16[3,2,512,128]{3,2,1,0:T(8,128)(2,1)}, bf16[3,2,512,128]{3,2,1,0:T(8,128)(2,1)}, u32[]{:S(2)}, u32[]{:S(2)}) collective-permute-start(bf16[3,2,512,128]{3,2,1,0:T(8,128)(2,1)} %get-tuple-element.55), channel_id=1, source_target_pairs={{0,1},{1,0},{2,3},{3,2},{4,5},{5,4},{6,7},{7,6},{8,9},{9,8},{10,11... | collective-permute-start | bytes 2359304 | tf_op jit(solution)/shard_map/ppermute | solution.py:280
  12.5 112.6 %collective-permute-start.1 = (bf16[3,2,512,128]{3,2,1,0:T(8,128)(2,1)}, bf16[3,2,512,128]{3,2,1,0:T(8,128)(2,1)}, u32[]{:S(2)}, u32[]{:S(2)}) collective-permute-start(bf16[3,2,512,128]{3,2,1,0:T(8,128)(2,1)} %get-tuple-element.56), channel_id=1, source_target_pairs={{0,2},{1,3},{2,0},{3,1},{4,6},{5,7},{6,4},{7,5},{8,10},{9,11},{10,... | collective-permute-start | bytes 2359304 | tf_op jit(solution)/shard_map/ppermute | solution.py:280
  79.9 130.2 %collective-permute-start.8 = (bf16[2,2,2048,128]{3,2,1,0:T(8,128)(2,1)}, bf16[2,2,2048,128]{3,2,1,0:T(8,128)(2,1)}, u32[]{:S(2)}, u32[]{:S(2)}) collective-permute-start(bf16[2,2,2048,128]{3,2,1,0:T(8,128)(2,1)} %join.6.refs_12_.refs_5_), channel_id=1, source_target_pairs={{0,4},{8,12},{16,20},{24,28},{4,0},{12,8},{20,16},{28,24},{1,5},{9... | collective-permute-start | bytes 6291464 | tf_op jit(solution)/shard_map/ppermute | solution.py:286
  116.8 59.6 %collective-permute-start.2 = (bf16[3,2,512,128]{3,2,1,0:T(8,128)(2,1)}, bf16[3,2,512,128]{3,2,1,0:T(8,128)(2,1)}, u32[]{:S(2)}, u32[]{:S(2)}) collective-permute-start(bf16[3,2,512,128]{3,2,1,0:T(8,128)(2,1)} %get-tuple-element.57), channel_id=1, source_target_pairs={{0,3},{1,2},{2,1},{3,0},{4,7},{5,6},{6,5},{7,4},{8,11},{9,10},{10,... | collective-permute-start | bytes 2359304 | tf_op jit(solution)/shard_map/ppermute | solution.py:280
  121.6 62.2 %collective-permute-start.10 = (bf16[3,2,512,128]{3,2,1,0:T(8,128)(2,1)}, bf16[3,2,512,128]{3,2,1,0:T(8,128)(2,1)S(1)}, u32[]{:S(2)}, u32[]{:S(2)}) collective-permute-start(bf16[3,2,512,128]{3,2,1,0:T(8,128)(2,1)} %get-tuple-element.67), channel_id=1, source_target_pairs={{0,1},{1,0},{2,3},{3,2},{4,5},{5,4},{6,7},{7,6},{8,9},{9,8},{10,11... | collective-permute-start | bytes 2359304 | tf_op jit(solution)/shard_map/ppermute | solution.py:280
  121.7 91.0 %collective-permute-start.9 = (bf16[2,2,2048,128]{3,2,1,0:T(8,128)(2,1)S(1)}, bf16[2,2,2048,128]{3,2,1,0:T(8,128)(2,1)}, u32[]{:S(2)}, u32[]{:S(2)}) collective-permute-start(bf16[2,2,2048,128]{3,2,1,0:T(8,128)(2,1)S(1)} %copy-done), channel_id=1, source_target_pairs={{4,8},{12,16},{20,24},{8,4},{16,12},{24,20},{5,9},{13,17},{21,25},... | collective-permute-start | bytes 6291464 | tf_op jit(solution)/shard_map/ppermute | solution.py:286
  125.1 67.2 %collective-permute-start.11 = (bf16[3,2,512,128]{3,2,1,0:T(8,128)(2,1)}, bf16[3,2,512,128]{3,2,1,0:T(8,128)(2,1)}, u32[]{:S(2)}, u32[]{:S(2)}) collective-permute-start(bf16[3,2,512,128]{3,2,1,0:T(8,128)(2,1)} %get-tuple-element.68), channel_id=1, source_target_pairs={{0,2},{1,3},{2,0},{3,1},{4,6},{5,7},{6,4},{7,5},{8,10},{9,11},{10,... | collective-permute-start | bytes 2359304 | tf_op jit(solution)/shard_map/ppermute | solution.py:280
  180.2 86.8 %collective-permute-start.6 = (bf16[2,2,2048,128]{3,2,1,0:T(8,128)(2,1)}, bf16[2,2,2048,128]{3,2,1,0:T(8,128)(2,1)}, u32[]{:S(2)}, u32[]{:S(2)}) collective-permute-start(bf16[2,2,2048,128]{3,2,1,0:T(8,128)(2,1)} %join.7.refs_12_.refs_5_), channel_id=1, source_target_pairs={{0,4},{8,12},{16,20},{24,28},{4,0},{12,8},{20,16},{28,24},{1,5},{9... | collective-permute-start | bytes 6291464 | tf_op jit(solution)/shard_map/ppermute | solution.py:286
  192.3 77.9 %collective-permute-start.7 = (bf16[2,2,2048,128]{3,2,1,0:T(8,128)(2,1)}, bf16[2,2,2048,128]{3,2,1,0:T(8,128)(2,1)}, u32[]{:S(2)}, u32[]{:S(2)}) collective-permute-start(bf16[2,2,2048,128]{3,2,1,0:T(8,128)(2,1)} %join.7.refs_12_.refs_5_), channel_id=1, source_target_pairs={{4,8},{12,16},{20,24},{8,4},{16,12},{24,20},{5,9},{13,17},{21,25},... | collective-permute-start | bytes 6291464 | tf_op jit(solution)/shard_map/ppermute | solution.py:286
  210.1 40.0 %collective-permute-start.21 = (bf16[3,2,512,128]{3,2,1,0:T(8,128)(2,1)}, bf16[3,2,512,128]{3,2,1,0:T(8,128)(2,1)S(1)}, u32[]{:S(2)}, u32[]{:S(2)}) collective-permute-start(bf16[3,2,512,128]{3,2,1,0:T(8,128)(2,1)} %get-tuple-element.78), channel_id=1, source_target_pairs={{0,1},{1,0},{2,3},{3,2},{4,5},{5,4},{6,7},{7,6},{8,9},{9,8},{10,11... | collective-permute-start | bytes 2359304 | tf_op jit(solution)/shard_map/ppermute | solution.py:280
  210.1 41.1 %collective-permute-start.22 = (bf16[3,2,512,128]{3,2,1,0:T(8,128)(2,1)}, bf16[3,2,512,128]{3,2,1,0:T(8,128)(2,1)}, u32[]{:S(2)}, u32[]{:S(2)}) collective-permute-start(bf16[3,2,512,128]{3,2,1,0:T(8,128)(2,1)} %get-tuple-element.79), channel_id=1, source_target_pairs={{0,2},{1,3},{2,0},{3,1},{4,6},{5,7},{6,4},{7,5},{8,10},{9,11},{10,... | collective-permute-start | bytes 2359304 | tf_op jit(solution)/shard_map/ppermute | solution.py:280
  212.8 87.1 %collective-permute-start.23 = (bf16[3,2,512,128]{3,2,1,0:T(8,128)(2,1)}, bf16[3,2,512,128]{3,2,1,0:T(8,128)(2,1)}, u32[]{:S(2)}, u32[]{:S(2)}) collective-permute-start(bf16[3,2,512,128]{3,2,1,0:T(8,128)(2,1)} %get-tuple-element.80), channel_id=1, source_target_pairs={{0,3},{1,2},{2,1},{3,0},{4,7},{5,6},{6,5},{7,4},{8,11},{9,10},{10,... | collective-permute-start | bytes 2359304 | tf_op jit(solution)/shard_map/ppermute | solution.py:280
  250.1 55.4 %collective-permute-start.16 = (bf16[3,2,512,128]{3,2,1,0:T(8,128)(2,1)}, bf16[3,2,512,128]{3,2,1,0:T(8,128)(2,1)}, u32[]{:S(2)}, u32[]{:S(2)}) collective-permute-start(bf16[3,2,512,128]{3,2,1,0:T(8,128)(2,1)} %get-tuple-element.75), channel_id=1, source_target_pairs={{0,1},{1,0},{2,3},{3,2},{4,5},{5,4},{6,7},{7,6},{8,9},{9,8},{10,11... | collective-permute-start | bytes 2359304 | tf_op jit(solution)/shard_map/ppermute | solution.py:280
  251.2 95.7 %collective-permute-start.19 = (bf16[2,2,2048,128]{3,2,1,0:T(8,128)(2,1)S(1)}, bf16[2,2,2048,128]{3,2,1,0:T(8,128)(2,1)}, u32[]{:S(2)}, u32[]{:S(2)}) collective-permute-start(bf16[2,2,2048,128]{3,2,1,0:T(8,128)(2,1)S(1)} %copy-done.1), channel_id=1, source_target_pairs={{0,4},{8,12},{16,20},{24,28},{4,0},{12,8},{20,16},{28,24},{1,5},{9... | collective-permute-start | bytes 6291464 | tf_op jit(solution)/shard_map/ppermute | solution.py:286
  267.0 82.4 %collective-permute-start.20 = (bf16[2,2,2048,128]{3,2,1,0:T(8,128)(2,1)S(1)}, bf16[2,2,2048,128]{3,2,1,0:T(8,128)(2,1)}, u32[]{:S(2)}, u32[]{:S(2)}) collective-permute-start(bf16[2,2,2048,128]{3,2,1,0:T(8,128)(2,1)S(1)} %copy-done.1), channel_id=1, source_target_pairs={{4,8},{12,16},{20,24},{8,4},{16,12},{24,20},{5,9},{13,17},{21,25},... | collective-permute-start | bytes 6291464 | tf_op jit(solution)/shard_map/ppermute | solution.py:286
  270.2 41.8 %collective-permute-start.17 = (bf16[3,2,512,128]{3,2,1,0:T(8,128)(2,1)}, bf16[3,2,512,128]{3,2,1,0:T(8,128)(2,1)}, u32[]{:S(2)}, u32[]{:S(2)}) collective-permute-start(bf16[3,2,512,128]{3,2,1,0:T(8,128)(2,1)} %get-tuple-element.76), channel_id=1, source_target_pairs={{0,2},{1,3},{2,0},{3,1},{4,6},{5,7},{6,4},{7,5},{8,10},{9,11},{10,... | collective-permute-start | bytes 2359304 | tf_op jit(solution)/shard_map/ppermute | solution.py:280
  303.9 76.0 %collective-permute-start.26 = (bf16[2,2,2048,128]{3,2,1,0:T(8,128)(2,1)}, bf16[2,2,2048,128]{3,2,1,0:T(8,128)(2,1)}, u32[]{:S(2)}, u32[]{:S(2)}) collective-permute-start(bf16[2,2,2048,128]{3,2,1,0:T(8,128)(2,1)} %join.9.refs_12_.refs_5_), channel_id=1, source_target_pairs={{0,4},{8,12},{16,20},{24,28},{4,0},{12,8},{20,16},{28,24},{1,5},{9... | collective-permute-start | bytes 6291464 | tf_op jit(solution)/shard_map/ppermute | solution.py:286
  305.6 79.7 %collective-permute-start.27 = (bf16[2,2,2048,128]{3,2,1,0:T(8,128)(2,1)}, bf16[2,2,2048,128]{3,2,1,0:T(8,128)(2,1)}, u32[]{:S(2)}, u32[]{:S(2)}) collective-permute-start(bf16[2,2,2048,128]{3,2,1,0:T(8,128)(2,1)} %join.9.refs_12_.refs_5_), channel_id=1, source_target_pairs={{4,8},{12,16},{20,24},{8,4},{16,12},{24,20},{5,9},{13,17},{21,25},... | collective-permute-start | bytes 6291464 | tf_op jit(solution)/shard_map/ppermute | solution.py:286
  346.9 66.7 %collective-permute-start.28 = (bf16[3,2,512,128]{3,2,1,0:T(8,128)(2,1)}, bf16[3,2,512,128]{3,2,1,0:T(8,128)(2,1)S(1)}, u32[]{:S(2)}, u32[]{:S(2)}) collective-permute-start(bf16[3,2,512,128]{3,2,1,0:T(8,128)(2,1)} %get-tuple-element.90), channel_id=1, source_target_pairs={{0,1},{1,0},{2,3},{3,2},{4,5},{5,4},{6,7},{7,6},{8,9},{9,8},{10,11... | collective-permute-start | bytes 2359304 | tf_op jit(solution)/shard_map/ppermute | solution.py:280
  346.9 66.7 %collective-permute-start.29 = (bf16[3,2,512,128]{3,2,1,0:T(8,128)(2,1)}, bf16[3,2,512,128]{3,2,1,0:T(8,128)(2,1)}, u32[]{:S(2)}, u32[]{:S(2)}) collective-permute-start(bf16[3,2,512,128]{3,2,1,0:T(8,128)(2,1)} %get-tuple-element.91), channel_id=1, source_target_pairs={{0,2},{1,3},{2,0},{3,1},{4,6},{5,7},{6,4},{7,5},{8,10},{9,11},{10,... | collective-permute-start | bytes 2359304 | tf_op jit(solution)/shard_map/ppermute | solution.py:280
  349.4 65.7 %collective-permute-start.30 = (bf16[3,2,512,128]{3,2,1,0:T(8,128)(2,1)}, bf16[3,2,512,128]{3,2,1,0:T(8,128)(2,1)S(1)}, u32[]{:S(2)}, u32[]{:S(2)}) collective-permute-start(bf16[3,2,512,128]{3,2,1,0:T(8,128)(2,1)} %get-tuple-element.92), channel_id=1, source_target_pairs={{0,3},{1,2},{2,1},{3,0},{4,7},{5,6},{6,5},{7,4},{8,11},{9,10},{10,... | collective-permute-start | bytes 2359304 | tf_op jit(solution)/shard_map/ppermute | solution.py:280
  379.9 47.2 %collective-permute-start.24 = (bf16[2,2,2048,128]{3,2,1,0:T(8,128)(2,1)}, bf16[2,2,2048,128]{3,2,1,0:T(8,128)(2,1)}, u32[]{:S(2)}, u32[]{:S(2)}) collective-permute-start(bf16[2,2,2048,128]{3,2,1,0:T(8,128)(2,1)} %join.10.refs_11_.refs_5_), channel_id=1, source_target_pairs={{0,4},{8,12},{16,20},{24,28},{4,0},{12,8},{20,16},{28,24},{1,5},{9... | collective-permute-start | bytes 6291464 | tf_op jit(solution)/shard_map/ppermute | solution.py:286
  385.2 51.1 %collective-permute-start.25 = (bf16[2,2,2048,128]{3,2,1,0:T(8,128)(2,1)}, bf16[2,2,2048,128]{3,2,1,0:T(8,128)(2,1)}, u32[]{:S(2)}, u32[]{:S(2)}) collective-permute-start(bf16[2,2,2048,128]{3,2,1,0:T(8,128)(2,1)} %join.10.refs_11_.refs_5_), channel_id=1, source_target_pairs={{4,8},{12,16},{20,24},{8,4},{16,12},{24,20},{5,9},{13,17},{21,25},... | collective-permute-start | bytes 6291464 | tf_op jit(solution)/shard_map/ppermute | solution.py:286
  419.9 46.9 %collective-permute-start.34 = (bf16[2,2,2048,128]{3,2,1,0:T(8,128)(2,1)}, bf16[2,2,2048,128]{3,2,1,0:T(8,128)(2,1)S(1)}, u32[]{:S(2)}, u32[]{:S(2)}) collective-permute-start(bf16[2,2,2048,128]{3,2,1,0:T(8,128)(2,1)} %join.11.refs_11_.refs_5_), channel_id=1, source_target_pairs={{0,4},{8,12},{16,20},{24,28},{4,0},{12,8},{20,16},{28,24},{1,5},{9... | collective-permute-start | bytes 6291464 | tf_op jit(solution)/shard_map/ppermute | solution.py:286
  423.6 55.1 %collective-permute-start.35 = (bf16[2,2,2048,128]{3,2,1,0:T(8,128)(2,1)}, bf16[2,2,2048,128]{3,2,1,0:T(8,128)(2,1)}, u32[]{:S(2)}, u32[]{:S(2)}) collective-permute-start(bf16[2,2,2048,128]{3,2,1,0:T(8,128)(2,1)} %join.11.refs_11_.refs_5_), channel_id=1, source_target_pairs={{4,8},{12,16},{20,24},{8,4},{16,12},{24,20},{5,9},{13,17},{21,25},... | collective-permute-start | bytes 6291464 | tf_op jit(solution)/shard_map/ppermute | solution.py:286
  427.1 79.5 %collective-permute-start.14 = (bf16[4,512,128]{2,1,0:T(8,128)(2,1)}, bf16[4,512,128]{2,1,0:T(8,128)(2,1)}, u32[]{:S(2)}, u32[]{:S(2)}) collective-permute-start(bf16[4,512,128]{2,1,0:T(8,128)(2,1)} %get-tuple-element.73), channel_id=1, source_target_pairs={{0,2},{1,3},{2,0},{3,1},{4,6},{5,7},{6,4},{7,5},{8,10},{9,11},{10,... | collective-permute-start | bytes 1572872 | tf_op jit(solution)/shard_map/ppermute | solution.py:280
  436.3 72.1 %collective-permute-start.15 = (bf16[4,512,128]{2,1,0:T(8,128)(2,1)}, bf16[4,512,128]{2,1,0:T(8,128)(2,1)}, u32[]{:S(2)}, u32[]{:S(2)}) collective-permute-start(bf16[4,512,128]{2,1,0:T(8,128)(2,1)} %get-tuple-element.74), channel_id=1, source_target_pairs={{0,3},{1,2},{2,1},{3,0},{4,7},{5,6},{6,5},{7,4},{8,11},{9,10},{10,... | collective-permute-start | bytes 1572872 | tf_op jit(solution)/shard_map/ppermute | solution.py:280
  464.9 101.0 %collective-permute-start.31 = (bf16[6,512,128]{2,1,0:T(8,128)(2,1)}, bf16[6,512,128]{2,1,0:T(8,128)(2,1)S(1)}, u32[]{:S(2)}, u32[]{:S(2)}) collective-permute-start(bf16[6,512,128]{2,1,0:T(8,128)(2,1)} %get-tuple-element.94), channel_id=1, source_target_pairs={{0,1},{1,0},{2,3},{3,2},{4,5},{5,4},{6,7},{7,6},{8,9},{9,8},{10,11... | collective-permute-start | bytes 2359304 | tf_op jit(solution)/shard_map/ppermute | solution.py:280
  466.8 99.1 %collective-permute-start.32 = (bf16[6,512,128]{2,1,0:T(8,128)(2,1)}, bf16[6,512,128]{2,1,0:T(8,128)(2,1)S(1)}, u32[]{:S(2)}, u32[]{:S(2)}) collective-permute-start(bf16[6,512,128]{2,1,0:T(8,128)(2,1)} %get-tuple-element.95), channel_id=1, source_target_pairs={{0,2},{1,3},{2,0},{3,1},{4,6},{5,7},{6,4},{7,5},{8,10},{9,11},{10,... | collective-permute-start | bytes 2359304 | tf_op jit(solution)/shard_map/ppermute | solution.py:280
  478.7 87.2 %collective-permute-start.33 = (bf16[6,512,128]{2,1,0:T(8,128)(2,1)}, bf16[6,512,128]{2,1,0:T(8,128)(2,1)}, u32[]{:S(2)}, u32[]{:S(2)}) collective-permute-start(bf16[6,512,128]{2,1,0:T(8,128)(2,1)} %get-tuple-element.96), channel_id=1, source_target_pairs={{0,3},{1,2},{2,1},{3,0},{4,7},{5,6},{6,5},{7,4},{8,11},{9,10},{10,... | collective-permute-start | bytes 2359304 | tf_op jit(solution)/shard_map/ppermute | solution.py:280
  508.4 51.1 %collective-permute-start.37 = (bf16[2,512,128]{2,1,0:T(8,128)(2,1)}, bf16[2,512,128]{2,1,0:T(8,128)(2,1)S(1)}, u32[]{:S(2)}, u32[]{:S(2)}) collective-permute-start(bf16[2,512,128]{2,1,0:T(8,128)(2,1)} %get-tuple-element.99), channel_id=1, source_target_pairs={{0,2},{1,3},{2,0},{3,1},{4,6},{5,7},{6,4},{7,5},{8,10},{9,11},{10,... | collective-permute-start | bytes 786440 | tf_op jit(solution)/shard_map/ppermute | solution.py:280
  (27 other events, 498.4 us)
